TPU v7x, 512 devices: a whole 4x4x16 slice. The times are simulated.
512 devices in a mesh: sta: 32 (over y, z_lo), tm: 16 (over z_hi, x, core).
Axes of the slice: x: 4, y: 4, z: 16 (z_hi: 2, z_lo: 8; z = z_hi * 8 + z_lo), core: 2. Of those that a mesh axis runs over, the one named last changes fastest.
Arguments:
- records: bfloat16 [8192, 28800], P('sta', 'tm'), may hold values from -6 to 6
- validity: int32 [8192, 48], P('sta', 'tm'), may hold values from 0 to 1, as said below
- partners: int32 [32, 2], replicated, may hold values from -1 to 31, as said below
Outputs:
- correlation: float32 [8192, 2, 65, 256], P(('sta', 'tm'))
Inputs may be any that keep to these rules, and one draw needn't show every extreme that they name: `partners`: entry 0 of row b is a block other than b at most 2 blocks away; entry 1 is -1 (no second partner) or another such block different from entry 0. `validity`: some stations have no usable window.
All inputs are finite; a program needn't handle non-finite values.
Results may differ from a plain program's by a relative error of at most 0.0046.
Values may be sent and summed in bfloat16 or wider, within the bound.
No kernel may reach another device: no remote copies, remote signals or barrier semaphores. Data moves between devices by JAX's collectives and lax.ppermute only.
A program may use at most 64 MiB of HBM per device.

v0:
```python
import math

import jax
import jax.numpy as jnp
from jax import lax
from jax.sharding import PartitionSpec as P

WIN = 600
BINS = 64
LAG = 32
SLOTS = 2
REACH = 2


def shifted(array, axis, by):
    peers = lax.axis_size(axis)
    pairs = [(i, i + by) for i in range(peers) if 0 <= i + by < peers]
    return lax.ppermute(array, axis, pairs)


def forward_table(win_len, bin_count):
    sample_idx = jnp.arange(win_len, dtype=jnp.int32)
    harmonic = jnp.arange(1, bin_count + 1, dtype=jnp.int32)
    residue = sample_idx[:, None] * harmonic[None, :] % win_len
    phase_turns = residue.astype(jnp.float32) * (2.0 * math.pi / win_len)
    taper = 0.5 - 0.5 * jnp.cos((sample_idx.astype(jnp.float32) + 0.5) * (2.0 * math.pi / win_len))
    norm_factor = 1.0 / math.sqrt(win_len)
    table = jnp.concatenate(
        [taper[:, None] * jnp.cos(phase_turns), -taper[:, None] * jnp.sin(phase_turns)], axis=1
    )
    return (table * norm_factor).astype(jnp.bfloat16)


def inverse_table(win_len, bin_count, max_lag):
    lag_values = jnp.arange(2 * max_lag + 1, dtype=jnp.int32) - max_lag
    harmonic = jnp.arange(1, bin_count + 1, dtype=jnp.int32)
    residue = jnp.mod(lag_values[:, None] * harmonic[None, :], win_len)
    phase_turns = residue.astype(jnp.float32) * (2.0 * math.pi / win_len)
    return jnp.concatenate([jnp.cos(phase_turns), -jnp.sin(phase_turns)], axis=1)


def whiten(spectra, maskf):
    bin_count = spectra.shape[-1] // 2
    real_part = spectra[..., :bin_count]
    imag_part = spectra[..., bin_count:]
    power_bins = real_part * real_part + imag_part * imag_part
    bin_idx = jnp.arange(bin_count, dtype=jnp.int32)
    nearby = (jnp.abs(bin_idx[:, None] - bin_idx[None, :]) <= 2).astype(jnp.float32)
    average = nearby / jnp.sum(nearby, axis=0, keepdims=True)
    smooth = jnp.einsum("wsf,fg->wsg", power_bins, average, precision=lax.Precision.HIGHEST)
    inv_scale = 1.0 / jnp.sqrt(smooth + 0.05)
    inv_scale = jnp.concatenate([inv_scale, inv_scale], axis=-1)
    return (spectra * inv_scale * maskf[..., None]).astype(jnp.bfloat16)


def into_lags(lag_table, cross, tallies):
    lagged = jnp.einsum("tcf,iqcfj->iqtj", lag_table, cross, precision=lax.Precision.HIGHEST)
    return lagged / jnp.maximum(tallies, 1.0)[:, :, None, :]


def body(records, validity, partners):
    rows_per = records.shape[0]
    win_dev = validity.shape[1]
    table = forward_table(WIN, BINS)
    lag_table = inverse_table(WIN, BINS, LAG).reshape(2 * LAG + 1, 2, BINS)
    frames = records.reshape(rows_per, win_dev, WIN)
    spectra = jnp.einsum("swt,tc->wsc", frames, table, preferred_element_type=jnp.float32)
    maskf = validity.T.astype(jnp.float32)
    white = whiten(spectra, maskf)
    mask_half = maskf.astype(jnp.bfloat16)
    block_id = lax.axis_index("sta")
    own_pair = lax.dynamic_index_in_dim(partners, block_id, 0, keepdims=False)
    part_white = jnp.zeros((SLOTS,) + white.shape, jnp.bfloat16)
    part_mask = jnp.zeros((SLOTS,) + mask_half.shape, jnp.bfloat16)
    offsets = [offset for offset in range(-REACH, REACH + 1) if offset != 0]
    for offset in offsets:
        moved_white, moved_mask = shifted((white, mask_half), "sta", -offset)
        found = own_pair == block_id + offset
        part_white = jnp.where(found[:, None, None, None], moved_white[None], part_white)
        part_mask = jnp.where(found[:, None, None], moved_mask[None], part_mask)
    every_white = jnp.concatenate([white[None], part_white], axis=0)
    every_mask = jnp.concatenate([mask_half[None], part_mask], axis=0)
    split_white, split_mask = (
        lax.all_to_all(every_white, "tm", split_axis=2, concat_axis=1, tiled=True),
        lax.all_to_all(every_mask, "tm", split_axis=2, concat_axis=1, tiled=True),
    )
    all_windows = split_white.shape[1]
    own_rows = split_white.shape[2]
    own_white = split_white[0]
    own_mask = split_mask[0]
    far_white = split_white[1:]
    far_mask = split_mask[1:]
    own_parts = own_white.reshape(all_windows, own_rows, 2, BINS)
    own_mixed = jnp.stack([own_parts, jnp.stack([own_parts[:, :, 1], -own_parts[:, :, 0]], axis=2)])
    piece_white, piece_mask = lax.all_gather((far_white, far_mask), "tm", axis=2, tiled=True)
    piece_len = piece_white.shape[2]
    far_parts = piece_white.reshape(piece_white.shape[0], all_windows, piece_len, 2, BINS)
    cross = jnp.einsum(
        "cwief,qwjef->iqcfj", own_mixed, far_parts, preferred_element_type=jnp.float32
    )
    tallies = jnp.einsum("wi,qwj->iqj", own_mask, piece_mask, preferred_element_type=jnp.float32)
    return into_lags(lag_table, cross, tallies)


def solution(mesh):
    placed = (P("sta", "tm"), P("sta", "tm"), P())
    return jax.shard_map(
        body,
        mesh=mesh,
        in_specs=placed,
        out_specs=P(("sta", "tm"), None, None, None),
        check_vma=False,
    )
```

profile of v0, /device:TPU:11, one launch (start us, length us, event | category | flops | bytes accessed | tf_op | source)
XLA Modules:
  0.0 299.1 jit_solution(10912963684370913895)
XLA Ops:
  6.5 0.1 convert_reduce_fusion
  6.7 0.8 fusion.40
  7.5 1.3 cosine_multiply_fusion
  8.8 0.5 convolution_bitcast_fusion
  9.3 0.4 fusion.10
  9.7 4.9 %collective-permute-start.3 = (bf16[3,256,128]{1,2,0:T(8,128)(2,1)S(1)}, bf16[3,256,128]{1,2,0:T(8,128)(2,1)S(1)}, u32[]{:S(2)}, u32[]{:S(2)}) collective-permute-start(bf16[3,256,128]{1,2,0:T(8,128)(2,1)S(1)} %fusion.14), channel_id=1, source_target_pairs={{0,32},{16,48},{32,64},{48,80},{64,96},{80,112},{96,128},{112,144}... | collective-permute-start | bytes 589832 | tf_op jit(solution)/shard_map/ppermute | solution.py:18
  14.6 3.6 %collective-permute-start.2 = (bf16[3,256,128]{1,2,0:T(8,128)(2,1)S(1)}, bf16[3,256,128]{1,2,0:T(8,128)(2,1)S(1)}, u32[]{:S(2)}, u32[]{:S(2)}) collective-permute-start(bf16[3,256,128]{1,2,0:T(8,128)(2,1)S(1)} %fusion.14), channel_id=1, source_target_pairs={{0,16},{16,32},{32,48},{48,64},{64,80},{80,96},{96,112},{112,128},... | collective-permute-start | bytes 589832 | tf_op jit(solution)/shard_map/ppermute | solution.py:18
  18.2 9.2 %collective-permute-start.1 = (bf16[3,256,128]{1,2,0:T(8,128)(2,1)S(1)}, bf16[3,256,128]{1,2,0:T(8,128)(2,1)S(1)}, u32[]{:S(2)}, u32[]{:S(2)}) collective-permute-start(bf16[3,256,128]{1,2,0:T(8,128)(2,1)S(1)} %fusion.14), channel_id=1, source_target_pairs={{16,0},{32,16},{48,32},{64,48},{80,64},{96,80},{112,96},{128,112},... | collective-permute-start | bytes 589832 | tf_op jit(solution)/shard_map/ppermute | solution.py:18
  27.4 2.3 collective-permute-start
  29.7 0.2 copy.98
  29.9 0.2 compare_reduce_fusion
  30.1 4.1 %collective-permute-done.3 = bf16[3,256,128]{1,2,0:T(8,128)(2,1)S(1)} collective-permute-done((bf16[3,256,128]{1,2,0:T(8,128)(2,1)S(1)}, bf16[3,256,128]{1,2,0:T(8,128)(2,1)S(1)}, u32[]{:S(2)}, u32[]{:S(2)}) %collective-permute-start.3) | collective-permute-done | bytes 196640 | tf_op jit(solution)/shard_map/ppermute | solution.py:18
  34.2 0.2 copy.97
  34.4 0.2 copy.96
  34.6 0.2 copy.95
  34.8 12.9 %collective-permute-done = bf16[3,256,128]{1,2,0:T(8,128)(2,1)S(1)} collective-permute-done((bf16[3,256,128]{1,2,0:T(8,128)(2,1)S(1)}, bf16[3,256,128]{1,2,0:T(8,128)(2,1)S(1)}, u32[]{:S(2)}, u32[]{:S(2)}) %collective-permute-start) | collective-permute-done | bytes 196640 | tf_op jit(solution)/shard_map/ppermute | solution.py:18
  47.7 0.2 copy.94
  47.8 0.5 select_select_fusion
  48.4 0.5 pad_maximum_fusion
  48.9 50.9 %all_to_all.30 = bf16[3,3,256,128]{3,1,0,2:T(4,128)(2,1)S(1)} all-to-all(bf16[3,3,256,128]{3,1,0,2:T(4,128)(2,1)S(1)} %pad_maximum_fusion), channel_id=1, replica_groups=mesh['sta'=32,'tm'=16] {'tm'}, dimensions={2} | all-to-all | bytes 1179648 | tf_op jit(solution)/shard_map/all_to_all | solution.py:84
  99.8 0.1 copy.99
  99.9 0.8 copy.100
  100.7 7.9 %collective-permute-start.7 = (bf16[3,256]{1,0:T(4,128)(2,1)S(1)}, bf16[3,256]{1,0:T(4,128)(2,1)S(1)}, u32[]{:S(2)}, u32[]{:S(2)}) collective-permute-start(bf16[3,256]{1,0:T(4,128)(2,1)S(1)} %get-tuple-element.11), channel_id=1, source_target_pairs={{0,32},{16,48},{32,64},{48,80},{64,96},{80,112},{96,128},{112,144}... | collective-permute-start | bytes 4616 | tf_op jit(solution)/shard_map/ppermute | solution.py:18
  108.6 3.7 %collective-permute-start.6 = (bf16[3,256]{1,0:T(4,128)(2,1)S(1)}, bf16[3,256]{1,0:T(4,128)(2,1)S(1)}, u32[]{:S(2)}, u32[]{:S(2)}) collective-permute-start(bf16[3,256]{1,0:T(4,128)(2,1)S(1)} %get-tuple-element.11), channel_id=1, source_target_pairs={{0,16},{16,32},{32,48},{48,64},{64,80},{80,96},{96,112},{112,128},... | collective-permute-start | bytes 4616 | tf_op jit(solution)/shard_map/ppermute | solution.py:18
  112.4 9.7 %collective-permute-start.5 = (bf16[3,256]{1,0:T(4,128)(2,1)S(1)}, bf16[3,256]{1,0:T(4,128)(2,1)S(1)}, u32[]{:S(2)}, u32[]{:S(2)}) collective-permute-start(bf16[3,256]{1,0:T(4,128)(2,1)S(1)} %get-tuple-element.11), channel_id=1, source_target_pairs={{16,0},{32,16},{48,32},{64,48},{80,64},{96,80},{112,96},{128,112},... | collective-permute-start | bytes 4616 | tf_op jit(solution)/shard_map/ppermute | solution.py:18
  122.1 2.2 collective-permute-start.4
  124.3 3.2 %collective-permute-done.4 = bf16[3,256]{1,0:T(4,128)(2,1)S(1)} collective-permute-done((bf16[3,256]{1,0:T(4,128)(2,1)S(1)}, bf16[3,256]{1,0:T(4,128)(2,1)S(1)}, u32[]{:S(2)}, u32[]{:S(2)}) %collective-permute-start.4) | collective-permute-done | bytes 1568 | tf_op jit(solution)/shard_map/ppermute | solution.py:18
  127.6 0.1 select_select_fusion.1
  127.7 0.9 copy.109
  128.6 11.4 %all-to-all-start.1 = ((bf16[3,3,256]{1,0,2:T(4,128)(2,1)}), bf16[3,3,256]{1,0,2:T(4,128)(2,1)S(1)}, u32[]{:S(2)}, u32[]{:S(2)}) async-start(bf16[3,3,256]{1,0,2:T(4,128)(2,1)} %copy.109), calls=%async_computation.1 | async-start | bytes 524288 | tf_op jit(solution)/shard_map/all_to_all | solution.py:85
  140.0 0.2 fusion.34
  140.2 17.9 %all-to-all-done.1 = bf16[3,3,256]{1,0,2:T(4,128)(2,1)S(1)} async-done(((bf16[3,3,256]{1,0,2:T(4,128)(2,1)}), bf16[3,3,256]{1,0,2:T(4,128)(2,1)S(1)}, u32[]{:S(2)}, u32[]{:S(2)}) %all-to-all-start.1) | async-done | bytes 4640 | tf_op jit(solution)/shard_map/all_to_all | solution.py:85
  158.1 0.4 copy.125
  158.6 0.1 copy.113
  158.7 41.0 %all_gather.7 = bf16[2,48,256]{1,2,0:T(8,128)(2,1)S(1)} all-gather(bf16[2,48,16]{1,2,0:T(8,128)(2,1)S(1)} %copy.113), channel_id=1, replica_groups=mesh['sta'=32,'tm'=16] {'tm'}, dimensions={2}, use_global_device_ids=true | all-gather | bytes 52224 | tf_op jit(solution)/shard_map/all_gather | solution.py:95
  199.7 0.2 convolution_maximum_fusion
  200.0 0.2 reshape_squeeze.3
  200.2 0.2 stack_reshape_squeeze.3
  200.3 0.8 copy.106
  201.1 0.5 fusion.46
  201.7 0.5 copy.127
  202.2 0.5 copy.128
  202.7 0.1 maximum_bitcast_fusion.2
  202.8 63.5 %all-gather.2.cloned.1.call-done = bf16[2,48,256,128]{3,2,1,0:T(8,128)(2,1)} async-done(((bf16[2,48,16,128]{3,2,1,0:T(8,128)(2,1)}), bf16[2,48,256,128]{3,2,1,0:T(8,128)(2,1)}) %all-gather.2.cloned.1.call-update) | async-done | bytes 6291472 | tf_op jit(solution)/shard_map/all_gather | solution.py:95
  266.3 8.7 %copy.101 = bf16[2,48,256,128]{2,3,1,0:T(8,128)(2,1)} copy(bf16[2,48,256,128]{3,2,1,0:T(8,128)(2,1)} %all-gather.2.cloned.1.call-done) | data formatting | bytes 12582912 | tf_op jit(solution)/shard_map/all_gather | solution.py:95
  274.9 9.7 %fusion.5 = f32[16,2,2,64,256]{4,0,2,1,3:T(8,128)S(1)} fusion(bf16[2,48,256,2,64,1]{2,4,3,1,0,5:T(8,128)(2,1)} %bitcast.59, bf16[1,48,16,2,64]{1,2,3,0,4:T(8,128)(2,1)S(1)} %maximum_bitcast_fusion.2, bf16[1,48,16,2,64]{1,2,3,0,4:T(8,128)(2,1)S(1)} %copy.106), kind=kOutput, calls=%fused_computation.6 | convolution fusion | flops 202113024 | bytes 10878976 | tf_op jit(solution)/shard_map/cwief,qwjef->iqcfj/dot_general | solution.py:98
  284.7 5.1 %fusion.4 = f32[16,2,65,256]{3,2,1,0:T(8,128)S(1)} fusion(f32[16,2,2,64,256]{4,0,2,1,3:T(8,128)S(1)} %fusion.5, f32[16,2,256]{2,1,0:T(2,128)S(1)} %copy.115, f32[65,1,64]{0,2,1:T(8,128)S(1)} %get-tuple-element.14, f32[65,1,64]{0,2,1:T(8,128)S(1)} %get-tuple-element.13), kind=kOutput, calls=%fused_computation.5 | convolution fusion | flops 818430080 | bytes 6390272 | tf_op jit(solution)/shard_map/tcf,iqcfj->iqtj/dot_general | solution.py:57
  289.8 2.4 copy.116
  (26 shorter events, 0.4 us)
Async XLA Ops:
  6.5 2.2 copy-start
  6.5 23.4 %copy-start.1 = (s32[32,2]{0,1:T(2,128)S(1)}, s32[32,2]{0,1:T(2,128)}, u32[]{:S(2)}) copy-start(s32[32,2]{0,1:T(2,128)} %param.5) | copy-start | bytes 772
  6.5 259.7 %all-gather.2.cloned.1.call-start = ((), (), s32[]{:S(2)}) async-start(), calls=%async_computation.2 | async-start | bytes 6684672 | tf_op jit(solution)/shard_map/all_gather | solution.py:95
  9.7 24.5 %collective-permute-start.3 = (bf16[3,256,128]{1,2,0:T(8,128)(2,1)S(1)}, bf16[3,256,128]{1,2,0:T(8,128)(2,1)S(1)}, u32[]{:S(2)}, u32[]{:S(2)}) collective-permute-start(bf16[3,256,128]{1,2,0:T(8,128)(2,1)S(1)} %fusion.14), channel_id=1, source_target_pairs={{0,32},{16,48},{32,64},{48,80},{64,96},{80,112},{96,128},{112,144}... | collective-permute-start | bytes 589832 | tf_op jit(solution)/shard_map/ppermute | solution.py:18
  14.6 19.8 %collective-permute-start.2 = (bf16[3,256,128]{1,2,0:T(8,128)(2,1)S(1)}, bf16[3,256,128]{1,2,0:T(8,128)(2,1)S(1)}, u32[]{:S(2)}, u32[]{:S(2)}) collective-permute-start(bf16[3,256,128]{1,2,0:T(8,128)(2,1)S(1)} %fusion.14), channel_id=1, source_target_pairs={{0,16},{16,32},{32,48},{48,64},{64,80},{80,96},{96,112},{112,128},... | collective-permute-start | bytes 589832 | tf_op jit(solution)/shard_map/ppermute | solution.py:18
  18.2 16.4 %collective-permute-start.1 = (bf16[3,256,128]{1,2,0:T(8,128)(2,1)S(1)}, bf16[3,256,128]{1,2,0:T(8,128)(2,1)S(1)}, u32[]{:S(2)}, u32[]{:S(2)}) collective-permute-start(bf16[3,256,128]{1,2,0:T(8,128)(2,1)S(1)} %fusion.14), channel_id=1, source_target_pairs={{16,0},{32,16},{48,32},{64,48},{80,64},{96,80},{112,96},{128,112},... | collective-permute-start | bytes 589832 | tf_op jit(solution)/shard_map/ppermute | solution.py:18
  27.4 20.2 %collective-permute-start = (bf16[3,256,128]{1,2,0:T(8,128)(2,1)S(1)}, bf16[3,256,128]{1,2,0:T(8,128)(2,1)S(1)}, u32[]{:S(2)}, u32[]{:S(2)}) collective-permute-start(bf16[3,256,128]{1,2,0:T(8,128)(2,1)S(1)} %fusion.14), channel_id=1, source_target_pairs={{32,0},{48,16},{64,32},{80,48},{96,64},{112,80},{128,96},{144,112}... | collective-permute-start | bytes 589832 | tf_op jit(solution)/shard_map/ppermute | solution.py:18
  100.7 23.6 %collective-permute-start.7 = (bf16[3,256]{1,0:T(4,128)(2,1)S(1)}, bf16[3,256]{1,0:T(4,128)(2,1)S(1)}, u32[]{:S(2)}, u32[]{:S(2)}) collective-permute-start(bf16[3,256]{1,0:T(4,128)(2,1)S(1)} %get-tuple-element.11), channel_id=1, source_target_pairs={{0,32},{16,48},{32,64},{48,80},{64,96},{80,112},{96,128},{112,144}... | collective-permute-start | bytes 4616 | tf_op jit(solution)/shard_map/ppermute | solution.py:18
  108.6 15.7 %collective-permute-start.6 = (bf16[3,256]{1,0:T(4,128)(2,1)S(1)}, bf16[3,256]{1,0:T(4,128)(2,1)S(1)}, u32[]{:S(2)}, u32[]{:S(2)}) collective-permute-start(bf16[3,256]{1,0:T(4,128)(2,1)S(1)} %get-tuple-element.11), channel_id=1, source_target_pairs={{0,16},{16,32},{32,48},{48,64},{64,80},{80,96},{96,112},{112,128},... | collective-permute-start | bytes 4616 | tf_op jit(solution)/shard_map/ppermute | solution.py:18
  112.4 11.9 %collective-permute-start.5 = (bf16[3,256]{1,0:T(4,128)(2,1)S(1)}, bf16[3,256]{1,0:T(4,128)(2,1)S(1)}, u32[]{:S(2)}, u32[]{:S(2)}) collective-permute-start(bf16[3,256]{1,0:T(4,128)(2,1)S(1)} %get-tuple-element.11), channel_id=1, source_target_pairs={{16,0},{32,16},{48,32},{64,48},{80,64},{96,80},{112,96},{128,112},... | collective-permute-start | bytes 4616 | tf_op jit(solution)/shard_map/ppermute | solution.py:18
  122.1 5.5 %collective-permute-start.4 = (bf16[3,256]{1,0:T(4,128)(2,1)S(1)}, bf16[3,256]{1,0:T(4,128)(2,1)S(1)}, u32[]{:S(2)}, u32[]{:S(2)}) collective-permute-start(bf16[3,256]{1,0:T(4,128)(2,1)S(1)} %get-tuple-element.11), channel_id=1, source_target_pairs={{32,0},{48,16},{64,32},{80,48},{96,64},{112,80},{128,96},{144,112}... | collective-permute-start | bytes 4616 | tf_op jit(solution)/shard_map/ppermute | solution.py:18
  128.6 29.5 %all-to-all-start.1 = ((bf16[3,3,256]{1,0,2:T(4,128)(2,1)}), bf16[3,3,256]{1,0,2:T(4,128)(2,1)S(1)}, u32[]{:S(2)}, u32[]{:S(2)}) async-start(bf16[3,3,256]{1,0,2:T(4,128)(2,1)} %copy.109), calls=%async_computation.1 | async-start | bytes 524288 | tf_op jit(solution)/shard_map/all_to_all | solution.py:85
Sparse Core Ops, SparseCore 0:
  100.9 165.3 all-gather.1
where the time goes:
time: 300 us; the launch traced here: 299 us
  waiting for transfers between devices  102 us (34%)
  blocking collectives  91.9 us (31%)
  starting transfers between devices  54.9 us (18%)
  local copies, waits for them, and re-layouts  17 us (6%)
  matrix products  15.9 us (5%)
  between operations  13.8 us (5%)
  other arithmetic  4.01 us (1%)
    all_gather x1, waiting for transfers between devices, body(): lax.all_gather((far_white, far_mask), 'tm', axis=2, tiled=True)  63.5 us
    all_to_all x1, blocking collectives, body(): lax.all_to_all(every_white, 'tm', split_axis=2, concat_axis=1, tiled=True)  50.9 us
    ppermute x8, starting transfers between devices, shifted(): return lax.ppermute(array, axis, pairs)  43.5 us
    all_gather x1, blocking collectives, body(): lax.all_gather((far_white, far_mask), 'tm', axis=2, tiled=True)  41 us
    ppermute x8, waiting for transfers between devices, shifted(): return lax.ppermute(array, axis, pairs)  20.2 us
    all_to_all x1, waiting for transfers between devices, body(): lax.all_to_all(every_mask, 'tm', split_axis=2, concat_axis=1, tiled=True)  17.9 us
    all_to_all x1, starting transfers between devices, body(): lax.all_to_all(every_mask, 'tm', split_axis=2, concat_axis=1, tiled=True)  11.4 us
    dot_general x1, matrix products, body(): jnp.einsum('cwief,qwjef->iqcfj', own_mixed, far_parts, preferred_element_...  9.72 us
  transfers between devices with their start and end apart: 10, of which 5 were waited for; matrix products, arithmetic and copies ran while one was open for 2% of the time, Pallas kernels for 0%

commit v1 on v0

v1 whole, which is shorter than its diff:
```python
import functools
import math

import jax
import jax.numpy as jnp
import numpy as np
from jax import lax
from jax.experimental import pallas as pl
from jax.experimental.pallas import tpu as pltpu
from jax.sharding import PartitionSpec as P

WIN = 600
BINS = 64
LAG = 32
SLOTS = 2
STA = 256
BLOCKS = 32
TM = 16
HALF = 8
CHIPS = 4
COLS = 2 * BINS
LAGS = 2 * LAG + 1
LPAD = 72
TALLY_ROW = LAGS
MASK_ROWS = 16
ROW_BLOCK = 128 // HALF
CHIP_ROWS = 2 * ROW_BLOCK
CHUNKS = (2, 1)
AXES = ("sta", "tm")
MIB = 1 << 20


def forward_table():
    sample = np.arange(WIN)
    harmonic = np.arange(1, BINS + 1)
    residue = sample[:, None] * harmonic[None, :] % WIN
    phase = residue.astype(np.float32) * np.float32(2.0 * math.pi / WIN)
    taper = np.float32(0.5) - np.float32(0.5) * np.cos(
        (sample.astype(np.float32) + np.float32(0.5)) * np.float32(2.0 * math.pi / WIN)
    )
    table = np.concatenate([taper[:, None] * np.cos(phase), -taper[:, None] * np.sin(phase)], axis=1)
    return (table * np.float32(1.0 / math.sqrt(WIN))).astype(jnp.bfloat16)


def window_spans(win_dev):
    total = win_dev * WIN
    spans = []
    for w in range(win_dev):
        lo = w * WIN // 128 * 128
        hi = min(-(-(w + 1) * WIN // 128) * 128, total)
        spans.append((lo, hi))
    return spans


def window_tables(win_dev):
    table = forward_table()
    out = []
    for w, (lo, hi) in enumerate(window_spans(win_dev)):
        padded = np.zeros((hi - lo, COLS), table.dtype)
        padded[w * WIN - lo : (w + 1) * WIN - lo] = table
        out.append(np.ascontiguousarray(padded.T))
    return out


def band_average():
    bins = np.arange(BINS)
    nearby = (np.abs(bins[:, None] - bins[None, :]) <= 2).astype(np.float32)
    return np.ascontiguousarray((nearby / nearby.sum(axis=0, keepdims=True)).T)


def lag_tables():
    lags = np.arange(LAGS) - LAG
    harmonic = np.arange(1, BINS + 1)
    phase = np.mod(lags[:, None] * harmonic[None, :], WIN) * (2.0 * math.pi / WIN)
    cosine = np.zeros((LPAD, COLS), np.float32)
    sine = np.zeros((LPAD, COLS), np.float32)
    cosine[:LAGS] = np.tile(np.cos(phase), (1, 2))
    sine[:LAGS] = np.concatenate([-np.sin(phase), np.sin(phase)], axis=1)
    return cosine, sine


def routes(target):
    pairs = []
    for b in range(BLOCKS):
        for t in range(TM):
            there = target(b, t)
            if there is not None:
                pairs.append((b * TM + t, there[0] * TM + there[1]))
    return pairs


def to_other_half(b, t):
    return b, (t + HALF) % TM


def to_block(by):
    def target(b, t):
        nb = b + by
        if not 0 <= nb < BLOCKS:
            return None
        return nb, t if nb // 8 == b // 8 else (t + HALF) % TM

    return target


def to_chip(by):
    return lambda b, t: (b, t // HALF * HALF + (t % HALF // 2 + by) % CHIPS * 2 + t % 2)


def to_core(b, t):
    return b, t ^ 1


def send(array, target):
    return lax.ppermute(array, AXES, routes(target))


CHIP_GROUPS = [[z * HALF + 2 * i + c for i in range(CHIPS)] for z in range(TM // HALF) for c in range(2)]


def whiten_kernel(spans, rec_ref, mask_ref, avg_ref, *refs):
    win_dev = len(spans)
    tables, outs = refs[:win_dev], refs[win_dev:]
    mask = mask_ref[...]
    w = 0
    for part, windows in enumerate(CHUNKS):
        for k in range(windows):
            lo, hi = spans[w]
            spectra = lax.dot_general(
                tables[w][...], rec_ref[:, lo:hi], (((1,), (1,)), ((), ())), preferred_element_type=jnp.float32
            )
            real, imag = spectra[:BINS], spectra[BINS:]
            power = real * real + imag * imag
            smooth = jnp.dot(avg_ref[...], power, precision=lax.Precision.HIGHEST, preferred_element_type=jnp.float32)
            scale = mask[w : w + 1] / jnp.sqrt(smooth + 0.05)
            outs[part][k * COLS : k * COLS + BINS] = (real * scale).astype(jnp.bfloat16)
            outs[part][k * COLS + BINS : (k + 1) * COLS] = (imag * scale).astype(jnp.bfloat16)
            w += 1
    outs[0][CHUNKS[0] * COLS :] = mask.astype(jnp.bfloat16)


def whitened(records, validity):
    rows, samples = records.shape
    win_dev = validity.shape[1]
    spans = window_spans(win_dev)
    mask = jnp.pad(validity.T.astype(jnp.float32), ((0, MASK_ROWS - win_dev), (0, 0)))
    vmem = pl.BlockSpec(memory_space=pltpu.VMEM)
    shapes = [
        jax.ShapeDtypeStruct((n * COLS + (MASK_ROWS if i == 0 else 0), rows), jnp.bfloat16)
        for i, n in enumerate(CHUNKS)
    ]
    return pl.pallas_call(
        functools.partial(whiten_kernel, spans),
        out_shape=shapes,
        in_specs=[vmem] * (3 + win_dev),
        out_specs=[vmem] * len(shapes),
        compiler_params=pltpu.CompilerParams(vmem_limit_bytes=16 * MIB),
        name="whiten",
    )(records, mask, band_average(), *window_tables(win_dev))


def rotate_kernel(groups, own_ref, cos_ref, sin_ref, out_ref):
    cosine, sine = cos_ref[...], sin_ref[...]
    for m in range(own_ref.shape[0]):
        for g in range(groups):
            lanes = slice(g * COLS, (g + 1) * COLS)
            row = own_ref[m : m + 1, lanes]
            other = pltpu.roll(row, BINS, 1)
            out_ref[m * LPAD : (m + 1) * LPAD, lanes] = (row * cosine + other * sine).astype(jnp.bfloat16)


def rotated(own):
    stations, width = own.shape
    cosine, sine = lag_tables()
    step = 8
    return pl.pallas_call(
        functools.partial(rotate_kernel, width // COLS),
        out_shape=jax.ShapeDtypeStruct((stations * LPAD, width), jnp.bfloat16),
        grid=(stations // step,),
        in_specs=[
            pl.BlockSpec((step, width), lambda i: (i, 0)),
            pl.BlockSpec((LPAD, COLS), lambda i: (0, 0)),
            pl.BlockSpec((LPAD, COLS), lambda i: (0, 0)),
        ],
        out_specs=pl.BlockSpec((step * LPAD, width), lambda i: (i, 0)),
        compiler_params=pltpu.CompilerParams(vmem_limit_bytes=32 * MIB),
        cost_estimate=pl.CostEstimate(
            flops=3 * stations * LPAD * width, bytes_accessed=2 * stations * LPAD * width, transcendentals=0
        ),
        name="rotate",
    )(own, cosine, sine)


def lags_kernel(depth, pieces, has_acc, has_tally, turned_ref, *refs):
    far = refs[:pieces]
    refs = refs[pieces:]
    out_ref = refs[-1]
    total = refs[0][...].astype(jnp.float32) if has_acc else None
    for d in range(pieces):
        term = jnp.dot(
            turned_ref[:, d * depth : (d + 1) * depth], far[d][:depth], preferred_element_type=jnp.float32
        )
        total = term if total is None else total + term
    out_ref[...] = total.astype(out_ref.dtype)
    if has_tally:
        tally_ref = refs[1 if has_acc else 0]
        for m in range(tally_ref.shape[0]):
            row = m * LPAD + TALLY_ROW
            out_ref[row : row + 1] = tally_ref[m : m + 1].astype(out_ref.dtype)


def into_lags(turned, far, depth, first, count, acc=None, tally=None, dtype=jnp.float32):
    width = far[0].shape[1]
    step = 8
    base = first // step
    rows = step * LPAD
    args = [turned, *far]
    specs = [pl.BlockSpec((rows, turned.shape[1]), lambda i: (base + i, 0))]
    specs += [pl.BlockSpec(f.shape, lambda i: (0, 0)) for f in far]
    if acc is not None:
        args.append(acc)
        specs.append(pl.BlockSpec((rows, width), lambda i: (base + i, 0)))
    if tally is not None:
        args.append(tally)
        specs.append(pl.BlockSpec((step, width), lambda i: (base + i, 0)))
    return pl.pallas_call(
        functools.partial(lags_kernel, depth, len(far), acc is not None, tally is not None),
        out_shape=jax.ShapeDtypeStruct((count * LPAD, width), dtype),
        grid=(count // step,),
        in_specs=specs,
        out_specs=pl.BlockSpec((rows, width), lambda i: (i, 0)),
        compiler_params=pltpu.CompilerParams(vmem_limit_bytes=40 * MIB),
        cost_estimate=pl.CostEstimate(
            flops=2 * count * LPAD * width * depth * len(far),
            bytes_accessed=2 * count * LPAD * turned.shape[1] + 4 * count * LPAD * width,
            transcendentals=0,
        ),
        name="lags",
    )(*args)


def combine_kernel(mine_ref, theirs_ref, out_ref):
    for m in range(out_ref.shape[0]):
        rows = slice(m * LPAD, (m + 1) * LPAD)
        total = mine_ref[rows] + theirs_ref[rows].astype(jnp.float32)
        result = total[:LAGS] / jnp.maximum(total[TALLY_ROW : TALLY_ROW + 1], 1.0)
        for q in range(SLOTS):
            out_ref[m, q] = result[:, q * STA : (q + 1) * STA]


def combined(mine, theirs):
    stations = mine.shape[0] // LPAD
    step = 4
    block = pl.BlockSpec((step * LPAD, mine.shape[1]), lambda i: (i, 0))
    return pl.pallas_call(
        combine_kernel,
        out_shape=jax.ShapeDtypeStruct((stations, SLOTS, LAGS, STA), jnp.float32),
        grid=(stations // step,),
        in_specs=[block, block],
        out_specs=pl.BlockSpec((step, SLOTS, LAGS, STA), lambda i: (i, 0, 0, 0)),
        compiler_params=pltpu.CompilerParams(vmem_limit_bytes=16 * MIB),
        name="combine",
    )(mine, theirs)


def body(records, validity, partners):
    place = lax.axis_index("tm")
    z_hi, chip, core = place // HALF, place % HALF // 2, place % 2
    block_id = lax.axis_index("sta")
    pair = lax.dynamic_index_in_dim(partners, block_id, 0, keepdims=False)

    parts = []
    for i, white in enumerate(whitened(records, validity)):
        other = send(white, to_other_half)
        first = jnp.where(z_hi == 0, white, other)
        second = jnp.where(z_hi == 0, other, white)
        depth = CHUNKS[i] * COLS
        parts.append(jnp.concatenate([first[:depth], second[:depth], first[depth:], second[depth:]], axis=0))

    mine = [lax.dynamic_slice_in_dim(part, z_hi * 128, 128, axis=1) for part in parts]
    rows = jnp.concatenate(mine, axis=0).T.reshape(CHIPS, CHIP_ROWS, -1)
    rows = lax.all_to_all(rows, "tm", 0, 0, axis_index_groups=CHIP_GROUPS, tiled=True)
    order = (chip + jnp.array([0, CHIPS - 1, 1, 2])) % CHIPS
    rows = jnp.take(rows, order, axis=0, mode="clip")
    rows = jnp.where(core == 0, jnp.roll(rows, ROW_BLOCK, axis=1), rows)
    rows = rows.transpose(1, 0, 2)

    turned, own_mask, at = [], None, 0
    for i, windows in enumerate(CHUNKS):
        depth = 2 * windows * COLS
        own = rows[:, :, at : at + depth].reshape(CHIP_ROWS, CHIPS * depth)
        turned.append(rotated(own.astype(jnp.float32)))
        at += depth
        if i == 0:
            own_mask = rows[:, :, at : at + 2 * MASK_ROWS].reshape(CHIP_ROWS, -1)
            at += 2 * MASK_ROWS

    far = []
    for part in parts:
        near = {-1: send(part, to_block(1)), 1: send(part, to_block(-1))}
        near[-2] = send(near[-1], to_block(1))
        near[2] = send(near[1], to_block(-1))
        chosen = []
        for q in range(SLOTS):
            picked = jnp.zeros_like(part)
            for by, array in near.items():
                picked = jnp.where((pair[q] == block_id + by) & (pair[q] >= 0), array, picked)
            chosen.append(picked)
        held = jnp.concatenate(chosen, axis=1)
        far.append([held, send(held, to_chip(1)), send(held, to_chip(-1)), send(held, to_chip(2))])

    depth = 2 * CHUNKS[0] * COLS
    far_mask = jnp.concatenate([piece[depth:] for piece in far[0]], axis=0)
    tally = jnp.dot(own_mask, far_mask, preferred_element_type=jnp.float32)

    acc = None
    for i in range(len(CHUNKS) - 1):
        acc = into_lags(turned[i], far[i], 2 * CHUNKS[i] * COLS, 0, CHIP_ROWS, acc)
    last = functools.partial(into_lags, turned[-1], far[-1], 2 * CHUNKS[-1] * COLS, acc=acc, tally=tally)
    theirs = send(last(0, ROW_BLOCK, dtype=jnp.bfloat16), to_core)
    return combined(last(ROW_BLOCK, ROW_BLOCK), theirs)


def solution(mesh):
    return jax.shard_map(
        body,
        mesh=mesh,
        in_specs=(P("sta", "tm"), P("sta", "tm"), P()),
        out_specs=P(("sta", "tm"), None, None, None),
        check_vma=False,
    )
```

time: 300 us -> 145 us (0.48)
  the two profiles are of different devices: /device:TPU:11 before, /device:TPU:27 now
where the time goes in v1:
time: 145 us; the launch traced here: 144 us
  starting transfers between devices  81.1 us (56%)
  waiting for transfers between devices  22.4 us (15%)
  Pallas kernels  17.6 us (12%)
  local copies, waits for them, and re-layouts  14.1 us (10%)
  between operations  6.8 us (5%)
  other arithmetic  2.15 us (1%)
    ppermute x17, starting transfers between devices, send(): return lax.ppermute(array, AXES, routes(target))  76.9 us
    ppermute x17, waiting for transfers between devices, send(): return lax.ppermute(array, AXES, routes(target))  22.4 us
    pallas_call x3, Pallas kernels, into_lags(): pl.pallas_call(functools.partial(lags_kernel, depth, len(far), acc is not...  10.8 us
    unnamed x21, local copies, waits for them, and re-layouts  8.78 us
    pallas_call x2, Pallas kernels, rotated(): pl.pallas_call(functools.partial(rotate_kernel, width // COLS), out_shape...  5.06 us
    all_to_all x1, starting transfers between devices, body(): lax.all_to_all(rows, 'tm', 0, 0, axis_index_groups=CHIP_GROUPS, tiled=True)  4.26 us
  transfers between devices with their start and end apart: 18, of which 5 were waited for; matrix products, arithmetic and copies ran while one was open for 3% of the time, Pallas kernels for 10%

profile of v1, /device:TPU:27, one launch (start us, length us, event | category | flops | bytes accessed | tf_op | source)
XLA Modules:
  0.0 144.3 jit_solution(15330888820292711353)
XLA Ops:
  0.0 1.6 %copy.17.rec_ref = bf16[256,1800]{1,0:T(8,128)(2,1)S(1)} copy(bf16[256,1800]{0,1:T(8,128)(2,1)} %param.12) | data formatting | bytes 1843200 | tf_op args[0]
  1.6 0.7 convert_bitcast_fusion.2
  2.3 0.9 copy-done.2
  3.2 0.9 copy-done.3
  4.1 0.9 copy-done.4
  5.1 0.8 copy-done.7
  5.8 1.4 whiten.1
  7.2 15.4 %collective-permute-start = (bf16[272,256]{1,0:T(8,128)(2,1)S(1)}, bf16[272,256]{1,0:T(8,128)(2,1)S(1)}, u32[]{:S(2)}, u32[]{:S(2)}) collective-permute-start(bf16[272,256]{1,0:T(8,128)(2,1)S(1)} %get-tuple-element.7), channel_id=1, source_target_pairs={{0,8},{1,9},{2,10},{3,11},{4,12},{5,13},{6,14},{7,15},{8,0},{9,1},... | collective-permute-start | bytes 417800 | tf_op jit(solution)/shard_map/ppermute | solution.py:115
  22.7 1.9 %collective-permute-start.1 = (bf16[128,256]{1,0:T(8,128)(2,1)S(1)}, bf16[128,256]{1,0:T(8,128)(2,1)S(1)}, u32[]{:S(2)}, u32[]{:S(2)}) collective-permute-start(bf16[128,256]{1,0:T(8,128)(2,1)S(1)} %get-tuple-element.8), channel_id=1, source_target_pairs={{0,8},{1,9},{2,10},{3,11},{4,12},{5,13},{6,14},{7,15},{8,0},{9,1},... | collective-permute-start | bytes 196616 | tf_op jit(solution)/shard_map/ppermute | solution.py:115
  24.7 0.1 constant_dynamic-slice_fusion
  24.8 11.7 %collective-permute-done.1 = bf16[128,256]{1,0:T(8,128)(2,1)S(1)} collective-permute-done((bf16[128,256]{1,0:T(8,128)(2,1)S(1)}, bf16[128,256]{1,0:T(8,128)(2,1)S(1)}, u32[]{:S(2)}, u32[]{:S(2)}) %collective-permute-start.1) | collective-permute-done | bytes 65568 | tf_op jit(solution)/shard_map/ppermute | solution.py:115
  36.5 9.7 %collective-permute-start.2 = (bf16[256,256]{1,0:T(8,128)(2,1)S(1)}, bf16[256,256]{1,0:T(8,128)(2,1)S(1)}, u32[]{:S(2)}, u32[]{:S(2)}) collective-permute-start(bf16[256,256]{1,0:T(8,128)(2,1)S(1)} %pad_maximum_fusion.3), channel_id=1, source_target_pairs={{16,0},{17,1},{18,2},{19,3},{20,4},{21,5},{22,6},{23,7},{24,8},{25... | collective-permute-start | bytes 393224 | tf_op jit(solution)/shard_map/ppermute | solution.py:115
  46.2 1.9 %collective-permute-start.4 = (bf16[256,256]{1,0:T(8,128)(2,1)S(1)}, bf16[256,256]{1,0:T(8,128)(2,1)S(1)}, u32[]{:S(2)}, u32[]{:S(2)}) collective-permute-start(bf16[256,256]{1,0:T(8,128)(2,1)S(1)} %pad_maximum_fusion.3), channel_id=1, source_target_pairs={{0,16},{1,17},{2,18},{3,19},{4,20},{5,21},{6,22},{7,23},{8,24},{9,... | collective-permute-start | bytes 393224 | tf_op jit(solution)/shard_map/ppermute | solution.py:115
  48.4 0.8 copy.18
  49.2 4.3 %all-to-all-start = ((bf16[4,32,800]{2,1,0:T(8,128)(2,1)}), bf16[4,32,800]{2,1,0:T(8,128)(2,1)S(1)}, u32[]{:S(2)}, u32[]{:S(2)}) async-start(bf16[4,32,800]{2,1,0:T(8,128)(2,1)} %bitcast.2), calls=%async_computation | async-start | bytes 458752 | tf_op jit(solution)/shard_map/all_to_all | solution.py:282
  53.5 0.6 fusion.14
  54.1 5.5 %collective-permute-start.9 = (bf16[544,256]{1,0:T(8,128)(2,1)S(1)}, bf16[544,256]{1,0:T(8,128)(2,1)S(1)}, u32[]{:S(2)}, u32[]{:S(2)}) collective-permute-start(bf16[544,256]{1,0:T(8,128)(2,1)S(1)} %pad_maximum_fusion.1), channel_id=1, source_target_pairs={{16,0},{17,1},{18,2},{19,3},{20,4},{21,5},{22,6},{23,7},{24,8},{25... | collective-permute-start | bytes 835592 | tf_op jit(solution)/shard_map/ppermute | solution.py:115
  59.5 1.9 %collective-permute-start.11 = (bf16[544,256]{1,0:T(8,128)(2,1)S(1)}, bf16[544,256]{1,0:T(8,128)(2,1)S(1)}, u32[]{:S(2)}, u32[]{:S(2)}) collective-permute-start(bf16[544,256]{1,0:T(8,128)(2,1)S(1)} %pad_maximum_fusion.1), channel_id=1, source_target_pairs={{0,16},{1,17},{2,18},{3,19},{4,20},{5,21},{6,22},{7,23},{8,24},{9,... | collective-permute-start | bytes 835592 | tf_op jit(solution)/shard_map/ppermute | solution.py:115
  67.7 5.5 %collective-permute-start.3 = (bf16[256,256]{1,0:T(8,128)(2,1)S(1)}, bf16[256,256]{1,0:T(8,128)(2,1)}, u32[]{:S(2)}, u32[]{:S(2)}) collective-permute-start(bf16[256,256]{1,0:T(8,128)(2,1)S(1)} %collective-permute-done.2), channel_id=1, source_target_pairs={{16,0},{17,1},{18,2},{19,3},{20,4},{21,5},{22,6},{23,7},{24,8},{25... | collective-permute-start | bytes 393224 | tf_op jit(solution)/shard_map/ppermute | solution.py:115
  73.2 1.9 %collective-permute-start.5 = (bf16[256,256]{1,0:T(8,128)(2,1)S(1)}, bf16[256,256]{1,0:T(8,128)(2,1)}, u32[]{:S(2)}, u32[]{:S(2)}) collective-permute-start(bf16[256,256]{1,0:T(8,128)(2,1)S(1)} %collective-permute-done.4), channel_id=1, source_target_pairs={{0,16},{1,17},{2,18},{3,19},{4,20},{5,21},{6,22},{7,23},{8,24},{9,... | collective-permute-start | bytes 393224 | tf_op jit(solution)/shard_map/ppermute | solution.py:115
  75.1 0.6 gather_fusion
  75.7 5.5 %collective-permute-start.10 = (bf16[544,256]{1,0:T(8,128)(2,1)S(1)}, bf16[544,256]{1,0:T(8,128)(2,1)S(1)}, u32[]{:S(2)}, u32[]{:S(2)}) collective-permute-start(bf16[544,256]{1,0:T(8,128)(2,1)S(1)} %collective-permute-done.9), channel_id=1, source_target_pairs={{16,0},{17,1},{18,2},{19,3},{20,4},{21,5},{22,6},{23,7},{24,8},{25... | collective-permute-start | bytes 835592 | tf_op jit(solution)/shard_map/ppermute | solution.py:115
  81.2 1.9 %collective-permute-start.12 = (bf16[544,256]{1,0:T(8,128)(2,1)S(1)}, bf16[544,256]{1,0:T(8,128)(2,1)S(1)}, u32[]{:S(2)}, u32[]{:S(2)}) collective-permute-start(bf16[544,256]{1,0:T(8,128)(2,1)S(1)} %collective-permute-done.11), channel_id=1, source_target_pairs={{0,16},{1,17},{2,18},{3,19},{4,20},{5,21},{6,22},{7,23},{8,24},{9,... | collective-permute-start | bytes 835592 | tf_op jit(solution)/shard_map/ppermute | solution.py:115
  83.1 0.1 fusion
  83.3 1.4 collective-permute-done.10
  84.7 5.9 %collective-permute-done.12 = bf16[544,256]{1,0:T(8,128)(2,1)S(1)} collective-permute-done((bf16[544,256]{1,0:T(8,128)(2,1)S(1)}, bf16[544,256]{1,0:T(8,128)(2,1)S(1)}, u32[]{:S(2)}, u32[]{:S(2)}) %collective-permute-start.12) | collective-permute-done | bytes 278560 | tf_op jit(solution)/shard_map/ppermute | solution.py:115
  90.6 0.1 select_select_fusion.1
  90.7 3.1 %collective-permute-start.13 = (bf16[544,512]{1,0:T(8,128)(2,1)S(1)}, bf16[544,512]{1,0:T(8,128)(2,1)S(1)}, u32[]{:S(2)}, u32[]{:S(2)}) collective-permute-start(bf16[544,512]{1,0:T(8,128)(2,1)S(1)} %pad_maximum_fusion.refs_0_), channel_id=1, source_target_pairs={{0,2},{1,3},{2,4},{3,5},{4,6},{5,7},{6,0},{7,1},{8,10},{9,11},{10,... | collective-permute-start | bytes 1671176 | tf_op jit(solution)/shard_map/ppermute | solution.py:115
  93.8 2.2 %collective-permute-start.14 = (bf16[544,512]{1,0:T(8,128)(2,1)S(1)}, bf16[544,512]{1,0:T(8,128)(2,1)S(1)}, u32[]{:S(2)}, u32[]{:S(2)}) collective-permute-start(bf16[544,512]{1,0:T(8,128)(2,1)S(1)} %pad_maximum_fusion.refs_0_), channel_id=1, source_target_pairs={{0,6},{1,7},{2,0},{3,1},{4,2},{5,3},{6,4},{7,5},{8,14},{9,15},{10,... | collective-permute-start | bytes 1671176 | tf_op jit(solution)/shard_map/ppermute | solution.py:115
  96.0 3.7 %collective-permute-start.15 = (bf16[544,512]{1,0:T(8,128)(2,1)S(1)}, bf16[544,512]{1,0:T(8,128)(2,1)S(1)}, u32[]{:S(2)}, u32[]{:S(2)}) collective-permute-start(bf16[544,512]{1,0:T(8,128)(2,1)S(1)} %pad_maximum_fusion.refs_0_), channel_id=1, source_target_pairs={{0,4},{1,5},{2,6},{3,7},{4,0},{5,1},{6,2},{7,3},{8,12},{9,13},{10,... | collective-permute-start | bytes 1671176 | tf_op jit(solution)/shard_map/ppermute | solution.py:115
  99.8 0.1 convert_bitcast_fusion.1
  99.9 0.7 reshape.17
  100.6 1.8 %rotate.2.turned_ref = bf16[2304,1024]{1,0:T(8,128)(2,1)S(1)} custom-call(f32[32,1024]{1,0:T(8,128)S(1)} %bitcast.17, f32[72,128]{1,0:T(8,128)S(1)} %copy-done.5, f32[72,128]{1,0:T(8,128)S(1)} %copy-done.6), custom_call_target="tpu_custom_call" | custom-call | flops 7077888 | bytes 4718592 | tf_op jit(solution)/shard_map/rotate/pallas_call | solution.py:176
  102.4 3.3 %rotate.3.turned_ref = bf16[2304,2048]{1,0:T(8,128)(2,1)S(1)} custom-call(f32[32,2048]{1,0:T(8,128)S(1)} %bitcast.16, f32[72,128]{1,0:T(8,128)S(1)} %copy-done.5, f32[72,128]{1,0:T(8,128)S(1)} %copy-done.6), custom_call_target="tpu_custom_call" | custom-call | flops 14155776 | bytes 9437184 | tf_op jit(solution)/shard_map/rotate/pallas_call | solution.py:176
  105.7 3.7 %copy-done.1 = bf16[2304,2048]{1,0:T(8,128)(2,1)} copy-done((bf16[2304,2048]{1,0:T(8,128)(2,1)}, bf16[2304,2048]{1,0:T(8,128)(2,1)S(1)}, u32[]{:S(2)}) %copy-start.1) | copy-done | bytes 9437208
  109.4 1.0 select_select_fusion.3
  110.4 2.5 %collective-permute-start.6 = (bf16[256,512]{1,0:T(8,128)(2,1)S(1)}, bf16[256,512]{1,0:T(8,128)(2,1)S(1)}, u32[]{:S(2)}, u32[]{:S(2)}) collective-permute-start(bf16[256,512]{1,0:T(8,128)(2,1)S(1)} %pad_maximum_fusion.2.refs_0_), channel_id=1, source_target_pairs={{0,2},{1,3},{2,4},{3,5},{4,6},{5,7},{6,0},{7,1},{8,10},{9,11},{10,... | collective-permute-start | bytes 786440 | tf_op jit(solution)/shard_map/ppermute | solution.py:115
  113.0 2.8 %collective-permute-start.7 = (bf16[256,512]{1,0:T(8,128)(2,1)S(1)}, bf16[256,512]{1,0:T(8,128)(2,1)S(1)}, u32[]{:S(2)}, u32[]{:S(2)}) collective-permute-start(bf16[256,512]{1,0:T(8,128)(2,1)S(1)} %pad_maximum_fusion.2.refs_0_), channel_id=1, source_target_pairs={{0,6},{1,7},{2,0},{3,1},{4,2},{5,3},{6,4},{7,5},{8,14},{9,15},{10,... | collective-permute-start | bytes 786440 | tf_op jit(solution)/shard_map/ppermute | solution.py:115
  115.8 3.4 %collective-permute-start.8 = (bf16[256,512]{1,0:T(8,128)(2,1)S(1)}, bf16[256,512]{1,0:T(8,128)(2,1)S(1)}, u32[]{:S(2)}, u32[]{:S(2)}) collective-permute-start(bf16[256,512]{1,0:T(8,128)(2,1)S(1)} %pad_maximum_fusion.2.refs_0_), channel_id=1, source_target_pairs={{0,4},{1,5},{2,6},{3,7},{4,0},{5,1},{6,2},{7,3},{8,12},{9,13},{10,... | collective-permute-start | bytes 786440 | tf_op jit(solution)/shard_map/ppermute | solution.py:115
  119.2 7.6 %lags.3.refs_4_ = f32[2304,512]{1,0:T(8,128)S(1)} custom-call(bf16[2304,2048]{1,0:T(8,128)(2,1)} %copy-done.1, bf16[544,512]{1,0:T(8,128)(2,1)S(1)} %pad_maximum_fusion.refs_0_, bf16[544,512]{1,0:T(8,128)(2,1)S(1)} %collective-permute-done.13.refs_1_, bf16[544,512]{1,0:T(8,128)(2,1)S(1)} %collective-permute-done.14.refs_2_, ...), custom_call_target="tpu_custom_call" | custom-call | flops 4831838208 | bytes 14155776 | tf_op jit(solution)/shard_map/lags/pallas_call | solution.py:226
  126.9 0.1 fusion.1.refs_5_
  127.0 2.4 %collective-permute-done.8.refs_3_ = bf16[256,512]{1,0:T(8,128)(2,1)S(1)} collective-permute-done((bf16[256,512]{1,0:T(8,128)(2,1)S(1)}, bf16[256,512]{1,0:T(8,128)(2,1)S(1)}, u32[]{:S(2)}, u32[]{:S(2)}) %collective-permute-start.8) | collective-permute-done | bytes 262176 | tf_op jit(solution)/shard_map/ppermute | solution.py:115
  129.5 1.6 %lags.5 = bf16[1152,512]{1,0:T(8,128)(2,1)S(1)} custom-call(bf16[2304,1024]{1,0:T(8,128)(2,1)S(1)} %rotate.2.turned_ref, bf16[256,512]{1,0:T(8,128)(2,1)S(1)} %pad_maximum_fusion.2.refs_0_, bf16[256,512]{1,0:T(8,128)(2,1)S(1)} %collective-permute-done.6.refs_1_, bf16[256,512]{1,0:T(8,128)(2,1)S(1)} %collective-permute-done.7.refs_2_, ...), custom_call_target="tpu_custom_call" | custom-call | flops 1207959552 | bytes 4718592 | tf_op jit(solution)/shard_map/lags/pallas_call | solution.py:226
  131.1 8.0 %collective-permute-start.16 = (bf16[1152,512]{1,0:T(8,128)(2,1)S(1)}, bf16[1152,512]{1,0:T(8,128)(2,1)S(1)}, u32[]{:S(2)}, u32[]{:S(2)}) collective-permute-start(bf16[1152,512]{1,0:T(8,128)(2,1)S(1)} %lags.5), channel_id=1, source_target_pairs={{0,1},{1,0},{2,3},{3,2},{4,5},{5,4},{6,7},{7,6},{8,9},{9,8},{10,11... | collective-permute-start | bytes 3538952 | tf_op jit(solution)/shard_map/ppermute | solution.py:115
  139.1 1.6 %lags.4.mine_ref = f32[1152,512]{1,0:T(8,128)S(1)} custom-call(bf16[2304,1024]{1,0:T(8,128)(2,1)S(1)} %rotate.2.turned_ref, bf16[256,512]{1,0:T(8,128)(2,1)S(1)} %pad_maximum_fusion.2.refs_0_, bf16[256,512]{1,0:T(8,128)(2,1)S(1)} %collective-permute-done.6.refs_1_, bf16[256,512]{1,0:T(8,128)(2,1)S(1)} %collective-permute-done.7.refs_2_, ...), custom_call_target="tpu_custom_call" | custom-call | flops 1207959552 | bytes 4718592 | tf_op jit(solution)/shard_map/lags/pallas_call | solution.py:226
  140.7 0.9 collective-permute-done.16.theirs_ref
  141.6 0.3 combine.1
  141.9 2.4 %copy.22 = f32[16,2,65,256]{3,1,2,0:T(2,128)} copy(f32[16,2,65,256]{3,2,1,0:T(8,128)S(1)} %combine.1) | data formatting | bytes 4259840 | tf_op jit(solution)/shard_map/combine/pallas_call | solution.py:255
  (54 shorter events, 0.4 us)
Async XLA Ops:
  0.0 24.7 %copy-start = (s32[32,2]{0,1:T(2,128)S(1)}, s32[32,2]{0,1:T(2,128)}, u32[]{:S(2)}) copy-start(s32[32,2]{0,1:T(2,128)} %param.14) | copy-start | bytes 772
  0.0 24.7 %copy-start.9 = (s32[4]{0:T(128)S(1)}, s32[4]{0:T(128)}, u32[]{:S(2)}) copy-start(s32[4]{0:T(128)} %constant.102.clone) | copy-start | bytes 52
  2.3 0.9 copy-start.2
  3.2 0.9 copy-start.3
  4.1 0.9 copy-start.4
  5.0 0.8 copy-start.7
  7.2 41.0 %collective-permute-start = (bf16[272,256]{1,0:T(8,128)(2,1)S(1)}, bf16[272,256]{1,0:T(8,128)(2,1)S(1)}, u32[]{:S(2)}, u32[]{:S(2)}) collective-permute-start(bf16[272,256]{1,0:T(8,128)(2,1)S(1)} %get-tuple-element.7), channel_id=1, source_target_pairs={{0,8},{1,9},{2,10},{3,11},{4,12},{5,13},{6,14},{7,15},{8,0},{9,1},... | collective-permute-start | bytes 417800 | tf_op jit(solution)/shard_map/ppermute | solution.py:115
  22.7 13.8 %collective-permute-start.1 = (bf16[128,256]{1,0:T(8,128)(2,1)S(1)}, bf16[128,256]{1,0:T(8,128)(2,1)S(1)}, u32[]{:S(2)}, u32[]{:S(2)}) collective-permute-start(bf16[128,256]{1,0:T(8,128)(2,1)S(1)} %get-tuple-element.8), channel_id=1, source_target_pairs={{0,8},{1,9},{2,10},{3,11},{4,12},{5,13},{6,14},{7,15},{8,0},{9,1},... | collective-permute-start | bytes 196616 | tf_op jit(solution)/shard_map/ppermute | solution.py:115
  36.5 31.1 %collective-permute-start.2 = (bf16[256,256]{1,0:T(8,128)(2,1)S(1)}, bf16[256,256]{1,0:T(8,128)(2,1)S(1)}, u32[]{:S(2)}, u32[]{:S(2)}) collective-permute-start(bf16[256,256]{1,0:T(8,128)(2,1)S(1)} %pad_maximum_fusion.3), channel_id=1, source_target_pairs={{16,0},{17,1},{18,2},{19,3},{20,4},{21,5},{22,6},{23,7},{24,8},{25... | collective-permute-start | bytes 393224 | tf_op jit(solution)/shard_map/ppermute | solution.py:115
  46.2 26.9 %collective-permute-start.4 = (bf16[256,256]{1,0:T(8,128)(2,1)S(1)}, bf16[256,256]{1,0:T(8,128)(2,1)S(1)}, u32[]{:S(2)}, u32[]{:S(2)}) collective-permute-start(bf16[256,256]{1,0:T(8,128)(2,1)S(1)} %pad_maximum_fusion.3), channel_id=1, source_target_pairs={{0,16},{1,17},{2,18},{3,19},{4,20},{5,21},{6,22},{7,23},{8,24},{9,... | collective-permute-start | bytes 393224 | tf_op jit(solution)/shard_map/ppermute | solution.py:115
  49.2 25.9 %all-to-all-start = ((bf16[4,32,800]{2,1,0:T(8,128)(2,1)}), bf16[4,32,800]{2,1,0:T(8,128)(2,1)S(1)}, u32[]{:S(2)}, u32[]{:S(2)}) async-start(bf16[4,32,800]{2,1,0:T(8,128)(2,1)} %bitcast.2), calls=%async_computation | async-start | bytes 458752 | tf_op jit(solution)/shard_map/all_to_all | solution.py:282
  54.1 21.7 %collective-permute-start.9 = (bf16[544,256]{1,0:T(8,128)(2,1)S(1)}, bf16[544,256]{1,0:T(8,128)(2,1)S(1)}, u32[]{:S(2)}, u32[]{:S(2)}) collective-permute-start(bf16[544,256]{1,0:T(8,128)(2,1)S(1)} %pad_maximum_fusion.1), channel_id=1, source_target_pairs={{16,0},{17,1},{18,2},{19,3},{20,4},{21,5},{22,6},{23,7},{24,8},{25... | collective-permute-start | bytes 835592 | tf_op jit(solution)/shard_map/ppermute | solution.py:115
  59.5 21.7 %collective-permute-start.11 = (bf16[544,256]{1,0:T(8,128)(2,1)S(1)}, bf16[544,256]{1,0:T(8,128)(2,1)S(1)}, u32[]{:S(2)}, u32[]{:S(2)}) collective-permute-start(bf16[544,256]{1,0:T(8,128)(2,1)S(1)} %pad_maximum_fusion.1), channel_id=1, source_target_pairs={{0,16},{1,17},{2,18},{3,19},{4,20},{5,21},{6,22},{7,23},{8,24},{9,... | collective-permute-start | bytes 835592 | tf_op jit(solution)/shard_map/ppermute | solution.py:115
  67.7 41.7 %collective-permute-start.3 = (bf16[256,256]{1,0:T(8,128)(2,1)S(1)}, bf16[256,256]{1,0:T(8,128)(2,1)}, u32[]{:S(2)}, u32[]{:S(2)}) collective-permute-start(bf16[256,256]{1,0:T(8,128)(2,1)S(1)} %collective-permute-done.2), channel_id=1, source_target_pairs={{16,0},{17,1},{18,2},{19,3},{20,4},{21,5},{22,6},{23,7},{24,8},{25... | collective-permute-start | bytes 393224 | tf_op jit(solution)/shard_map/ppermute | solution.py:115
  73.2 36.2 %collective-permute-start.5 = (bf16[256,256]{1,0:T(8,128)(2,1)S(1)}, bf16[256,256]{1,0:T(8,128)(2,1)}, u32[]{:S(2)}, u32[]{:S(2)}) collective-permute-start(bf16[256,256]{1,0:T(8,128)(2,1)S(1)} %collective-permute-done.4), channel_id=1, source_target_pairs={{0,16},{1,17},{2,18},{3,19},{4,20},{5,21},{6,22},{7,23},{8,24},{9,... | collective-permute-start | bytes 393224 | tf_op jit(solution)/shard_map/ppermute | solution.py:115
  75.7 8.9 %collective-permute-start.10 = (bf16[544,256]{1,0:T(8,128)(2,1)S(1)}, bf16[544,256]{1,0:T(8,128)(2,1)S(1)}, u32[]{:S(2)}, u32[]{:S(2)}) collective-permute-start(bf16[544,256]{1,0:T(8,128)(2,1)S(1)} %collective-permute-done.9), channel_id=1, source_target_pairs={{16,0},{17,1},{18,2},{19,3},{20,4},{21,5},{22,6},{23,7},{24,8},{25... | collective-permute-start | bytes 835592 | tf_op jit(solution)/shard_map/ppermute | solution.py:115
  81.2 9.4 %collective-permute-start.12 = (bf16[544,256]{1,0:T(8,128)(2,1)S(1)}, bf16[544,256]{1,0:T(8,128)(2,1)S(1)}, u32[]{:S(2)}, u32[]{:S(2)}) collective-permute-start(bf16[544,256]{1,0:T(8,128)(2,1)S(1)} %collective-permute-done.11), channel_id=1, source_target_pairs={{0,16},{1,17},{2,18},{3,19},{4,20},{5,21},{6,22},{7,23},{8,24},{9,... | collective-permute-start | bytes 835592 | tf_op jit(solution)/shard_map/ppermute | solution.py:115
  83.2 17.4 %copy-start.5 = (f32[72,128]{1,0:T(8,128)S(1)}, f32[72,128]{1,0:T(8,128)}, u32[]{:S(2)}) copy-start(f32[72,128]{1,0:T(8,128)} %constant.103.clone.cos_ref) | copy-start | bytes 110596
  83.2 17.4 %copy-start.6 = (f32[72,128]{1,0:T(8,128)S(1)}, f32[72,128]{1,0:T(8,128)}, u32[]{:S(2)}) copy-start(f32[72,128]{1,0:T(8,128)} %constant.104.clone.sin_ref) | copy-start | bytes 110596
  90.7 25.0 %collective-permute-start.13 = (bf16[544,512]{1,0:T(8,128)(2,1)S(1)}, bf16[544,512]{1,0:T(8,128)(2,1)S(1)}, u32[]{:S(2)}, u32[]{:S(2)}) collective-permute-start(bf16[544,512]{1,0:T(8,128)(2,1)S(1)} %pad_maximum_fusion.refs_0_), channel_id=1, source_target_pairs={{0,2},{1,3},{2,4},{3,5},{4,6},{5,7},{6,0},{7,1},{8,10},{9,11},{10,... | collective-permute-start | bytes 1671176 | tf_op jit(solution)/shard_map/ppermute | solution.py:115
  93.8 25.4 %collective-permute-start.14 = (bf16[544,512]{1,0:T(8,128)(2,1)S(1)}, bf16[544,512]{1,0:T(8,128)(2,1)S(1)}, u32[]{:S(2)}, u32[]{:S(2)}) collective-permute-start(bf16[544,512]{1,0:T(8,128)(2,1)S(1)} %pad_maximum_fusion.refs_0_), channel_id=1, source_target_pairs={{0,6},{1,7},{2,0},{3,1},{4,2},{5,3},{6,4},{7,5},{8,14},{9,15},{10,... | collective-permute-start | bytes 1671176 | tf_op jit(solution)/shard_map/ppermute | solution.py:115
  96.0 23.2 %collective-permute-start.15 = (bf16[544,512]{1,0:T(8,128)(2,1)S(1)}, bf16[544,512]{1,0:T(8,128)(2,1)S(1)}, u32[]{:S(2)}, u32[]{:S(2)}) collective-permute-start(bf16[544,512]{1,0:T(8,128)(2,1)S(1)} %pad_maximum_fusion.refs_0_), channel_id=1, source_target_pairs={{0,4},{1,5},{2,6},{3,7},{4,0},{5,1},{6,2},{7,3},{8,12},{9,13},{10,... | collective-permute-start | bytes 1671176 | tf_op jit(solution)/shard_map/ppermute | solution.py:115
  105.7 3.7 %copy-start.1 = (bf16[2304,2048]{1,0:T(8,128)(2,1)}, bf16[2304,2048]{1,0:T(8,128)(2,1)S(1)}, u32[]{:S(2)}) copy-start(bf16[2304,2048]{1,0:T(8,128)(2,1)S(1)} %rotate.3.turned_ref) | copy-start | bytes 28311556
  110.4 16.6 %collective-permute-start.6 = (bf16[256,512]{1,0:T(8,128)(2,1)S(1)}, bf16[256,512]{1,0:T(8,128)(2,1)S(1)}, u32[]{:S(2)}, u32[]{:S(2)}) collective-permute-start(bf16[256,512]{1,0:T(8,128)(2,1)S(1)} %pad_maximum_fusion.2.refs_0_), channel_id=1, source_target_pairs={{0,2},{1,3},{2,4},{3,5},{4,6},{5,7},{6,0},{7,1},{8,10},{9,11},{10,... | collective-permute-start | bytes 786440 | tf_op jit(solution)/shard_map/ppermute | solution.py:115
  113.0 14.1 %collective-permute-start.7 = (bf16[256,512]{1,0:T(8,128)(2,1)S(1)}, bf16[256,512]{1,0:T(8,128)(2,1)S(1)}, u32[]{:S(2)}, u32[]{:S(2)}) collective-permute-start(bf16[256,512]{1,0:T(8,128)(2,1)S(1)} %pad_maximum_fusion.2.refs_0_), channel_id=1, source_target_pairs={{0,6},{1,7},{2,0},{3,1},{4,2},{5,3},{6,4},{7,5},{8,14},{9,15},{10,... | collective-permute-start | bytes 786440 | tf_op jit(solution)/shard_map/ppermute | solution.py:115
  115.8 11.1 %copy-start.8 = (bf16[32,128]{1,0:T(8,128)(2,1)S(1)}, bf16[32,128]{1,0:T(8,128)(2,1)}, u32[]{:S(2)}) copy-start(bf16[32,128]{1,0:T(8,128)(2,1)} %reshape.17) | copy-start | bytes 24580
  115.8 13.7 %collective-permute-start.8 = (bf16[256,512]{1,0:T(8,128)(2,1)S(1)}, bf16[256,512]{1,0:T(8,128)(2,1)S(1)}, u32[]{:S(2)}, u32[]{:S(2)}) collective-permute-start(bf16[256,512]{1,0:T(8,128)(2,1)S(1)} %pad_maximum_fusion.2.refs_0_), channel_id=1, source_target_pairs={{0,4},{1,5},{2,6},{3,7},{4,0},{5,1},{6,2},{7,3},{8,12},{9,13},{10,... | collective-permute-start | bytes 786440 | tf_op jit(solution)/shard_map/ppermute | solution.py:115
  131.1 10.5 %collective-permute-start.16 = (bf16[1152,512]{1,0:T(8,128)(2,1)S(1)}, bf16[1152,512]{1,0:T(8,128)(2,1)S(1)}, u32[]{:S(2)}, u32[]{:S(2)}) collective-permute-start(bf16[1152,512]{1,0:T(8,128)(2,1)S(1)} %lags.5), channel_id=1, source_target_pairs={{0,1},{1,0},{2,3},{3,2},{4,5},{5,4},{6,7},{7,6},{8,9},{9,8},{10,11... | collective-permute-start | bytes 3538952 | tf_op jit(solution)/shard_map/ppermute | solution.py:115

commit v2 on v1

v2 whole, which is shorter than its diff:
```python
import functools
import math

import jax
import jax.numpy as jnp
import numpy as np
from jax import lax
from jax.experimental import pallas as pl
from jax.experimental.pallas import tpu as pltpu
from jax.sharding import PartitionSpec as P

WIN = 600
BINS = 64
LAG = 32
SLOTS = 2
STA = 256
BLOCKS = 32
TM = 16
HALF = 8
CHIPS = 4
COLS = 2 * BINS
LAGS = 2 * LAG + 1
LPAD = 72
TALLY_ROW = LAGS
MASK_ROWS = 16
ROW_BLOCK = 128 // HALF
CHIP_ROWS = 2 * ROW_BLOCK
WHITE = 3 * COLS
SENT = WHITE + MASK_ROWS
WIDE = WHITE + 128
TURNS = (0, 1, -1, 2)
TILE = 8 * LPAD
DEEP = CHIPS * WHITE
SPAN = 616
AXES = ("sta", "tm")
MIB = 1 << 20


def forward_table():
    sample = np.arange(WIN)
    harmonic = np.arange(1, BINS + 1)
    residue = sample[:, None] * harmonic[None, :] % WIN
    phase = residue.astype(np.float32) * np.float32(2.0 * math.pi / WIN)
    taper = np.float32(0.5) - np.float32(0.5) * np.cos(
        (sample.astype(np.float32) + np.float32(0.5)) * np.float32(2.0 * math.pi / WIN)
    )
    table = np.concatenate([taper[:, None] * np.cos(phase), -taper[:, None] * np.sin(phase)], axis=1)
    return (table * np.float32(1.0 / math.sqrt(WIN))).astype(jnp.bfloat16)


def window_start(w):
    return w * (WIN // 16 * 16)


def window_tables(win_dev):
    table = forward_table()
    out = np.zeros((win_dev, COLS, SPAN), table.dtype)
    for w in range(win_dev):
        at = w * WIN - window_start(w)
        out[w, :, at : at + WIN] = table.T
    return out


def band_average():
    bins = np.arange(BINS)
    nearby = (np.abs(bins[:, None] - bins[None, :]) <= 2).astype(np.float32)
    return np.ascontiguousarray((nearby / nearby.sum(axis=0, keepdims=True)).T)


def lag_tables():
    lags = np.arange(LAGS) - LAG
    harmonic = np.arange(1, BINS + 1)
    phase = np.mod(lags[:, None] * harmonic[None, :], WIN) * (2.0 * math.pi / WIN)
    cosine = np.zeros((LPAD, COLS), np.float32)
    sine = np.zeros((LPAD, COLS), np.float32)
    cosine[:LAGS] = np.tile(np.cos(phase), (1, 2))
    sine[:LAGS] = np.concatenate([-np.sin(phase), np.sin(phase)], axis=1)
    return cosine, sine


def routes(target):
    pairs = []
    for b in range(BLOCKS):
        for t in range(TM):
            there = target(b, t)
            if there is not None:
                pairs.append((b * TM + t, there[0] * TM + there[1]))
    return pairs


def to_other_half(b, t):
    return b, (t + HALF) % TM


def to_block(by):
    def target(b, t):
        nb = b + by
        if not 0 <= nb < BLOCKS:
            return None
        return nb, t if nb // 8 == b // 8 else (t + HALF) % TM

    return target


def to_chip(by):
    return lambda b, t: (b, t // HALF * HALF + (t % HALF // 2 + by) % CHIPS * 2 + t % 2)


def to_core(b, t):
    return b, t ^ 1


def send(array, target):
    return lax.ppermute(array, AXES, routes(target))


VMEM = pl.BlockSpec(memory_space=pltpu.VMEM)
SMEM = pl.BlockSpec(memory_space=pltpu.SMEM)
ANY = pl.BlockSpec(memory_space=pl.ANY)


def store_rows(out_ref, white, z_hi):
    lanes = pl.ds(pl.multiple_of(z_hi * 128, 128), 128)
    for g in range(WHITE // COLS):
        block = white[g * COLS : (g + 1) * COLS, lanes].astype(jnp.float32)
        out_ref[:, g * COLS : (g + 1) * COLS] = block.T.astype(jnp.bfloat16)
    mask = white[WHITE:SENT, lanes].astype(jnp.float32)
    mask = jnp.concatenate([mask, jnp.zeros((128 - MASK_ROWS, 128), jnp.float32)], axis=0)
    out_ref[:, WHITE:] = mask.T.astype(jnp.bfloat16)


def whiten_kernel(place_ref, rec_hbm, mask_hbm, avg_hbm, table_hbm, out_ref, rows_ref, rec, mask_in, avg, table, sems):
    win_dev = table_hbm.shape[0]
    copies = [pltpu.make_async_copy(mask_hbm, mask_in, sems.at[0]), pltpu.make_async_copy(avg_hbm, avg, sems.at[1])]
    for w in range(win_dev):
        copies.append(pltpu.make_async_copy(table_hbm.at[w], table.at[w], sems.at[2 + 2 * w]))
        samples = pl.ds(window_start(w), SPAN)
        copies.append(pltpu.make_async_copy(rec_hbm.at[samples], rec.at[w], sems.at[3 + 2 * w]))
    for copy in copies:
        copy.start()
    copies[0].wait()
    copies[1].wait()
    mask = mask_in[...].astype(jnp.float32)
    for w in range(win_dev):
        copies[2 + 2 * w].wait()
        copies[3 + 2 * w].wait()
        spectra = jnp.dot(table[w], rec[w], preferred_element_type=jnp.float32)
        real, imag = spectra[:BINS], spectra[BINS:]
        power = real * real + imag * imag
        smooth = jnp.dot(avg[...], power, precision=lax.Precision.HIGHEST, preferred_element_type=jnp.float32)
        scale = mask[w : w + 1] / jnp.sqrt(smooth + 0.05)
        out_ref[w * COLS : w * COLS + BINS] = (real * scale).astype(jnp.bfloat16)
        out_ref[w * COLS + BINS : (w + 1) * COLS] = (imag * scale).astype(jnp.bfloat16)
    empty = jnp.zeros((MASK_ROWS - win_dev, STA), jnp.float32)
    out_ref[WHITE:] = jnp.concatenate([mask, empty], axis=0).astype(jnp.bfloat16)
    store_rows(rows_ref, out_ref, place_ref[0])


def whitened(place, records, validity):
    rows, win_dev = validity.shape
    return pl.pallas_call(
        whiten_kernel,
        out_shape=[
            jax.ShapeDtypeStruct((SENT, rows), jnp.bfloat16),
            jax.ShapeDtypeStruct((128, WIDE), jnp.bfloat16),
        ],
        in_specs=[SMEM, ANY, ANY, ANY, ANY],
        out_specs=[VMEM, VMEM],
        scratch_shapes=[
            pltpu.VMEM((win_dev, SPAN, rows), records.dtype),
            pltpu.VMEM((win_dev, rows), jnp.int32),
            pltpu.VMEM((BINS, BINS), jnp.float32),
            pltpu.VMEM((win_dev, COLS, SPAN), jnp.bfloat16),
            pltpu.SemaphoreType.DMA((2 + 2 * win_dev,)),
        ],
        compiler_params=pltpu.CompilerParams(vmem_limit_bytes=60 * MIB),
        name="whiten",
    )(place, records.T, validity.T, band_average(), window_tables(win_dev))


def choose_kernel(choice_ref, place_ref, *refs):
    blocks, refs = refs[:4], refs[4:]
    outs = refs
    if len(refs) > 1:
        rows_ref, other_ref, other_rows = refs[0], refs[1], refs[-1]
        outs = refs[2:-1]
        store_rows(other_rows, other_ref, place_ref[0])
    for q in range(SLOTS):
        rows = slice(q * SENT, (q + 1) * SENT)

        @pl.when(choice_ref[q] == 0)
        def _():
            for out_ref in outs:
                out_ref[rows] = jnp.zeros((SENT, STA), jnp.bfloat16)

        for k, ref in enumerate(blocks):

            @pl.when(choice_ref[q] == k + 1)
            def _():
                for out_ref in outs:
                    out_ref[rows] = ref[...]

    if len(refs) > 1:
        for by, out_ref in zip(TURNS, outs):
            chip = lax.rem(place_ref[1] + CHIPS + by, CHIPS)
            stations = pl.ds(pl.multiple_of(chip * CHIP_ROWS, CHIP_ROWS), CHIP_ROWS)
            at = SLOTS * SENT
            for source in (rows_ref, other_rows):
                for lanes in (slice(0, STA), slice(STA, WIDE)):
                    out_ref[at : at + CHIP_ROWS] = source[stations, lanes]
                    at += CHIP_ROWS


def chosen(choice, place, blocks, own=()):
    rows = SLOTS * SENT + (4 * CHIP_ROWS if own else 0)
    count = CHIPS if own else 1
    return pl.pallas_call(
        choose_kernel,
        out_shape=[jax.ShapeDtypeStruct((rows, STA), jnp.bfloat16)] * count,
        in_specs=[SMEM, SMEM] + [VMEM] * (len(blocks) + len(own)),
        out_specs=[VMEM] * count,
        scratch_shapes=[pltpu.VMEM((128, WIDE), jnp.bfloat16)] if own else [],
        compiler_params=pltpu.CompilerParams(vmem_limit_bytes=6 * MIB),
        name="choose",
    )(choice, place, *blocks, *own)


def turn_kernel(place_ref, *refs):
    far, (cos_ref, sin_ref, out_ref, mask_ref, held) = refs[:CHIPS], refs[CHIPS:]
    core = place_ref[2]
    cosine, sine = cos_ref[...], sin_ref[...]
    for half in range(2):
        at = SLOTS * SENT + half * 2 * CHIP_ROWS
        for d in range(CHIPS):
            for h, whose in enumerate((1 - core, core)):
                here = slice(h * ROW_BLOCK, (h + 1) * ROW_BLOCK)
                for part in range(2):
                    start = pl.multiple_of(at + part * CHIP_ROWS + whose * ROW_BLOCK, ROW_BLOCK)
                    rows = far[d][pl.ds(start, ROW_BLOCK)]
                    held[d, here, part * STA : (part + 1) * STA] = rows.astype(jnp.float32)
        mask = held[0, :, WHITE:]
        for d in range(1, CHIPS):
            mask += pltpu.roll(held[d, :, WHITE:], d * MASK_ROWS, 1)
        mask_ref[half] = mask.astype(jnp.bfloat16)

        def eight(i, carry):
            stations = pl.ds(pl.multiple_of(i * 8, 8), 8)
            for d in range(CHIPS):
                for g in range(WHITE // COLS):
                    block = held[d, stations, g * COLS : (g + 1) * COLS]
                    swapped = pltpu.roll(block, BINS, 1)
                    lanes = slice(d * WHITE + g * COLS, d * WHITE + (g + 1) * COLS)
                    for k in range(0, 8, 2):
                        turned = [block[m : m + 1] * cosine + swapped[m : m + 1] * sine for m in (k, k + 1)]
                        at = pl.multiple_of(i * TILE + k * LPAD, 2 * LPAD)
                        out_ref[half, pl.ds(at, 2 * LPAD), lanes] = jnp.concatenate(turned, axis=0).astype(jnp.bfloat16)
            return carry

        lax.fori_loop(0, CHIP_ROWS // 8, eight, 0)


def turned_rows(place, far):
    cosine, sine = lag_tables()
    height = CHIP_ROWS * LPAD
    return pl.pallas_call(
        turn_kernel,
        out_shape=[
            jax.ShapeDtypeStruct((2, height, DEEP), jnp.bfloat16),
            jax.ShapeDtypeStruct((2, CHIP_ROWS, 128), jnp.bfloat16),
        ],
        in_specs=[SMEM] + [VMEM] * (CHIPS + 2),
        out_specs=[VMEM, VMEM],
        scratch_shapes=[pltpu.VMEM((CHIPS, CHIP_ROWS, WIDE), jnp.float32)],
        compiler_params=pltpu.CompilerParams(vmem_limit_bytes=18 * MIB),
        cost_estimate=pl.CostEstimate(flops=6 * height * DEEP, bytes_accessed=4 * height * DEEP, transcendentals=0),
        name="turn",
    )(place, *far, cosine, sine)


def lags_kernel(half, first, count, has_acc, choice_ref, turned_ref, valid_ref, *refs):
    far = refs[:CHIPS]
    acc_ref = refs[CHIPS] if has_acc else None
    out_ref = refs[-1]
    which = [(choice_ref[SLOTS + q] + half) % 2 for q in range(SLOTS)]

    def tile(i, carry):
        source = pl.ds(pl.multiple_of(first * LPAD + i * TILE, TILE), TILE)
        target = pl.ds(pl.multiple_of(i * TILE, TILE), TILE)
        for q in range(SLOTS):
            lanes = slice(q * STA, (q + 1) * STA)
            piece = jnp.concatenate([ref[q * SENT : q * SENT + WHITE] for ref in far], axis=0)
            total = jnp.dot(turned_ref[which[q], source], piece, preferred_element_type=jnp.float32)
            if has_acc:
                total += acc_ref[source, lanes]
            out_ref[target, lanes] = total.astype(out_ref.dtype)
        return carry

    lax.fori_loop(0, count * LPAD // TILE, tile, 0)
    for q in range(SLOTS):
        lanes = slice(q * STA, (q + 1) * STA)
        mask = jnp.concatenate([ref[q * SENT + WHITE : (q + 1) * SENT] for ref in far], axis=0)
        valid = valid_ref[which[q], first : first + count, : CHIPS * MASK_ROWS]
        tally = jnp.dot(valid, mask, preferred_element_type=jnp.float32)
        for m in range(count):
            row = m * LPAD + TALLY_ROW
            value = tally[m : m + 1]
            if has_acc:
                value += acc_ref[first * LPAD + row : first * LPAD + row + 1, lanes]
            out_ref[row : row + 1, lanes] = value.astype(out_ref.dtype)


def into_lags(choice, own, far, half, first, count, acc=None, dtype=jnp.float32):
    args = [choice, *own, *far] + ([] if acc is None else [acc])
    return pl.pallas_call(
        functools.partial(lags_kernel, half, first, count, acc is not None),
        out_shape=jax.ShapeDtypeStruct((count * LPAD, SLOTS * STA), dtype),
        in_specs=[SMEM] + [VMEM] * (len(args) - 1),
        out_specs=VMEM,
        compiler_params=pltpu.CompilerParams(vmem_limit_bytes=8 * MIB),
        cost_estimate=pl.CostEstimate(
            flops=2 * count * LPAD * SLOTS * STA * DEEP,
            bytes_accessed=4 * count * LPAD * SLOTS * STA,
            transcendentals=0,
        ),
        name="lags",
    )(*args)


def combine_kernel(mine_ref, theirs_ref, out_ref):
    for m in range(out_ref.shape[0]):
        rows = slice(m * LPAD, (m + 1) * LPAD)
        total = mine_ref[rows] + theirs_ref[rows].astype(jnp.float32)
        result = total[:LAGS] / jnp.maximum(total[TALLY_ROW : TALLY_ROW + 1], 1.0)
        for q in range(SLOTS):
            out_ref[m, :, q] = result[:, q * STA : (q + 1) * STA]


def combined(mine, theirs):
    stations = mine.shape[0] // LPAD
    step = 4
    block = pl.BlockSpec((step * LPAD, mine.shape[1]), lambda i: (i, 0))
    out = pl.pallas_call(
        combine_kernel,
        out_shape=jax.ShapeDtypeStruct((stations, LAGS, SLOTS, STA), jnp.float32),
        grid=(stations // step,),
        in_specs=[block, block],
        out_specs=pl.BlockSpec((step, LAGS, SLOTS, STA), lambda i: (i, 0, 0, 0)),
        compiler_params=pltpu.CompilerParams(vmem_limit_bytes=8 * MIB),
        name="combine",
    )(mine, theirs)
    return out.transpose(0, 2, 1, 3)


def body(records, validity, partners):
    index = lax.axis_index("tm")
    place = jnp.stack([index // HALF, index % HALF // 2, index % 2])
    block_id = lax.axis_index("sta")
    pair = lax.dynamic_index_in_dim(partners, block_id, 0, keepdims=False)
    by = pair - block_id
    choice = jnp.where(by == -1, 1, jnp.where(by == 1, 2, jnp.where(by == -2, 3, jnp.where(by == 2, 4, 0))))
    choice = jnp.where(pair >= 0, choice, 0)
    choice = jnp.concatenate([choice, (pair // 8 != block_id // 8).astype(jnp.int32)])

    def neighbours(white):
        back, on = send(white, to_block(1)), send(white, to_block(-1))
        return [back, on, send(back, to_block(1)), send(on, to_block(-1))]

    def to_chips(arrays):
        return [arrays[0]] + [send(array, to_chip(by)) for by, array in zip(TURNS[1:], arrays[1:])]

    white, rows = whitened(place, records, validity)
    other = send(white, to_other_half)
    far = to_chips(chosen(choice, place, neighbours(white), (rows, other)))
    other_far = to_chips(chosen(choice, place, neighbours(other)) * CHIPS)
    own = turned_rows(place, far)

    acc = into_lags(choice, own, far, 0, 0, CHIP_ROWS)
    last = functools.partial(into_lags, choice, own, other_far, 1, acc=acc)
    theirs = send(last(0, ROW_BLOCK, dtype=jnp.bfloat16), to_core)
    return combined(last(ROW_BLOCK, ROW_BLOCK), theirs)


def solution(mesh):
    return jax.shard_map(
        body,
        mesh=mesh,
        in_specs=(P("sta", "tm"), P("sta", "tm"), P()),
        out_specs=P(("sta", "tm"), None, None, None),
        check_vma=False,
    )
```

time: 145 us -> 126 us (0.87)
  the two profiles are of different devices: /device:TPU:27 before, /device:TPU:9 now
where the time goes in v2:
time: 126 us; the launch traced here: 125 us
  starting transfers between devices  63.3 us (50%)
  waiting for transfers between devices  35.1 us (28%)
  Pallas kernels  23.9 us (19%)
  local copies, waits for them, and re-layouts  1.74 us (1%)
    ppermute x16, starting transfers between devices, send(): return lax.ppermute(array, AXES, routes(target))  63.3 us
    ppermute x16, waiting for transfers between devices, send(): return lax.ppermute(array, AXES, routes(target))  35.1 us
    pallas_call x3, Pallas kernels, into_lags(): pl.pallas_call(functools.partial(lags_kernel, half, first, count, acc is...  10.7 us
    pallas_call x1, Pallas kernels, turned_rows(): pl.pallas_call(turn_kernel, out_shape=[jax.ShapeDtypeStruct((2, height, D...  5.14 us
    pallas_call x1, Pallas kernels, whitened(): pl.pallas_call(whiten_kernel, out_shape=[jax.ShapeDtypeStruct((SENT, rows...  4.24 us
  transfers between devices with their start and end apart: 16, of which 7 were waited for; matrix products, arithmetic and copies ran while one was open for 0% of the time, Pallas kernels for 11%

profile of v2, /device:TPU:9, one launch (start us, length us, event | category | flops | bytes accessed | tf_op | source)
XLA Modules:
  0.0 125.1 jit_solution(9652517814748769704)
XLA Ops:
  0.1 0.6 pad_add_fusion.1.place_ref
  0.7 4.2 %whiten.1 = (bf16[400,256]{1,0:T(8,128)(2,1)}, bf16[128,512]{1,0:T(8,128)(2,1)}) custom-call(s32[3]{0:T(128)} %pad_add_fusion.1.place_ref, bf16[1800,256]{1,0:T(8,128)(2,1)} %bitcast.6, s32[3,256]{1,0:T(4,128)} %bitcast.7, f32[64,64]{1,0:T(8,128)} %constant.92.clone.avg_hbm, bf16[3,128,616]{2,1,0:T(8,128)(2,1)} %constant.93.clone.table_hbm), custom_call_target="tpu_custom_call" | custom-call | tf_op jit(solution)/shard_map/whiten/pallas_call | solution.py:161
  4.9 15.4 %collective-permute-start.4 = (bf16[400,256]{1,0:T(8,128)(2,1)}, bf16[400,256]{1,0:T(8,128)(2,1)S(1)}, u32[]{:S(2)}, u32[]{:S(2)}) collective-permute-start(bf16[400,256]{1,0:T(8,128)(2,1)} %get-tuple-element.13), channel_id=1, source_target_pairs={{0,8},{1,9},{2,10},{3,11},{4,12},{5,13},{6,14},{7,15},{8,0},{9,1},... | collective-permute-start | bytes 614408 | tf_op jit(solution)/shard_map/ppermute | solution.py:114
  20.4 1.9 %collective-permute-start.1 = (bf16[400,256]{1,0:T(8,128)(2,1)}, bf16[400,256]{1,0:T(8,128)(2,1)S(1)}, u32[]{:S(2)}, u32[]{:S(2)}) collective-permute-start(bf16[400,256]{1,0:T(8,128)(2,1)} %get-tuple-element.13), channel_id=1, source_target_pairs={{16,0},{17,1},{18,2},{19,3},{20,4},{21,5},{22,6},{23,7},{24,8},{25... | collective-permute-start | bytes 614408 | tf_op jit(solution)/shard_map/ppermute | solution.py:114
  22.3 3.4 %collective-permute-start = (bf16[400,256]{1,0:T(8,128)(2,1)}, bf16[400,256]{1,0:T(8,128)(2,1)S(1)}, u32[]{:S(2)}, u32[]{:S(2)}) collective-permute-start(bf16[400,256]{1,0:T(8,128)(2,1)} %get-tuple-element.13), channel_id=1, source_target_pairs={{0,16},{1,17},{2,18},{3,19},{4,20},{5,21},{6,22},{7,23},{8,24},{9,... | collective-permute-start | bytes 614408 | tf_op jit(solution)/shard_map/ppermute | solution.py:114
  25.7 0.2 dynamic-slice_reduce_fusion
  25.9 17.6 %collective-permute-done.1.refs_1_ = bf16[400,256]{1,0:T(8,128)(2,1)S(1)} collective-permute-done((bf16[400,256]{1,0:T(8,128)(2,1)}, bf16[400,256]{1,0:T(8,128)(2,1)S(1)}, u32[]{:S(2)}, u32[]{:S(2)}) %collective-permute-start.1) | collective-permute-done | bytes 204832 | tf_op jit(solution)/shard_map/ppermute | solution.py:114
  43.5 6.1 %collective-permute-start.3 = (bf16[400,256]{1,0:T(8,128)(2,1)S(1)}, bf16[400,256]{1,0:T(8,128)(2,1)S(1)}, u32[]{:S(2)}, u32[]{:S(2)}) collective-permute-start(bf16[400,256]{1,0:T(8,128)(2,1)S(1)} %collective-permute-done.1.refs_1_), channel_id=1, source_target_pairs={{16,0},{17,1},{18,2},{19,3},{20,4},{21,5},{22,6},{23,7},{24,8},{25... | collective-permute-start | bytes 614408 | tf_op jit(solution)/shard_map/ppermute | solution.py:114
  49.6 0.0 collective-permute-done.refs_0_
  49.6 1.9 %collective-permute-start.2 = (bf16[400,256]{1,0:T(8,128)(2,1)S(1)}, bf16[400,256]{1,0:T(8,128)(2,1)S(1)}, u32[]{:S(2)}, u32[]{:S(2)}) collective-permute-start(bf16[400,256]{1,0:T(8,128)(2,1)S(1)} %collective-permute-done.refs_0_), channel_id=1, source_target_pairs={{0,16},{1,17},{2,18},{3,19},{4,20},{5,21},{6,22},{7,23},{8,24},{9,... | collective-permute-start | bytes 614408 | tf_op jit(solution)/shard_map/ppermute | solution.py:114
  51.5 0.1 pad_add_fusion.choice_ref
  51.6 0.0 collective-permute-done.4.refs_5_
  51.6 1.9 %collective-permute-done.3.refs_3_ = bf16[400,256]{1,0:T(8,128)(2,1)S(1)} collective-permute-done((bf16[400,256]{1,0:T(8,128)(2,1)S(1)}, bf16[400,256]{1,0:T(8,128)(2,1)S(1)}, u32[]{:S(2)}, u32[]{:S(2)}) %collective-permute-start.3) | collective-permute-done | bytes 204832 | tf_op jit(solution)/shard_map/ppermute | solution.py:114
  53.5 5.9 %collective-permute-done.2.refs_2_ = bf16[400,256]{1,0:T(8,128)(2,1)S(1)} collective-permute-done((bf16[400,256]{1,0:T(8,128)(2,1)S(1)}, bf16[400,256]{1,0:T(8,128)(2,1)S(1)}, u32[]{:S(2)}, u32[]{:S(2)}) %collective-permute-start.2) | collective-permute-done | bytes 204832 | tf_op jit(solution)/shard_map/ppermute | solution.py:114
  59.4 0.9 copy-done.1
  60.3 0.6 copy-done.4
  61.0 0.9 choose.2
  61.9 3.1 %collective-permute-start.5 = (bf16[928,256]{1,0:T(8,128)(2,1)S(1)}, bf16[928,256]{1,0:T(8,128)(2,1)S(1)}, u32[]{:S(2)}, u32[]{:S(2)}) collective-permute-start(bf16[928,256]{1,0:T(8,128)(2,1)S(1)} %get-tuple-element.16), channel_id=1, source_target_pairs={{0,2},{1,3},{2,4},{3,5},{4,6},{5,7},{6,0},{7,1},{8,10},{9,11},{10,... | collective-permute-start | bytes 1425416 | tf_op jit(solution)/shard_map/ppermute | solution.py:114
  65.0 1.9 %collective-permute-start.9 = (bf16[400,256]{1,0:T(8,128)(2,1)S(1)}, bf16[400,256]{1,0:T(8,128)(2,1)S(1)}, u32[]{:S(2)}, u32[]{:S(2)}) collective-permute-start(bf16[400,256]{1,0:T(8,128)(2,1)S(1)} %collective-permute-done.4.refs_5_), channel_id=1, source_target_pairs={{16,0},{17,1},{18,2},{19,3},{20,4},{21,5},{22,6},{23,7},{24,8},{25... | collective-permute-start | bytes 614408 | tf_op jit(solution)/shard_map/ppermute | solution.py:114
  66.9 3.4 %collective-permute-start.8 = (bf16[400,256]{1,0:T(8,128)(2,1)S(1)}, bf16[400,256]{1,0:T(8,128)(2,1)S(1)}, u32[]{:S(2)}, u32[]{:S(2)}) collective-permute-start(bf16[400,256]{1,0:T(8,128)(2,1)S(1)} %collective-permute-done.4.refs_5_), channel_id=1, source_target_pairs={{0,16},{1,17},{2,18},{3,19},{4,20},{5,21},{6,22},{7,23},{8,24},{9,... | collective-permute-start | bytes 614408 | tf_op jit(solution)/shard_map/ppermute | solution.py:114
  70.3 3.4 %collective-permute-start.6 = (bf16[928,256]{1,0:T(8,128)(2,1)S(1)}, bf16[928,256]{1,0:T(8,128)(2,1)S(1)}, u32[]{:S(2)}, u32[]{:S(2)}) collective-permute-start(bf16[928,256]{1,0:T(8,128)(2,1)S(1)} %get-tuple-element.17), channel_id=1, source_target_pairs={{0,6},{1,7},{2,0},{3,1},{4,2},{5,3},{6,4},{7,5},{8,14},{9,15},{10,... | collective-permute-start | bytes 1425416 | tf_op jit(solution)/shard_map/ppermute | solution.py:114
  73.7 3.4 %collective-permute-start.7 = (bf16[928,256]{1,0:T(8,128)(2,1)S(1)}, bf16[928,256]{1,0:T(8,128)(2,1)S(1)}, u32[]{:S(2)}, u32[]{:S(2)}) collective-permute-start(bf16[928,256]{1,0:T(8,128)(2,1)S(1)} %get-tuple-element.18), channel_id=1, source_target_pairs={{0,4},{1,5},{2,6},{3,7},{4,0},{5,1},{6,2},{7,3},{8,12},{9,13},{10,... | collective-permute-start | bytes 1425416 | tf_op jit(solution)/shard_map/ppermute | solution.py:114
  77.1 0.0 collective-permute-done.9.refs_1_
  77.1 4.0 %collective-permute-start.11 = (bf16[400,256]{1,0:T(8,128)(2,1)S(1)}, bf16[400,256]{1,0:T(8,128)(2,1)S(1)}, u32[]{:S(2)}, u32[]{:S(2)}) collective-permute-start(bf16[400,256]{1,0:T(8,128)(2,1)S(1)} %collective-permute-done.9.refs_1_), channel_id=1, source_target_pairs={{16,0},{17,1},{18,2},{19,3},{20,4},{21,5},{22,6},{23,7},{24,8},{25... | collective-permute-start | bytes 614408 | tf_op jit(solution)/shard_map/ppermute | solution.py:114
  81.2 0.0 collective-permute-done.8.refs_0_
  81.2 1.9 %collective-permute-start.10 = (bf16[400,256]{1,0:T(8,128)(2,1)S(1)}, bf16[400,256]{1,0:T(8,128)(2,1)S(1)}, u32[]{:S(2)}, u32[]{:S(2)}) collective-permute-start(bf16[400,256]{1,0:T(8,128)(2,1)S(1)} %collective-permute-done.8.refs_0_), channel_id=1, source_target_pairs={{0,16},{1,17},{2,18},{3,19},{4,20},{5,21},{6,22},{7,23},{8,24},{9,... | collective-permute-start | bytes 614408 | tf_op jit(solution)/shard_map/ppermute | solution.py:114
  83.1 0.8 collective-permute-done.11.refs_3_
  83.9 6.0 %collective-permute-done.10.refs_2_ = bf16[400,256]{1,0:T(8,128)(2,1)S(1)} collective-permute-done((bf16[400,256]{1,0:T(8,128)(2,1)S(1)}, bf16[400,256]{1,0:T(8,128)(2,1)S(1)}, u32[]{:S(2)}, u32[]{:S(2)}) %collective-permute-start.10) | collective-permute-done | bytes 204832 | tf_op jit(solution)/shard_map/ppermute | solution.py:114
  90.0 0.6 choose.3.refs_0_
  90.6 3.2 %collective-permute-start.14 = (bf16[800,256]{1,0:T(8,128)(2,1)S(1)}, bf16[800,256]{1,0:T(8,128)(2,1)S(1)}, u32[]{:S(2)}, u32[]{:S(2)}) collective-permute-start(bf16[800,256]{1,0:T(8,128)(2,1)S(1)} %choose.3.refs_0_), channel_id=1, source_target_pairs={{0,4},{1,5},{2,6},{3,7},{4,0},{5,1},{6,2},{7,3},{8,12},{9,13},{10,... | collective-permute-start | bytes 1228808 | tf_op jit(solution)/shard_map/ppermute | solution.py:114
  93.8 3.2 %collective-permute-start.13 = (bf16[800,256]{1,0:T(8,128)(2,1)S(1)}, bf16[800,256]{1,0:T(8,128)(2,1)S(1)}, u32[]{:S(2)}, u32[]{:S(2)}) collective-permute-start(bf16[800,256]{1,0:T(8,128)(2,1)S(1)} %choose.3.refs_0_), channel_id=1, source_target_pairs={{0,6},{1,7},{2,0},{3,1},{4,2},{5,3},{6,4},{7,5},{8,14},{9,15},{10,... | collective-permute-start | bytes 1228808 | tf_op jit(solution)/shard_map/ppermute | solution.py:114
  97.0 0.0 collective-permute-done.5.refs_1_
  97.0 2.1 %collective-permute-start.12 = (bf16[800,256]{1,0:T(8,128)(2,1)S(1)}, bf16[800,256]{1,0:T(8,128)(2,1)S(1)}, u32[]{:S(2)}, u32[]{:S(2)}) collective-permute-start(bf16[800,256]{1,0:T(8,128)(2,1)S(1)} %choose.3.refs_0_), channel_id=1, source_target_pairs={{0,2},{1,3},{2,4},{3,5},{4,6},{5,7},{6,0},{7,1},{8,10},{9,11},{10,... | collective-permute-start | bytes 1228808 | tf_op jit(solution)/shard_map/ppermute | solution.py:114
  99.1 0.0 collective-permute-done.6.refs_2_
  99.1 0.0 collective-permute-done.7.refs_3_
  99.1 0.0 copy-done.2
  99.1 0.0 copy-done.3
  99.1 0.0 copy-done.5
  99.2 5.1 %turn.1 = (bf16[2,2304,1536]{2,1,0:T(8,128)(2,1)S(1)}, bf16[2,32,128]{2,1,0:T(8,128)(2,1)S(1)}) custom-call(s32[3]{0:T(128)S(1)} %copy-done.5, bf16[928,256]{1,0:T(8,128)(2,1)S(1)} %get-tuple-element.15.refs_0_, bf16[928,256]{1,0:T(8,128)(2,1)S(1)} %collective-permute-done.5.refs_1_, bf16[928,256]{1,0:T(8,128)(2,1)S(1)} %collective-permute-done.6.refs_2_, ...), custom_call_target="tpu_custom_call" | custom-call | flops 21233664 | bytes 14155776 | tf_op jit(solution)/shard_map/turn/pallas_call | solution.py:265
  104.3 5.0 %lags.3.refs_4_ = f32[2304,512]{1,0:T(8,128)S(1)} custom-call(s32[4]{0:T(128)S(1)} %pad_add_fusion.choice_ref, bf16[2,2304,1536]{2,1,0:T(8,128)(2,1)S(1)} %get-tuple-element.19.turned_ref, bf16[2,32,128]{2,1,0:T(8,128)(2,1)S(1)} %get-tuple-element.20.valid_ref, bf16[928,256]{1,0:T(8,128)(2,1)S(1)} %get-tuple-element.15.refs_0_, ...), custom_call_target="tpu_custom_call" | custom-call | flops 3623878656 | bytes 4718592 | tf_op jit(solution)/shard_map/lags/pallas_call | solution.py:314
  109.3 0.0 collective-permute-done.14.refs_3_
  109.3 1.0 collective-permute-done.13.refs_2_
  110.3 1.8 %collective-permute-done.12.refs_1_ = bf16[800,256]{1,0:T(8,128)(2,1)S(1)} collective-permute-done((bf16[800,256]{1,0:T(8,128)(2,1)S(1)}, bf16[800,256]{1,0:T(8,128)(2,1)S(1)}, u32[]{:S(2)}, u32[]{:S(2)}) %collective-permute-start.12) | collective-permute-done | bytes 409632 | tf_op jit(solution)/shard_map/ppermute | solution.py:114
  112.1 2.8 %lags.5 = bf16[1152,512]{1,0:T(8,128)(2,1)S(1)} custom-call(s32[4]{0:T(128)S(1)} %pad_add_fusion.choice_ref, bf16[2,2304,1536]{2,1,0:T(8,128)(2,1)S(1)} %get-tuple-element.19.turned_ref, bf16[2,32,128]{2,1,0:T(8,128)(2,1)S(1)} %get-tuple-element.20.valid_ref, bf16[800,256]{1,0:T(8,128)(2,1)S(1)} %choose.3.refs_0_, ...), custom_call_target="tpu_custom_call" | custom-call | flops 1811939328 | bytes 2359296 | tf_op jit(solution)/shard_map/lags/pallas_call | solution.py:314
  115.0 5.0 %collective-permute-start.15 = (bf16[1152,512]{1,0:T(8,128)(2,1)S(1)}, bf16[1152,512]{1,0:T(8,128)(2,1)S(1)}, u32[]{:S(2)}, u32[]{:S(2)}) collective-permute-start(bf16[1152,512]{1,0:T(8,128)(2,1)S(1)} %lags.5), channel_id=1, source_target_pairs={{0,1},{1,0},{2,3},{3,2},{4,5},{5,4},{6,7},{7,6},{8,9},{9,8},{10,11... | collective-permute-start | bytes 3538952 | tf_op jit(solution)/shard_map/ppermute | solution.py:114
  119.9 2.8 %lags.4.mine_ref = f32[1152,512]{1,0:T(8,128)S(1)} custom-call(s32[4]{0:T(128)S(1)} %pad_add_fusion.choice_ref, bf16[2,2304,1536]{2,1,0:T(8,128)(2,1)S(1)} %get-tuple-element.19.turned_ref, bf16[2,32,128]{2,1,0:T(8,128)(2,1)S(1)} %get-tuple-element.20.valid_ref, bf16[800,256]{1,0:T(8,128)(2,1)S(1)} %choose.3.refs_0_, ...), custom_call_target="tpu_custom_call" | custom-call | flops 1811939328 | bytes 2359296 | tf_op jit(solution)/shard_map/lags/pallas_call | solution.py:314
  122.8 0.0 collective-permute-done.15.theirs_ref
  122.8 2.3 %combine.1 = f32[16,65,2,256]{3,2,1,0:T(2,128)} custom-call(f32[1152,512]{1,0:T(8,128)S(1)} %lags.4.mine_ref, bf16[1152,512]{1,0:T(8,128)(2,1)S(1)} %collective-permute-done.15.theirs_ref), custom_call_target="tpu_custom_call" | custom-call | tf_op jit(solution)/shard_map/combine/pallas_call | solution.py:342
  (9 shorter events, 0.0 us)
Async XLA Ops:
  0.0 25.7 %copy-start = (s32[32,2]{0,1:T(2,128)S(1)}, s32[32,2]{0,1:T(2,128)}, u32[]{:S(2)}) copy-start(s32[32,2]{0,1:T(2,128)} %param.9) | copy-start | bytes 772
  0.0 99.1 %copy-start.2 = (f32[72,128]{1,0:T(8,128)S(1)}, f32[72,128]{1,0:T(8,128)}, u32[]{:S(2)}) copy-start(f32[72,128]{1,0:T(8,128)} %constant.95.clone.refs_5_) | copy-start | bytes 110596
  0.0 99.1 %copy-start.3 = (f32[72,128]{1,0:T(8,128)S(1)}, f32[72,128]{1,0:T(8,128)}, u32[]{:S(2)}) copy-start(f32[72,128]{1,0:T(8,128)} %constant.94.clone.refs_4_) | copy-start | bytes 110596
  0.7 98.5 %copy-start.5 = (s32[3]{0:T(128)S(1)}, s32[3]{0:T(128)}, u32[]{:S(2)}) copy-start(s32[3]{0:T(128)} %pad_add_fusion.1.place_ref) | copy-start | bytes 40
  4.9 46.7 %collective-permute-start.4 = (bf16[400,256]{1,0:T(8,128)(2,1)}, bf16[400,256]{1,0:T(8,128)(2,1)S(1)}, u32[]{:S(2)}, u32[]{:S(2)}) collective-permute-start(bf16[400,256]{1,0:T(8,128)(2,1)} %get-tuple-element.13), channel_id=1, source_target_pairs={{0,8},{1,9},{2,10},{3,11},{4,12},{5,13},{6,14},{7,15},{8,0},{9,1},... | collective-permute-start | bytes 614408 | tf_op jit(solution)/shard_map/ppermute | solution.py:114
  20.4 23.1 %collective-permute-start.1 = (bf16[400,256]{1,0:T(8,128)(2,1)}, bf16[400,256]{1,0:T(8,128)(2,1)S(1)}, u32[]{:S(2)}, u32[]{:S(2)}) collective-permute-start(bf16[400,256]{1,0:T(8,128)(2,1)} %get-tuple-element.13), channel_id=1, source_target_pairs={{16,0},{17,1},{18,2},{19,3},{20,4},{21,5},{22,6},{23,7},{24,8},{25... | collective-permute-start | bytes 614408 | tf_op jit(solution)/shard_map/ppermute | solution.py:114
  22.3 27.3 %collective-permute-start = (bf16[400,256]{1,0:T(8,128)(2,1)}, bf16[400,256]{1,0:T(8,128)(2,1)S(1)}, u32[]{:S(2)}, u32[]{:S(2)}) collective-permute-start(bf16[400,256]{1,0:T(8,128)(2,1)} %get-tuple-element.13), channel_id=1, source_target_pairs={{0,16},{1,17},{2,18},{3,19},{4,20},{5,21},{6,22},{7,23},{8,24},{9,... | collective-permute-start | bytes 614408 | tf_op jit(solution)/shard_map/ppermute | solution.py:114
  43.5 10.0 %collective-permute-start.3 = (bf16[400,256]{1,0:T(8,128)(2,1)S(1)}, bf16[400,256]{1,0:T(8,128)(2,1)S(1)}, u32[]{:S(2)}, u32[]{:S(2)}) collective-permute-start(bf16[400,256]{1,0:T(8,128)(2,1)S(1)} %collective-permute-done.1.refs_1_), channel_id=1, source_target_pairs={{16,0},{17,1},{18,2},{19,3},{20,4},{21,5},{22,6},{23,7},{24,8},{25... | collective-permute-start | bytes 614408 | tf_op jit(solution)/shard_map/ppermute | solution.py:114
  49.6 9.8 %collective-permute-start.2 = (bf16[400,256]{1,0:T(8,128)(2,1)S(1)}, bf16[400,256]{1,0:T(8,128)(2,1)S(1)}, u32[]{:S(2)}, u32[]{:S(2)}) collective-permute-start(bf16[400,256]{1,0:T(8,128)(2,1)S(1)} %collective-permute-done.refs_0_), channel_id=1, source_target_pairs={{0,16},{1,17},{2,18},{3,19},{4,20},{5,21},{6,22},{7,23},{8,24},{9,... | collective-permute-start | bytes 614408 | tf_op jit(solution)/shard_map/ppermute | solution.py:114
  59.4 0.9 copy-start.1
  60.3 0.6 copy-start.4
  61.9 35.1 %collective-permute-start.5 = (bf16[928,256]{1,0:T(8,128)(2,1)S(1)}, bf16[928,256]{1,0:T(8,128)(2,1)S(1)}, u32[]{:S(2)}, u32[]{:S(2)}) collective-permute-start(bf16[928,256]{1,0:T(8,128)(2,1)S(1)} %get-tuple-element.16), channel_id=1, source_target_pairs={{0,2},{1,3},{2,4},{3,5},{4,6},{5,7},{6,0},{7,1},{8,10},{9,11},{10,... | collective-permute-start | bytes 1425416 | tf_op jit(solution)/shard_map/ppermute | solution.py:114
  65.0 12.1 %collective-permute-start.9 = (bf16[400,256]{1,0:T(8,128)(2,1)S(1)}, bf16[400,256]{1,0:T(8,128)(2,1)S(1)}, u32[]{:S(2)}, u32[]{:S(2)}) collective-permute-start(bf16[400,256]{1,0:T(8,128)(2,1)S(1)} %collective-permute-done.4.refs_5_), channel_id=1, source_target_pairs={{16,0},{17,1},{18,2},{19,3},{20,4},{21,5},{22,6},{23,7},{24,8},{25... | collective-permute-start | bytes 614408 | tf_op jit(solution)/shard_map/ppermute | solution.py:114
  66.9 14.3 %collective-permute-start.8 = (bf16[400,256]{1,0:T(8,128)(2,1)S(1)}, bf16[400,256]{1,0:T(8,128)(2,1)S(1)}, u32[]{:S(2)}, u32[]{:S(2)}) collective-permute-start(bf16[400,256]{1,0:T(8,128)(2,1)S(1)} %collective-permute-done.4.refs_5_), channel_id=1, source_target_pairs={{0,16},{1,17},{2,18},{3,19},{4,20},{5,21},{6,22},{7,23},{8,24},{9,... | collective-permute-start | bytes 614408 | tf_op jit(solution)/shard_map/ppermute | solution.py:114
  70.3 28.8 %collective-permute-start.6 = (bf16[928,256]{1,0:T(8,128)(2,1)S(1)}, bf16[928,256]{1,0:T(8,128)(2,1)S(1)}, u32[]{:S(2)}, u32[]{:S(2)}) collective-permute-start(bf16[928,256]{1,0:T(8,128)(2,1)S(1)} %get-tuple-element.17), channel_id=1, source_target_pairs={{0,6},{1,7},{2,0},{3,1},{4,2},{5,3},{6,4},{7,5},{8,14},{9,15},{10,... | collective-permute-start | bytes 1425416 | tf_op jit(solution)/shard_map/ppermute | solution.py:114
  73.7 25.4 %collective-permute-start.7 = (bf16[928,256]{1,0:T(8,128)(2,1)S(1)}, bf16[928,256]{1,0:T(8,128)(2,1)S(1)}, u32[]{:S(2)}, u32[]{:S(2)}) collective-permute-start(bf16[928,256]{1,0:T(8,128)(2,1)S(1)} %get-tuple-element.18), channel_id=1, source_target_pairs={{0,4},{1,5},{2,6},{3,7},{4,0},{5,1},{6,2},{7,3},{8,12},{9,13},{10,... | collective-permute-start | bytes 1425416 | tf_op jit(solution)/shard_map/ppermute | solution.py:114
  77.1 6.8 %collective-permute-start.11 = (bf16[400,256]{1,0:T(8,128)(2,1)S(1)}, bf16[400,256]{1,0:T(8,128)(2,1)S(1)}, u32[]{:S(2)}, u32[]{:S(2)}) collective-permute-start(bf16[400,256]{1,0:T(8,128)(2,1)S(1)} %collective-permute-done.9.refs_1_), channel_id=1, source_target_pairs={{16,0},{17,1},{18,2},{19,3},{20,4},{21,5},{22,6},{23,7},{24,8},{25... | collective-permute-start | bytes 614408 | tf_op jit(solution)/shard_map/ppermute | solution.py:114
  81.2 8.8 %collective-permute-start.10 = (bf16[400,256]{1,0:T(8,128)(2,1)S(1)}, bf16[400,256]{1,0:T(8,128)(2,1)S(1)}, u32[]{:S(2)}, u32[]{:S(2)}) collective-permute-start(bf16[400,256]{1,0:T(8,128)(2,1)S(1)} %collective-permute-done.8.refs_0_), channel_id=1, source_target_pairs={{0,16},{1,17},{2,18},{3,19},{4,20},{5,21},{6,22},{7,23},{8,24},{9,... | collective-permute-start | bytes 614408 | tf_op jit(solution)/shard_map/ppermute | solution.py:114
  90.6 18.7 %collective-permute-start.14 = (bf16[800,256]{1,0:T(8,128)(2,1)S(1)}, bf16[800,256]{1,0:T(8,128)(2,1)S(1)}, u32[]{:S(2)}, u32[]{:S(2)}) collective-permute-start(bf16[800,256]{1,0:T(8,128)(2,1)S(1)} %choose.3.refs_0_), channel_id=1, source_target_pairs={{0,4},{1,5},{2,6},{3,7},{4,0},{5,1},{6,2},{7,3},{8,12},{9,13},{10,... | collective-permute-start | bytes 1228808 | tf_op jit(solution)/shard_map/ppermute | solution.py:114
  93.8 16.6 %collective-permute-start.13 = (bf16[800,256]{1,0:T(8,128)(2,1)S(1)}, bf16[800,256]{1,0:T(8,128)(2,1)S(1)}, u32[]{:S(2)}, u32[]{:S(2)}) collective-permute-start(bf16[800,256]{1,0:T(8,128)(2,1)S(1)} %choose.3.refs_0_), channel_id=1, source_target_pairs={{0,6},{1,7},{2,0},{3,1},{4,2},{5,3},{6,4},{7,5},{8,14},{9,15},{10,... | collective-permute-start | bytes 1228808 | tf_op jit(solution)/shard_map/ppermute | solution.py:114
  97.0 15.1 %collective-permute-start.12 = (bf16[800,256]{1,0:T(8,128)(2,1)S(1)}, bf16[800,256]{1,0:T(8,128)(2,1)S(1)}, u32[]{:S(2)}, u32[]{:S(2)}) collective-permute-start(bf16[800,256]{1,0:T(8,128)(2,1)S(1)} %choose.3.refs_0_), channel_id=1, source_target_pairs={{0,2},{1,3},{2,4},{3,5},{4,6},{5,7},{6,0},{7,1},{8,10},{9,11},{10,... | collective-permute-start | bytes 1228808 | tf_op jit(solution)/shard_map/ppermute | solution.py:114
  115.0 7.9 %collective-permute-start.15 = (bf16[1152,512]{1,0:T(8,128)(2,1)S(1)}, bf16[1152,512]{1,0:T(8,128)(2,1)S(1)}, u32[]{:S(2)}, u32[]{:S(2)}) collective-permute-start(bf16[1152,512]{1,0:T(8,128)(2,1)S(1)} %lags.5), channel_id=1, source_target_pairs={{0,1},{1,0},{2,3},{3,2},{4,5},{5,4},{6,7},{7,6},{8,9},{9,8},{10,11... | collective-permute-start | bytes 3538952 | tf_op jit(solution)/shard_map/ppermute | solution.py:114

commit v3 on v2

--- a/solution.py
+++ b/solution.py
@@ -28,6 +28,7 @@
 WHITE = 3 * COLS
 SENT = WHITE + MASK_ROWS
 WIDE = WHITE + 128
+OWN = 4 * CHIP_ROWS
 TURNS = (0, 1, -1, 2)
 TILE = 8 * LPAD
 DEEP = CHIPS * WHITE
@@ -75,7 +76,7 @@
     sine = np.zeros((LPAD, COLS), np.float32)
     cosine[:LAGS] = np.tile(np.cos(phase), (1, 2))
     sine[:LAGS] = np.concatenate([-np.sin(phase), np.sin(phase)], axis=1)
-    return cosine, sine
+    return np.stack([cosine, sine])
 
 
 def routes(target):
@@ -114,22 +115,26 @@
     return lax.ppermute(array, AXES, routes(target))
 
 
+CHIP_GROUPS = [[z * HALF + 2 * i + c for i in range(CHIPS)] for z in range(TM // HALF) for c in range(2)]
+
+
 VMEM = pl.BlockSpec(memory_space=pltpu.VMEM)
 SMEM = pl.BlockSpec(memory_space=pltpu.SMEM)
 ANY = pl.BlockSpec(memory_space=pl.ANY)
 
 
-def store_rows(out_ref, white, z_hi):
-    lanes = pl.ds(pl.multiple_of(z_hi * 128, 128), 128)
-    for g in range(WHITE // COLS):
-        block = white[g * COLS : (g + 1) * COLS, lanes].astype(jnp.float32)
-        out_ref[:, g * COLS : (g + 1) * COLS] = block.T.astype(jnp.bfloat16)
-    mask = white[WHITE:SENT, lanes].astype(jnp.float32)
-    mask = jnp.concatenate([mask, jnp.zeros((128 - MASK_ROWS, 128), jnp.float32)], axis=0)
-    out_ref[:, WHITE:] = mask.T.astype(jnp.bfloat16)
-
-
-def whiten_kernel(place_ref, rec_hbm, mask_hbm, avg_hbm, table_hbm, out_ref, rows_ref, rec, mask_in, avg, table, sems):
+def place():
+    index = lax.axis_index("tm")
+    return index // HALF, index % HALF // 2, index % 2
+
+
+def partner(partners_ref, q):
+    block = lax.axis_index("sta")
+    target = partners_ref[q, block]
+    return block, target, jnp.where(target // 8 == block // 8, 0, 1)
+
+
+def whiten_kernel(rec_hbm, mask_hbm, avg_hbm, table_hbm, out_ref, rec, mask_in, avg, table, sems):
     win_dev = table_hbm.shape[0]
     copies = [pltpu.make_async_copy(mask_hbm, mask_in, sems.at[0]), pltpu.make_async_copy(avg_hbm, avg, sems.at[1])]
     for w in range(win_dev):
@@ -153,19 +158,15 @@
         out_ref[w * COLS + BINS : (w + 1) * COLS] = (imag * scale).astype(jnp.bfloat16)
     empty = jnp.zeros((MASK_ROWS - win_dev, STA), jnp.float32)
     out_ref[WHITE:] = jnp.concatenate([mask, empty], axis=0).astype(jnp.bfloat16)
-    store_rows(rows_ref, out_ref, place_ref[0])
-
-
-def whitened(place, records, validity):
+
+
+def whitened(records, validity):
     rows, win_dev = validity.shape
     return pl.pallas_call(
         whiten_kernel,
-        out_shape=[
-            jax.ShapeDtypeStruct((SENT, rows), jnp.bfloat16),
-            jax.ShapeDtypeStruct((128, WIDE), jnp.bfloat16),
-        ],
-        in_specs=[SMEM, ANY, ANY, ANY, ANY],
-        out_specs=[VMEM, VMEM],
+        out_shape=jax.ShapeDtypeStruct((SENT, rows), jnp.bfloat16),
+        in_specs=[ANY] * 4,
+        out_specs=VMEM,
         scratch_shapes=[
             pltpu.VMEM((win_dev, SPAN, rows), records.dtype),
             pltpu.VMEM((win_dev, rows), jnp.int32),
@@ -175,73 +176,88 @@
         ],
         compiler_params=pltpu.CompilerParams(vmem_limit_bytes=60 * MIB),
         name="whiten",
-    )(place, records.T, validity.T, band_average(), window_tables(win_dev))
-
-
-def choose_kernel(choice_ref, place_ref, *refs):
-    blocks, refs = refs[:4], refs[4:]
-    outs = refs
-    if len(refs) > 1:
-        rows_ref, other_ref, other_rows = refs[0], refs[1], refs[-1]
-        outs = refs[2:-1]
-        store_rows(other_rows, other_ref, place_ref[0])
+    )(records.T, validity.T, band_average(), window_tables(win_dev))
+
+
+def own_kernel(white_hbm, other_ref, out_ref, white_ref, sem):
+    copy = pltpu.make_async_copy(white_hbm, white_ref, sem)
+    copy.start()
+    lanes = pl.ds(pl.multiple_of(place()[0] * 128, 128), 128)
+    for half, ref in ((1, other_ref), (0, white_ref)):
+        if half == 0:
+            copy.wait()
+        blocks = [ref[g * COLS : (g + 1) * COLS, lanes].astype(jnp.float32) for g in range(WHITE // COLS)]
+        mask = ref[WHITE:SENT, lanes].astype(jnp.float32)
+        blocks.append(jnp.concatenate([mask, jnp.zeros((128 - MASK_ROWS, 128), jnp.float32)], axis=0))
+        for g, block in enumerate(blocks):
+            rows = block.T.astype(jnp.bfloat16)
+            at = (half * 2 + g // 2) * CHIP_ROWS
+            for x in range(CHIPS):
+                piece = rows[x * CHIP_ROWS : (x + 1) * CHIP_ROWS]
+                out_ref[x, at : at + CHIP_ROWS, g % 2 * 128 : (g % 2 + 1) * 128] = piece
+
+
+def own_stations(white, other):
+    return pl.pallas_call(
+        own_kernel,
+        out_shape=jax.ShapeDtypeStruct((CHIPS, OWN, STA), jnp.bfloat16),
+        in_specs=[ANY, VMEM],
+        out_specs=VMEM,
+        scratch_shapes=[pltpu.VMEM((SENT, STA), jnp.bfloat16), pltpu.SemaphoreType.DMA],
+        compiler_params=pltpu.CompilerParams(vmem_limit_bytes=4 * MIB),
+        name="own",
+    )(white, other)
+
+
+def choose_kernel(partners_ref, *refs):
+    blocks, out_ref = refs[:-1], refs[-1]
     for q in range(SLOTS):
         rows = slice(q * SENT, (q + 1) * SENT)
-
-        @pl.when(choice_ref[q] == 0)
+        block, target, _ = partner(partners_ref, q)
+        by = jnp.where(target < 0, 0, target - block)
+
+        @pl.when(by == 0)
         def _():
-            for out_ref in outs:
-                out_ref[rows] = jnp.zeros((SENT, STA), jnp.bfloat16)
-
-        for k, ref in enumerate(blocks):
-
-            @pl.when(choice_ref[q] == k + 1)
+            out_ref[rows] = jnp.zeros((SENT, STA), jnp.bfloat16)
+
+        for step, ref in zip((-1, 1, -2, 2), blocks):
+
+            @pl.when(by == step)
             def _():
-                for out_ref in outs:
-                    out_ref[rows] = ref[...]
-
-    if len(refs) > 1:
-        for by, out_ref in zip(TURNS, outs):
-            chip = lax.rem(place_ref[1] + CHIPS + by, CHIPS)
-            stations = pl.ds(pl.multiple_of(chip * CHIP_ROWS, CHIP_ROWS), CHIP_ROWS)
-            at = SLOTS * SENT
-            for source in (rows_ref, other_rows):
-                for lanes in (slice(0, STA), slice(STA, WIDE)):
-                    out_ref[at : at + CHIP_ROWS] = source[stations, lanes]
-                    at += CHIP_ROWS
-
-
-def chosen(choice, place, blocks, own=()):
-    rows = SLOTS * SENT + (4 * CHIP_ROWS if own else 0)
-    count = CHIPS if own else 1
+                out_ref[rows] = ref[...]
+
+
+def chosen(partners, blocks):
     return pl.pallas_call(
         choose_kernel,
-        out_shape=[jax.ShapeDtypeStruct((rows, STA), jnp.bfloat16)] * count,
-        in_specs=[SMEM, SMEM] + [VMEM] * (len(blocks) + len(own)),
-        out_specs=[VMEM] * count,
-        scratch_shapes=[pltpu.VMEM((128, WIDE), jnp.bfloat16)] if own else [],
-        compiler_params=pltpu.CompilerParams(vmem_limit_bytes=6 * MIB),
+        out_shape=jax.ShapeDtypeStruct((SLOTS * SENT, STA), jnp.bfloat16),
+        in_specs=[SMEM] + [VMEM] * len(blocks),
+        out_specs=VMEM,
+        compiler_params=pltpu.CompilerParams(vmem_limit_bytes=4 * MIB),
         name="choose",
-    )(choice, place, *blocks, *own)
-
-
-def turn_kernel(place_ref, *refs):
-    far, (cos_ref, sin_ref, out_ref, mask_ref, held) = refs[:CHIPS], refs[CHIPS:]
-    core = place_ref[2]
-    cosine, sine = cos_ref[...], sin_ref[...]
+    )(partners, *blocks)
+
+
+def turn_kernel(own_ref, lags_hbm, out_ref, mask_ref, held, lag_rows, sem):
+    _, chip, core = place()
+    copy = pltpu.make_async_copy(lags_hbm, lag_rows, sem)
+    copy.start()
     for half in range(2):
-        at = SLOTS * SENT + half * 2 * CHIP_ROWS
-        for d in range(CHIPS):
+        for d, by in enumerate(TURNS):
+            source = lax.rem(chip + CHIPS - by, CHIPS)
             for h, whose in enumerate((1 - core, core)):
                 here = slice(h * ROW_BLOCK, (h + 1) * ROW_BLOCK)
                 for part in range(2):
-                    start = pl.multiple_of(at + part * CHIP_ROWS + whose * ROW_BLOCK, ROW_BLOCK)
-                    rows = far[d][pl.ds(start, ROW_BLOCK)]
+                    start = pl.multiple_of((half * 2 + part) * CHIP_ROWS + whose * ROW_BLOCK, ROW_BLOCK)
+                    rows = own_ref[source, pl.ds(start, ROW_BLOCK)]
                     held[d, here, part * STA : (part + 1) * STA] = rows.astype(jnp.float32)
         mask = held[0, :, WHITE:]
         for d in range(1, CHIPS):
             mask += pltpu.roll(held[d, :, WHITE:], d * MASK_ROWS, 1)
         mask_ref[half] = mask.astype(jnp.bfloat16)
+        if half == 0:
+            copy.wait()
+        cosine, sine = lag_rows[0], lag_rows[1]
 
         def eight(i, carry):
             stations = pl.ds(pl.multiple_of(i * 8, 8), 8)
@@ -259,8 +275,7 @@
         lax.fori_loop(0, CHIP_ROWS // 8, eight, 0)
 
 
-def turned_rows(place, far):
-    cosine, sine = lag_tables()
+def turned_rows(own):
     height = CHIP_ROWS * LPAD
     return pl.pallas_call(
         turn_kernel,
@@ -268,20 +283,24 @@
             jax.ShapeDtypeStruct((2, height, DEEP), jnp.bfloat16),
             jax.ShapeDtypeStruct((2, CHIP_ROWS, 128), jnp.bfloat16),
         ],
-        in_specs=[SMEM] + [VMEM] * (CHIPS + 2),
+        in_specs=[VMEM, ANY],
         out_specs=[VMEM, VMEM],
-        scratch_shapes=[pltpu.VMEM((CHIPS, CHIP_ROWS, WIDE), jnp.float32)],
+        scratch_shapes=[
+            pltpu.VMEM((CHIPS, CHIP_ROWS, WIDE), jnp.float32),
+            pltpu.VMEM((2, LPAD, COLS), jnp.float32),
+            pltpu.SemaphoreType.DMA,
+        ],
         compiler_params=pltpu.CompilerParams(vmem_limit_bytes=18 * MIB),
         cost_estimate=pl.CostEstimate(flops=6 * height * DEEP, bytes_accessed=4 * height * DEEP, transcendentals=0),
         name="turn",
-    )(place, *far, cosine, sine)
-
-
-def lags_kernel(half, first, count, has_acc, choice_ref, turned_ref, valid_ref, *refs):
-    far = refs[:CHIPS]
-    acc_ref = refs[CHIPS] if has_acc else None
+    )(own, lag_tables())
+
+
+def lags_kernel(half, first, count, pieces, has_acc, partners_ref, turned_ref, valid_ref, *refs):
+    far = refs[:pieces]
+    acc_ref = refs[pieces] if has_acc else None
     out_ref = refs[-1]
-    which = [(choice_ref[SLOTS + q] + half) % 2 for q in range(SLOTS)]
+    which = [(partner(partners_ref, q)[2] + half) % 2 for q in range(SLOTS)]
 
     def tile(i, carry):
         source = pl.ds(pl.multiple_of(first * LPAD + i * TILE, TILE), TILE)
@@ -309,10 +328,10 @@
             out_ref[row : row + 1, lanes] = value.astype(out_ref.dtype)
 
 
-def into_lags(choice, own, far, half, first, count, acc=None, dtype=jnp.float32):
-    args = [choice, *own, *far] + ([] if acc is None else [acc])
+def into_lags(partners, own, far, half, first, count, acc=None, dtype=jnp.float32):
+    args = [partners, *own, *far] + ([] if acc is None else [acc])
     return pl.pallas_call(
-        functools.partial(lags_kernel, half, first, count, acc is not None),
+        functools.partial(lags_kernel, half, first, count, len(far), acc is not None),
         out_shape=jax.ShapeDtypeStruct((count * LPAD, SLOTS * STA), dtype),
         in_specs=[SMEM] + [VMEM] * (len(args) - 1),
         out_specs=VMEM,
@@ -352,30 +371,24 @@
 
 
 def body(records, validity, partners):
-    index = lax.axis_index("tm")
-    place = jnp.stack([index // HALF, index % HALF // 2, index % 2])
-    block_id = lax.axis_index("sta")
-    pair = lax.dynamic_index_in_dim(partners, block_id, 0, keepdims=False)
-    by = pair - block_id
-    choice = jnp.where(by == -1, 1, jnp.where(by == 1, 2, jnp.where(by == -2, 3, jnp.where(by == 2, 4, 0))))
-    choice = jnp.where(pair >= 0, choice, 0)
-    choice = jnp.concatenate([choice, (pair // 8 != block_id // 8).astype(jnp.int32)])
+    partners = partners.T
 
     def neighbours(white):
         back, on = send(white, to_block(1)), send(white, to_block(-1))
         return [back, on, send(back, to_block(1)), send(on, to_block(-1))]
 
-    def to_chips(arrays):
-        return [arrays[0]] + [send(array, to_chip(by)) for by, array in zip(TURNS[1:], arrays[1:])]
-
-    white, rows = whitened(place, records, validity)
+    def partner_rows(white):
+        held = chosen(partners, neighbours(white))
+        return [held] + [send(held, to_chip(by)) for by in TURNS[1:]]
+
+    white = whitened(records, validity)
     other = send(white, to_other_half)
-    far = to_chips(chosen(choice, place, neighbours(white), (rows, other)))
-    other_far = to_chips(chosen(choice, place, neighbours(other)) * CHIPS)
-    own = turned_rows(place, far)
-
-    acc = into_lags(choice, own, far, 0, 0, CHIP_ROWS)
-    last = functools.partial(into_lags, choice, own, other_far, 1, acc=acc)
+    far, other_far = partner_rows(white), partner_rows(other)
+    own = own_stations(white, other)
+    own = turned_rows(lax.all_to_all(own, "tm", 0, 0, axis_index_groups=CHIP_GROUPS, tiled=True))
+
+    acc = into_lags(partners, own, far, 0, 0, CHIP_ROWS)
+    last = functools.partial(into_lags, partners, own, other_far, 1, acc=acc)
     theirs = send(last(0, ROW_BLOCK, dtype=jnp.bfloat16), to_core)
     return combined(last(ROW_BLOCK, ROW_BLOCK), theirs)
 

time: 126 us -> 114 us (0.905)
  the two profiles are of different devices: /device:TPU:9 before, /device:TPU:11 now
where the time goes in v3:
time: 114 us; the launch traced here: 113 us
  starting transfers between devices  74.5 us (65%)
  Pallas kernels  23.6 us (21%)
  waiting for transfers between devices  12.4 us (11%)
  local copies, waits for them, and re-layouts  2.48 us (2%)
    ppermute x16, starting transfers between devices, send(): return lax.ppermute(array, AXES, routes(target))  70 us
    ppermute x16, waiting for transfers between devices, send(): return lax.ppermute(array, AXES, routes(target))  12.4 us
    pallas_call x3, Pallas kernels, into_lags(): pl.pallas_call(functools.partial(lags_kernel, half, first, count, len(far...  10.8 us
    pallas_call x1, Pallas kernels, turned_rows(): pl.pallas_call(turn_kernel, out_shape=[jax.ShapeDtypeStruct((2, height, D...  4.69 us
    all_to_all x1, starting transfers between devices, body(): lax.all_to_all(own, 'tm', 0, 0, axis_index_groups=CHIP_GROUPS, tiled=True)  4.54 us
    pallas_call x1, Pallas kernels, whitened(): pl.pallas_call(whiten_kernel, out_shape=jax.ShapeDtypeStruct((SENT, rows)...  3.35 us
    unnamed x8, local copies, waits for them, and re-layouts  2.48 us
    pallas_call x1, Pallas kernels, combined(): pl.pallas_call(combine_kernel, out_shape=jax.ShapeDtypeStruct((stations,...  2.3 us
  transfers between devices with their start and end apart: 17, of which 2 were waited for; matrix products, arithmetic and copies ran while one was open for 0% of the time, Pallas kernels for 13%

profile of v3, /device:TPU:11, one launch (start us, length us, event | category | flops | bytes accessed | tf_op | source)
XLA Modules:
  0.0 113.3 jit_solution(13711120240397577569)
XLA Ops:
  0.0 3.3 %whiten.1.white_hbm = bf16[400,256]{1,0:T(8,128)(2,1)} custom-call(bf16[1800,256]{1,0:T(8,128)(2,1)} %bitcast.9, s32[3,256]{1,0:T(4,128)} %bitcast.10, f32[64,64]{1,0:T(8,128)} %constant.6.clone.avg_hbm, bf16[3,128,616]{2,1,0:T(8,128)(2,1)} %constant.7.clone.table_hbm), custom_call_target="tpu_custom_call" | custom-call | tf_op jit(solution)/shard_map/whiten/pallas_call | solution.py:165
  3.4 11.0 %collective-permute-start.9 = (bf16[400,256]{1,0:T(8,128)(2,1)}, bf16[400,256]{1,0:T(8,128)(2,1)S(1)}, u32[]{:S(2)}, u32[]{:S(2)}) collective-permute-start(bf16[400,256]{1,0:T(8,128)(2,1)} %whiten.1.white_hbm), channel_id=1, source_target_pairs={{16,0},{17,1},{18,2},{19,3},{20,4},{21,5},{22,6},{23,7},{24,8},{25... | collective-permute-start | bytes 614408 | tf_op jit(solution)/shard_map/ppermute | solution.py:115
  14.4 1.9 %collective-permute-start.8 = (bf16[400,256]{1,0:T(8,128)(2,1)}, bf16[400,256]{1,0:T(8,128)(2,1)S(1)}, u32[]{:S(2)}, u32[]{:S(2)}) collective-permute-start(bf16[400,256]{1,0:T(8,128)(2,1)} %whiten.1.white_hbm), channel_id=1, source_target_pairs={{0,16},{1,17},{2,18},{3,19},{4,20},{5,21},{6,22},{7,23},{8,24},{9,... | collective-permute-start | bytes 614408 | tf_op jit(solution)/shard_map/ppermute | solution.py:115
  16.3 7.8 %collective-permute-start = (bf16[400,256]{1,0:T(8,128)(2,1)}, bf16[400,256]{1,0:T(8,128)(2,1)S(1)}, u32[]{:S(2)}, u32[]{:S(2)}) collective-permute-start(bf16[400,256]{1,0:T(8,128)(2,1)} %whiten.1.white_hbm), channel_id=1, source_target_pairs={{0,8},{1,9},{2,10},{3,11},{4,12},{5,13},{6,14},{7,15},{8,0},{9,1},... | collective-permute-start | bytes 614408 | tf_op jit(solution)/shard_map/ppermute | solution.py:115
  24.1 0.0 collective-permute-done.9.refs_1_
  24.1 4.0 %collective-permute-start.11 = (bf16[400,256]{1,0:T(8,128)(2,1)S(1)}, bf16[400,256]{1,0:T(8,128)(2,1)S(1)}, u32[]{:S(2)}, u32[]{:S(2)}) collective-permute-start(bf16[400,256]{1,0:T(8,128)(2,1)S(1)} %collective-permute-done.9.refs_1_), channel_id=1, source_target_pairs={{16,0},{17,1},{18,2},{19,3},{20,4},{21,5},{22,6},{23,7},{24,8},{25... | collective-permute-start | bytes 614408 | tf_op jit(solution)/shard_map/ppermute | solution.py:115
  28.2 0.0 collective-permute-done.8.refs_0_
  28.2 1.9 %collective-permute-start.10 = (bf16[400,256]{1,0:T(8,128)(2,1)S(1)}, bf16[400,256]{1,0:T(8,128)(2,1)S(1)}, u32[]{:S(2)}, u32[]{:S(2)}) collective-permute-start(bf16[400,256]{1,0:T(8,128)(2,1)S(1)} %collective-permute-done.8.refs_0_), channel_id=1, source_target_pairs={{0,16},{1,17},{2,18},{3,19},{4,20},{5,21},{6,22},{7,23},{8,24},{9,... | collective-permute-start | bytes 614408 | tf_op jit(solution)/shard_map/ppermute | solution.py:115
  30.1 11.1 %collective-permute-done.other_ref = bf16[400,256]{1,0:T(8,128)(2,1)S(1)} collective-permute-done((bf16[400,256]{1,0:T(8,128)(2,1)}, bf16[400,256]{1,0:T(8,128)(2,1)S(1)}, u32[]{:S(2)}, u32[]{:S(2)}) %collective-permute-start) | collective-permute-done | bytes 204832 | tf_op jit(solution)/shard_map/ppermute | solution.py:115
  41.2 6.5 %collective-permute-start.2 = (bf16[400,256]{1,0:T(8,128)(2,1)S(1)}, bf16[400,256]{1,0:T(8,128)(2,1)S(1)}, u32[]{:S(2)}, u32[]{:S(2)}) collective-permute-start(bf16[400,256]{1,0:T(8,128)(2,1)S(1)} %collective-permute-done.other_ref), channel_id=1, source_target_pairs={{16,0},{17,1},{18,2},{19,3},{20,4},{21,5},{22,6},{23,7},{24,8},{25... | collective-permute-start | bytes 614408 | tf_op jit(solution)/shard_map/ppermute | solution.py:115
  47.7 1.9 %collective-permute-start.1 = (bf16[400,256]{1,0:T(8,128)(2,1)S(1)}, bf16[400,256]{1,0:T(8,128)(2,1)S(1)}, u32[]{:S(2)}, u32[]{:S(2)}) collective-permute-start(bf16[400,256]{1,0:T(8,128)(2,1)S(1)} %collective-permute-done.other_ref), channel_id=1, source_target_pairs={{0,16},{1,17},{2,18},{3,19},{4,20},{5,21},{6,22},{7,23},{8,24},{9,... | collective-permute-start | bytes 614408 | tf_op jit(solution)/shard_map/ppermute | solution.py:115
  49.6 0.0 collective-permute-done.11.refs_3_
  49.6 0.0 collective-permute-done.10.refs_2_
  49.7 0.0 copy-start.2
  49.7 0.7 copy-done.2
  50.3 0.6 choose.3.refs_0_
  51.0 3.8 %collective-permute-start.14 = (bf16[800,256]{1,0:T(8,128)(2,1)S(1)}, bf16[800,256]{1,0:T(8,128)(2,1)S(1)}, u32[]{:S(2)}, u32[]{:S(2)}) collective-permute-start(bf16[800,256]{1,0:T(8,128)(2,1)S(1)} %choose.3.refs_0_), channel_id=1, source_target_pairs={{0,4},{1,5},{2,6},{3,7},{4,0},{5,1},{6,2},{7,3},{8,12},{9,13},{10,... | collective-permute-start | bytes 1228808 | tf_op jit(solution)/shard_map/ppermute | solution.py:115
  54.7 3.1 %collective-permute-start.13 = (bf16[800,256]{1,0:T(8,128)(2,1)S(1)}, bf16[800,256]{1,0:T(8,128)(2,1)S(1)}, u32[]{:S(2)}, u32[]{:S(2)}) collective-permute-start(bf16[800,256]{1,0:T(8,128)(2,1)S(1)} %choose.3.refs_0_), channel_id=1, source_target_pairs={{0,6},{1,7},{2,0},{3,1},{4,2},{5,3},{6,4},{7,5},{8,14},{9,15},{10,... | collective-permute-start | bytes 1228808 | tf_op jit(solution)/shard_map/ppermute | solution.py:115
  57.8 2.2 %collective-permute-start.12 = (bf16[800,256]{1,0:T(8,128)(2,1)S(1)}, bf16[800,256]{1,0:T(8,128)(2,1)S(1)}, u32[]{:S(2)}, u32[]{:S(2)}) collective-permute-start(bf16[800,256]{1,0:T(8,128)(2,1)S(1)} %choose.3.refs_0_), channel_id=1, source_target_pairs={{0,2},{1,3},{2,4},{3,5},{4,6},{5,7},{6,0},{7,1},{8,10},{9,11},{10,... | collective-permute-start | bytes 1228808 | tf_op jit(solution)/shard_map/ppermute | solution.py:115
  60.0 0.0 collective-permute-done.2.refs_1_
  60.0 5.5 %collective-permute-start.4 = (bf16[400,256]{1,0:T(8,128)(2,1)S(1)}, bf16[400,256]{1,0:T(8,128)(2,1)S(1)}, u32[]{:S(2)}, u32[]{:S(2)}) collective-permute-start(bf16[400,256]{1,0:T(8,128)(2,1)S(1)} %collective-permute-done.2.refs_1_), channel_id=1, source_target_pairs={{16,0},{17,1},{18,2},{19,3},{20,4},{21,5},{22,6},{23,7},{24,8},{25... | collective-permute-start | bytes 614408 | tf_op jit(solution)/shard_map/ppermute | solution.py:115
  65.5 0.0 collective-permute-done.1.refs_0_
  65.5 1.9 %collective-permute-start.3 = (bf16[400,256]{1,0:T(8,128)(2,1)S(1)}, bf16[400,256]{1,0:T(8,128)(2,1)S(1)}, u32[]{:S(2)}, u32[]{:S(2)}) collective-permute-start(bf16[400,256]{1,0:T(8,128)(2,1)S(1)} %collective-permute-done.1.refs_0_), channel_id=1, source_target_pairs={{0,16},{1,17},{2,18},{3,19},{4,20},{5,21},{6,22},{7,23},{8,24},{9,... | collective-permute-start | bytes 614408 | tf_op jit(solution)/shard_map/ppermute | solution.py:115
  67.5 0.0 copy-start
  67.5 0.9 copy-done
  68.4 1.3 %own.1 = bf16[4,128,256]{2,1,0:T(8,128)(2,1)} custom-call(bf16[400,256]{1,0:T(8,128)(2,1)S(1)} %copy-done, bf16[400,256]{1,0:T(8,128)(2,1)S(1)} %collective-permute-done.other_ref), custom_call_target="tpu_custom_call" | custom-call | tf_op jit(solution)/shard_map/own/pallas_call | solution.py:201
  69.7 4.5 %all-to-all-start = ((bf16[4,128,256]{2,1,0:T(8,128)(2,1)}), bf16[4,128,256]{2,1,0:T(8,128)(2,1)S(1)}, u32[]{:S(2)}, u32[]{:S(2)}) async-start(bf16[4,128,256]{2,1,0:T(8,128)(2,1)} %own.1), calls=%async_computation | async-start | bytes 524288 | tf_op jit(solution)/shard_map/all_to_all | solution.py:388
  74.2 0.0 collective-permute-done.4.refs_3_
  74.2 0.0 collective-permute-done.3.refs_2_
  74.2 0.6 choose.2.refs_0_
  74.9 4.2 %collective-permute-start.7 = (bf16[800,256]{1,0:T(8,128)(2,1)S(1)}, bf16[800,256]{1,0:T(8,128)(2,1)S(1)}, u32[]{:S(2)}, u32[]{:S(2)}) collective-permute-start(bf16[800,256]{1,0:T(8,128)(2,1)S(1)} %choose.2.refs_0_), channel_id=1, source_target_pairs={{0,4},{1,5},{2,6},{3,7},{4,0},{5,1},{6,2},{7,3},{8,12},{9,13},{10,... | collective-permute-start | bytes 1228808 | tf_op jit(solution)/shard_map/ppermute | solution.py:115
  79.0 2.6 %collective-permute-start.6 = (bf16[800,256]{1,0:T(8,128)(2,1)S(1)}, bf16[800,256]{1,0:T(8,128)(2,1)S(1)}, u32[]{:S(2)}, u32[]{:S(2)}) collective-permute-start(bf16[800,256]{1,0:T(8,128)(2,1)S(1)} %choose.2.refs_0_), channel_id=1, source_target_pairs={{0,6},{1,7},{2,0},{3,1},{4,2},{5,3},{6,4},{7,5},{8,14},{9,15},{10,... | collective-permute-start | bytes 1228808 | tf_op jit(solution)/shard_map/ppermute | solution.py:115
  81.7 0.0 collective-permute-done.14.refs_3_
  81.7 2.7 %collective-permute-start.5 = (bf16[800,256]{1,0:T(8,128)(2,1)S(1)}, bf16[800,256]{1,0:T(8,128)(2,1)S(1)}, u32[]{:S(2)}, u32[]{:S(2)}) collective-permute-start(bf16[800,256]{1,0:T(8,128)(2,1)S(1)} %choose.2.refs_0_), channel_id=1, source_target_pairs={{0,2},{1,3},{2,4},{3,5},{4,6},{5,7},{6,0},{7,1},{8,10},{9,11},{10,... | collective-permute-start | bytes 1228808 | tf_op jit(solution)/shard_map/ppermute | solution.py:115
  84.4 0.0 all-to-all-done.own_ref
  84.4 0.0 copy-start.1
  84.4 0.9 copy-done.1
  85.3 4.7 %turn.1 = (bf16[2,2304,1536]{2,1,0:T(8,128)(2,1)S(1)}, bf16[2,32,128]{2,1,0:T(8,128)(2,1)S(1)}) custom-call(bf16[4,128,256]{2,1,0:T(8,128)(2,1)S(1)} %all-to-all-done.own_ref, f32[2,72,128]{2,1,0:T(8,128)S(1)} %copy-done.1), custom_call_target="tpu_custom_call" | custom-call | flops 21233664 | bytes 14155776 | tf_op jit(solution)/shard_map/turn/pallas_call | solution.py:280
  90.0 0.0 collective-permute-done.13.refs_2_
  90.0 0.0 collective-permute-done.12.refs_1_
  90.0 5.0 %lags.3.refs_4_ = f32[2304,512]{1,0:T(8,128)S(1)} custom-call(s32[2,32]{1,0:T(2,128)S(1)} %bitcast.6, bf16[2,2304,1536]{2,1,0:T(8,128)(2,1)S(1)} %get-tuple-element.7.turned_ref, bf16[2,32,128]{2,1,0:T(8,128)(2,1)S(1)} %get-tuple-element.8.valid_ref, bf16[800,256]{1,0:T(8,128)(2,1)S(1)} %choose.3.refs_0_, ...), custom_call_target="tpu_custom_call" | custom-call | flops 3623878656 | bytes 4718592 | tf_op jit(solution)/shard_map/lags/pallas_call | solution.py:333
  95.0 0.0 collective-permute-done.7.refs_3_
  95.0 1.3 %collective-permute-done.6.refs_2_ = bf16[800,256]{1,0:T(8,128)(2,1)S(1)} collective-permute-done((bf16[800,256]{1,0:T(8,128)(2,1)S(1)}, bf16[800,256]{1,0:T(8,128)(2,1)S(1)}, u32[]{:S(2)}, u32[]{:S(2)}) %collective-permute-start.6) | collective-permute-done | bytes 409632 | tf_op jit(solution)/shard_map/ppermute | solution.py:115
  96.3 0.0 collective-permute-done.5.refs_1_
  96.3 2.9 %lags.5 = bf16[1152,512]{1,0:T(8,128)(2,1)S(1)} custom-call(s32[2,32]{1,0:T(2,128)S(1)} %bitcast.7, bf16[2,2304,1536]{2,1,0:T(8,128)(2,1)S(1)} %get-tuple-element.7.turned_ref, bf16[2,32,128]{2,1,0:T(8,128)(2,1)S(1)} %get-tuple-element.8.valid_ref, bf16[800,256]{1,0:T(8,128)(2,1)S(1)} %choose.2.refs_0_, bf16[800,256]{1,0:T(8,128)(2,1)S(1)} %collective-permute-done.5.refs_1_, ...), custom_call_target="tpu_custom_call" | custom-call | flops 1811939328 | bytes 2359296 | tf_op jit(solution)/shard_map/lags/pallas_call | solution.py:333
  99.1 9.0 %collective-permute-start.15 = (bf16[1152,512]{1,0:T(8,128)(2,1)S(1)}, bf16[1152,512]{1,0:T(8,128)(2,1)S(1)}, u32[]{:S(2)}, u32[]{:S(2)}) collective-permute-start(bf16[1152,512]{1,0:T(8,128)(2,1)S(1)} %lags.5), channel_id=1, source_target_pairs={{0,1},{1,0},{2,3},{3,2},{4,5},{5,4},{6,7},{7,6},{8,9},{9,8},{10,11... | collective-permute-start | bytes 3538952 | tf_op jit(solution)/shard_map/ppermute | solution.py:115
  108.1 2.9 %lags.4.mine_ref = f32[1152,512]{1,0:T(8,128)S(1)} custom-call(s32[2,32]{1,0:T(2,128)S(1)} %bitcast.8, bf16[2,2304,1536]{2,1,0:T(8,128)(2,1)S(1)} %get-tuple-element.7.turned_ref, bf16[2,32,128]{2,1,0:T(8,128)(2,1)S(1)} %get-tuple-element.8.valid_ref, bf16[800,256]{1,0:T(8,128)(2,1)S(1)} %choose.2.refs_0_, ...), custom_call_target="tpu_custom_call" | custom-call | flops 1811939328 | bytes 2359296 | tf_op jit(solution)/shard_map/lags/pallas_call | solution.py:333
  111.0 2.3 %combine.1 = f32[16,65,2,256]{3,2,1,0:T(2,128)} custom-call(f32[1152,512]{1,0:T(8,128)S(1)} %lags.4.mine_ref, bf16[1152,512]{1,0:T(8,128)(2,1)S(1)} %collective-permute-done.15.theirs_ref), custom_call_target="tpu_custom_call" | custom-call | tf_op jit(solution)/shard_map/combine/pallas_call | solution.py:361
  (3 shorter events, 0.0 us)
Async XLA Ops:
  0.0 74.2 %copy-start.3 = (s32[32,2]{0,1:T(2,128)S(1)}, s32[32,2]{0,1:T(2,128)}, u32[]{:S(2)}) copy-start(s32[32,2]{0,1:T(2,128)} %param.8) | copy-start | bytes 772
  3.4 20.7 %collective-permute-start.9 = (bf16[400,256]{1,0:T(8,128)(2,1)}, bf16[400,256]{1,0:T(8,128)(2,1)S(1)}, u32[]{:S(2)}, u32[]{:S(2)}) collective-permute-start(bf16[400,256]{1,0:T(8,128)(2,1)} %whiten.1.white_hbm), channel_id=1, source_target_pairs={{16,0},{17,1},{18,2},{19,3},{20,4},{21,5},{22,6},{23,7},{24,8},{25... | collective-permute-start | bytes 614408 | tf_op jit(solution)/shard_map/ppermute | solution.py:115
  14.4 13.8 %collective-permute-start.8 = (bf16[400,256]{1,0:T(8,128)(2,1)}, bf16[400,256]{1,0:T(8,128)(2,1)S(1)}, u32[]{:S(2)}, u32[]{:S(2)}) collective-permute-start(bf16[400,256]{1,0:T(8,128)(2,1)} %whiten.1.white_hbm), channel_id=1, source_target_pairs={{0,16},{1,17},{2,18},{3,19},{4,20},{5,21},{6,22},{7,23},{8,24},{9,... | collective-permute-start | bytes 614408 | tf_op jit(solution)/shard_map/ppermute | solution.py:115
  16.3 24.9 %collective-permute-start = (bf16[400,256]{1,0:T(8,128)(2,1)}, bf16[400,256]{1,0:T(8,128)(2,1)S(1)}, u32[]{:S(2)}, u32[]{:S(2)}) collective-permute-start(bf16[400,256]{1,0:T(8,128)(2,1)} %whiten.1.white_hbm), channel_id=1, source_target_pairs={{0,8},{1,9},{2,10},{3,11},{4,12},{5,13},{6,14},{7,15},{8,0},{9,1},... | collective-permute-start | bytes 614408 | tf_op jit(solution)/shard_map/ppermute | solution.py:115
  24.1 25.5 %collective-permute-start.11 = (bf16[400,256]{1,0:T(8,128)(2,1)S(1)}, bf16[400,256]{1,0:T(8,128)(2,1)S(1)}, u32[]{:S(2)}, u32[]{:S(2)}) collective-permute-start(bf16[400,256]{1,0:T(8,128)(2,1)S(1)} %collective-permute-done.9.refs_1_), channel_id=1, source_target_pairs={{16,0},{17,1},{18,2},{19,3},{20,4},{21,5},{22,6},{23,7},{24,8},{25... | collective-permute-start | bytes 614408 | tf_op jit(solution)/shard_map/ppermute | solution.py:115
  28.2 21.5 %collective-permute-start.10 = (bf16[400,256]{1,0:T(8,128)(2,1)S(1)}, bf16[400,256]{1,0:T(8,128)(2,1)S(1)}, u32[]{:S(2)}, u32[]{:S(2)}) collective-permute-start(bf16[400,256]{1,0:T(8,128)(2,1)S(1)} %collective-permute-done.8.refs_0_), channel_id=1, source_target_pairs={{0,16},{1,17},{2,18},{3,19},{4,20},{5,21},{6,22},{7,23},{8,24},{9,... | collective-permute-start | bytes 614408 | tf_op jit(solution)/shard_map/ppermute | solution.py:115
  41.2 18.9 %collective-permute-start.2 = (bf16[400,256]{1,0:T(8,128)(2,1)S(1)}, bf16[400,256]{1,0:T(8,128)(2,1)S(1)}, u32[]{:S(2)}, u32[]{:S(2)}) collective-permute-start(bf16[400,256]{1,0:T(8,128)(2,1)S(1)} %collective-permute-done.other_ref), channel_id=1, source_target_pairs={{16,0},{17,1},{18,2},{19,3},{20,4},{21,5},{22,6},{23,7},{24,8},{25... | collective-permute-start | bytes 614408 | tf_op jit(solution)/shard_map/ppermute | solution.py:115
  47.7 17.8 %collective-permute-start.1 = (bf16[400,256]{1,0:T(8,128)(2,1)S(1)}, bf16[400,256]{1,0:T(8,128)(2,1)S(1)}, u32[]{:S(2)}, u32[]{:S(2)}) collective-permute-start(bf16[400,256]{1,0:T(8,128)(2,1)S(1)} %collective-permute-done.other_ref), channel_id=1, source_target_pairs={{0,16},{1,17},{2,18},{3,19},{4,20},{5,21},{6,22},{7,23},{8,24},{9,... | collective-permute-start | bytes 614408 | tf_op jit(solution)/shard_map/ppermute | solution.py:115
  49.7 0.7 copy-start.2
  51.0 30.7 %collective-permute-start.14 = (bf16[800,256]{1,0:T(8,128)(2,1)S(1)}, bf16[800,256]{1,0:T(8,128)(2,1)S(1)}, u32[]{:S(2)}, u32[]{:S(2)}) collective-permute-start(bf16[800,256]{1,0:T(8,128)(2,1)S(1)} %choose.3.refs_0_), channel_id=1, source_target_pairs={{0,4},{1,5},{2,6},{3,7},{4,0},{5,1},{6,2},{7,3},{8,12},{9,13},{10,... | collective-permute-start | bytes 1228808 | tf_op jit(solution)/shard_map/ppermute | solution.py:115
  54.7 35.2 %collective-permute-start.13 = (bf16[800,256]{1,0:T(8,128)(2,1)S(1)}, bf16[800,256]{1,0:T(8,128)(2,1)S(1)}, u32[]{:S(2)}, u32[]{:S(2)}) collective-permute-start(bf16[800,256]{1,0:T(8,128)(2,1)S(1)} %choose.3.refs_0_), channel_id=1, source_target_pairs={{0,6},{1,7},{2,0},{3,1},{4,2},{5,3},{6,4},{7,5},{8,14},{9,15},{10,... | collective-permute-start | bytes 1228808 | tf_op jit(solution)/shard_map/ppermute | solution.py:115
  57.8 32.2 %collective-permute-start.12 = (bf16[800,256]{1,0:T(8,128)(2,1)S(1)}, bf16[800,256]{1,0:T(8,128)(2,1)S(1)}, u32[]{:S(2)}, u32[]{:S(2)}) collective-permute-start(bf16[800,256]{1,0:T(8,128)(2,1)S(1)} %choose.3.refs_0_), channel_id=1, source_target_pairs={{0,2},{1,3},{2,4},{3,5},{4,6},{5,7},{6,0},{7,1},{8,10},{9,11},{10,... | collective-permute-start | bytes 1228808 | tf_op jit(solution)/shard_map/ppermute | solution.py:115
  60.0 14.2 %collective-permute-start.4 = (bf16[400,256]{1,0:T(8,128)(2,1)S(1)}, bf16[400,256]{1,0:T(8,128)(2,1)S(1)}, u32[]{:S(2)}, u32[]{:S(2)}) collective-permute-start(bf16[400,256]{1,0:T(8,128)(2,1)S(1)} %collective-permute-done.2.refs_1_), channel_id=1, source_target_pairs={{16,0},{17,1},{18,2},{19,3},{20,4},{21,5},{22,6},{23,7},{24,8},{25... | collective-permute-start | bytes 614408 | tf_op jit(solution)/shard_map/ppermute | solution.py:115
  65.5 8.7 %collective-permute-start.3 = (bf16[400,256]{1,0:T(8,128)(2,1)S(1)}, bf16[400,256]{1,0:T(8,128)(2,1)S(1)}, u32[]{:S(2)}, u32[]{:S(2)}) collective-permute-start(bf16[400,256]{1,0:T(8,128)(2,1)S(1)} %collective-permute-done.1.refs_0_), channel_id=1, source_target_pairs={{0,16},{1,17},{2,18},{3,19},{4,20},{5,21},{6,22},{7,23},{8,24},{9,... | collective-permute-start | bytes 614408 | tf_op jit(solution)/shard_map/ppermute | solution.py:115
  67.5 0.9 copy-start
  69.7 14.7 %all-to-all-start = ((bf16[4,128,256]{2,1,0:T(8,128)(2,1)}), bf16[4,128,256]{2,1,0:T(8,128)(2,1)S(1)}, u32[]{:S(2)}, u32[]{:S(2)}) async-start(bf16[4,128,256]{2,1,0:T(8,128)(2,1)} %own.1), calls=%async_computation | async-start | bytes 524288 | tf_op jit(solution)/shard_map/all_to_all | solution.py:388
  74.9 20.1 %collective-permute-start.7 = (bf16[800,256]{1,0:T(8,128)(2,1)S(1)}, bf16[800,256]{1,0:T(8,128)(2,1)S(1)}, u32[]{:S(2)}, u32[]{:S(2)}) collective-permute-start(bf16[800,256]{1,0:T(8,128)(2,1)S(1)} %choose.2.refs_0_), channel_id=1, source_target_pairs={{0,4},{1,5},{2,6},{3,7},{4,0},{5,1},{6,2},{7,3},{8,12},{9,13},{10,... | collective-permute-start | bytes 1228808 | tf_op jit(solution)/shard_map/ppermute | solution.py:115
  79.0 17.2 %collective-permute-start.6 = (bf16[800,256]{1,0:T(8,128)(2,1)S(1)}, bf16[800,256]{1,0:T(8,128)(2,1)S(1)}, u32[]{:S(2)}, u32[]{:S(2)}) collective-permute-start(bf16[800,256]{1,0:T(8,128)(2,1)S(1)} %choose.2.refs_0_), channel_id=1, source_target_pairs={{0,6},{1,7},{2,0},{3,1},{4,2},{5,3},{6,4},{7,5},{8,14},{9,15},{10,... | collective-permute-start | bytes 1228808 | tf_op jit(solution)/shard_map/ppermute | solution.py:115
  81.7 14.6 %collective-permute-start.5 = (bf16[800,256]{1,0:T(8,128)(2,1)S(1)}, bf16[800,256]{1,0:T(8,128)(2,1)S(1)}, u32[]{:S(2)}, u32[]{:S(2)}) collective-permute-start(bf16[800,256]{1,0:T(8,128)(2,1)S(1)} %choose.2.refs_0_), channel_id=1, source_target_pairs={{0,2},{1,3},{2,4},{3,5},{4,6},{5,7},{6,0},{7,1},{8,10},{9,11},{10,... | collective-permute-start | bytes 1228808 | tf_op jit(solution)/shard_map/ppermute | solution.py:115
  84.4 0.9 copy-start.1
  99.1 11.9 %collective-permute-start.15 = (bf16[1152,512]{1,0:T(8,128)(2,1)S(1)}, bf16[1152,512]{1,0:T(8,128)(2,1)S(1)}, u32[]{:S(2)}, u32[]{:S(2)}) collective-permute-start(bf16[1152,512]{1,0:T(8,128)(2,1)S(1)} %lags.5), channel_id=1, source_target_pairs={{0,1},{1,0},{2,3},{3,2},{4,5},{5,4},{6,7},{7,6},{8,9},{9,8},{10,11... | collective-permute-start | bytes 3538952 | tf_op jit(solution)/shard_map/ppermute | solution.py:115

commit v4 on v3

--- a/solution.py
+++ b/solution.py
@@ -30,7 +30,7 @@
 WIDE = WHITE + 128
 OWN = 4 * CHIP_ROWS
 TURNS = (0, 1, -1, 2)
-TILE = 8 * LPAD
+TILE = 16 * LPAD
 DEEP = CHIPS * WHITE
 SPAN = 616
 AXES = ("sta", "tm")
@@ -66,17 +66,6 @@
     bins = np.arange(BINS)
     nearby = (np.abs(bins[:, None] - bins[None, :]) <= 2).astype(np.float32)
     return np.ascontiguousarray((nearby / nearby.sum(axis=0, keepdims=True)).T)
-
-
-def lag_tables():
-    lags = np.arange(LAGS) - LAG
-    harmonic = np.arange(1, BINS + 1)
-    phase = np.mod(lags[:, None] * harmonic[None, :], WIN) * (2.0 * math.pi / WIN)
-    cosine = np.zeros((LPAD, COLS), np.float32)
-    sine = np.zeros((LPAD, COLS), np.float32)
-    cosine[:LAGS] = np.tile(np.cos(phase), (1, 2))
-    sine[:LAGS] = np.concatenate([-np.sin(phase), np.sin(phase)], axis=1)
-    return np.stack([cosine, sine])
 
 
 def routes(target):
@@ -179,34 +168,33 @@
     )(records.T, validity.T, band_average(), window_tables(win_dev))
 
 
-def own_kernel(white_hbm, other_ref, out_ref, white_ref, sem):
-    copy = pltpu.make_async_copy(white_hbm, white_ref, sem)
-    copy.start()
+def rows_kernel(white_ref, out_ref, half=0):
     lanes = pl.ds(pl.multiple_of(place()[0] * 128, 128), 128)
-    for half, ref in ((1, other_ref), (0, white_ref)):
-        if half == 0:
-            copy.wait()
-        blocks = [ref[g * COLS : (g + 1) * COLS, lanes].astype(jnp.float32) for g in range(WHITE // COLS)]
-        mask = ref[WHITE:SENT, lanes].astype(jnp.float32)
-        blocks.append(jnp.concatenate([mask, jnp.zeros((128 - MASK_ROWS, 128), jnp.float32)], axis=0))
-        for g, block in enumerate(blocks):
-            rows = block.T.astype(jnp.bfloat16)
-            at = (half * 2 + g // 2) * CHIP_ROWS
-            for x in range(CHIPS):
-                piece = rows[x * CHIP_ROWS : (x + 1) * CHIP_ROWS]
-                out_ref[x, at : at + CHIP_ROWS, g % 2 * 128 : (g % 2 + 1) * 128] = piece
-
-
-def own_stations(white, other):
+    blocks = [white_ref[g * COLS : (g + 1) * COLS, lanes].astype(jnp.float32) for g in range(WHITE // COLS)]
+    mask = white_ref[WHITE:SENT, lanes].astype(jnp.float32)
+    blocks.append(jnp.concatenate([mask, jnp.zeros((128 - MASK_ROWS, 128), jnp.float32)], axis=0))
+    for g, block in enumerate(blocks):
+        rows = block.T.astype(jnp.bfloat16)
+        at = (half * 2 + g // 2) * CHIP_ROWS
+        for x in range(CHIPS):
+            piece = rows[x * CHIP_ROWS : (x + 1) * CHIP_ROWS]
+            out_ref[x, at : at + CHIP_ROWS, g % 2 * 128 : (g % 2 + 1) * 128] = piece
+
+
+def own_kernel(first_ref, other_ref, out_ref):
+    out_ref[:, : OWN // 2] = first_ref[...]
+    rows_kernel(other_ref, out_ref, 1)
+
+
+def by_rows(kernel, height, *args):
     return pl.pallas_call(
-        own_kernel,
-        out_shape=jax.ShapeDtypeStruct((CHIPS, OWN, STA), jnp.bfloat16),
-        in_specs=[ANY, VMEM],
+        kernel,
+        out_shape=jax.ShapeDtypeStruct((CHIPS, height, STA), jnp.bfloat16),
+        in_specs=[VMEM] * len(args),
         out_specs=VMEM,
-        scratch_shapes=[pltpu.VMEM((SENT, STA), jnp.bfloat16), pltpu.SemaphoreType.DMA],
         compiler_params=pltpu.CompilerParams(vmem_limit_bytes=4 * MIB),
-        name="own",
-    )(white, other)
+        name="rows",
+    )(*args)
 
 
 def choose_kernel(partners_ref, *refs):
@@ -238,10 +226,20 @@
     )(partners, *blocks)
 
 
-def turn_kernel(own_ref, lags_hbm, out_ref, mask_ref, held, lag_rows, sem):
+def lag_tables():
+    lag = lax.broadcasted_iota(jnp.int32, (LPAD, COLS), 0) - LAG
+    column = lax.broadcasted_iota(jnp.int32, (LPAD, COLS), 1)
+    harmonic = jnp.where(column < BINS, column, column - BINS) + 1
+    turns = (lag * harmonic).astype(jnp.float32) * (1.0 / WIN)
+    phase = (turns - jnp.round(turns)) * (2.0 * math.pi)
+    kept = lag <= LAG
+    sine = jnp.where(column < BINS, -jnp.sin(phase), jnp.sin(phase))
+    return jnp.where(kept, jnp.cos(phase), 0.0), jnp.where(kept, sine, 0.0)
+
+
+def turn_kernel(own_ref, out_ref, mask_ref, held):
     _, chip, core = place()
-    copy = pltpu.make_async_copy(lags_hbm, lag_rows, sem)
-    copy.start()
+    cosine, sine = lag_tables()
     for half in range(2):
         for d, by in enumerate(TURNS):
             source = lax.rem(chip + CHIPS - by, CHIPS)
@@ -255,9 +253,6 @@
         for d in range(1, CHIPS):
             mask += pltpu.roll(held[d, :, WHITE:], d * MASK_ROWS, 1)
         mask_ref[half] = mask.astype(jnp.bfloat16)
-        if half == 0:
-            copy.wait()
-        cosine, sine = lag_rows[0], lag_rows[1]
 
         def eight(i, carry):
             stations = pl.ds(pl.multiple_of(i * 8, 8), 8)
@@ -268,7 +263,7 @@
                     lanes = slice(d * WHITE + g * COLS, d * WHITE + (g + 1) * COLS)
                     for k in range(0, 8, 2):
                         turned = [block[m : m + 1] * cosine + swapped[m : m + 1] * sine for m in (k, k + 1)]
-                        at = pl.multiple_of(i * TILE + k * LPAD, 2 * LPAD)
+                        at = pl.multiple_of(i * 8 * LPAD + k * LPAD, 2 * LPAD)
                         out_ref[half, pl.ds(at, 2 * LPAD), lanes] = jnp.concatenate(turned, axis=0).astype(jnp.bfloat16)
             return carry
 
@@ -283,43 +278,48 @@
             jax.ShapeDtypeStruct((2, height, DEEP), jnp.bfloat16),
             jax.ShapeDtypeStruct((2, CHIP_ROWS, 128), jnp.bfloat16),
         ],
-        in_specs=[VMEM, ANY],
+        in_specs=[VMEM],
         out_specs=[VMEM, VMEM],
-        scratch_shapes=[
-            pltpu.VMEM((CHIPS, CHIP_ROWS, WIDE), jnp.float32),
-            pltpu.VMEM((2, LPAD, COLS), jnp.float32),
-            pltpu.SemaphoreType.DMA,
-        ],
+        scratch_shapes=[pltpu.VMEM((CHIPS, CHIP_ROWS, WIDE), jnp.float32)],
         compiler_params=pltpu.CompilerParams(vmem_limit_bytes=18 * MIB),
         cost_estimate=pl.CostEstimate(flops=6 * height * DEEP, bytes_accessed=4 * height * DEEP, transcendentals=0),
         name="turn",
-    )(own, lag_tables())
-
-
-def lags_kernel(half, first, count, pieces, has_acc, partners_ref, turned_ref, valid_ref, *refs):
-    far = refs[:pieces]
-    acc_ref = refs[pieces] if has_acc else None
+    )(own)
+
+
+def lags_kernel(groups, first, count, has_acc, partners_ref, turned_ref, valid_ref, *refs):
+    acc_ref = refs[-2] if has_acc else None
     out_ref = refs[-1]
-    which = [(partner(partners_ref, q)[2] + half) % 2 for q in range(SLOTS)]
+    taken, at = [], 0
+    for half, low, high in groups:
+        taken.append((half, low, high, refs[at : at + high - low]))
+        at += high - low
+
+    def half_of(q, half):
+        return (partner(partners_ref, q)[2] + half) % 2
 
     def tile(i, carry):
         source = pl.ds(pl.multiple_of(first * LPAD + i * TILE, TILE), TILE)
         target = pl.ds(pl.multiple_of(i * TILE, TILE), TILE)
         for q in range(SLOTS):
             lanes = slice(q * STA, (q + 1) * STA)
-            piece = jnp.concatenate([ref[q * SENT : q * SENT + WHITE] for ref in far], axis=0)
-            total = jnp.dot(turned_ref[which[q], source], piece, preferred_element_type=jnp.float32)
-            if has_acc:
-                total += acc_ref[source, lanes]
+            total = acc_ref[source, lanes] if has_acc else 0.0
+            for half, low, high, far in taken:
+                rows = jnp.concatenate([ref[q * SENT : q * SENT + WHITE] for ref in far], axis=0)
+                turned = turned_ref[half_of(q, half), source, low * WHITE : high * WHITE]
+                total += jnp.dot(turned, rows, preferred_element_type=jnp.float32)
             out_ref[target, lanes] = total.astype(out_ref.dtype)
         return carry
 
     lax.fori_loop(0, count * LPAD // TILE, tile, 0)
     for q in range(SLOTS):
         lanes = slice(q * STA, (q + 1) * STA)
-        mask = jnp.concatenate([ref[q * SENT + WHITE : (q + 1) * SENT] for ref in far], axis=0)
-        valid = valid_ref[which[q], first : first + count, : CHIPS * MASK_ROWS]
-        tally = jnp.dot(valid, mask, preferred_element_type=jnp.float32)
+        tally = 0.0
+        for half, low, high, far in taken:
+            mask = jnp.concatenate([ref[q * SENT + WHITE : (q + 1) * SENT] for ref in far], axis=0)
+            valid = valid_ref[half_of(q, half), first : first + count]
+            valid = valid[:, low * MASK_ROWS : high * MASK_ROWS]
+            tally += jnp.dot(valid, mask, preferred_element_type=jnp.float32)
         for m in range(count):
             row = m * LPAD + TALLY_ROW
             value = tally[m : m + 1]
@@ -328,16 +328,18 @@
             out_ref[row : row + 1, lanes] = value.astype(out_ref.dtype)
 
 
-def into_lags(partners, own, far, half, first, count, acc=None, dtype=jnp.float32):
+def into_lags(partners, own, groups, first, count, acc=None, dtype=jnp.float32):
+    far = [piece for _, _, pieces in groups for piece in pieces]
     args = [partners, *own, *far] + ([] if acc is None else [acc])
+    spans = tuple((half, low, low + len(pieces)) for half, low, pieces in groups)
     return pl.pallas_call(
-        functools.partial(lags_kernel, half, first, count, len(far), acc is not None),
+        functools.partial(lags_kernel, spans, first, count, acc is not None),
         out_shape=jax.ShapeDtypeStruct((count * LPAD, SLOTS * STA), dtype),
         in_specs=[SMEM] + [VMEM] * (len(args) - 1),
         out_specs=VMEM,
         compiler_params=pltpu.CompilerParams(vmem_limit_bytes=8 * MIB),
         cost_estimate=pl.CostEstimate(
-            flops=2 * count * LPAD * SLOTS * STA * DEEP,
+            flops=2 * count * LPAD * SLOTS * STA * WHITE * len(far),
             bytes_accessed=4 * count * LPAD * SLOTS * STA,
             transcendentals=0,
         ),
@@ -345,25 +347,32 @@
     )(*args)
 
 
-def combine_kernel(mine_ref, theirs_ref, out_ref):
-    for m in range(out_ref.shape[0]):
-        rows = slice(m * LPAD, (m + 1) * LPAD)
-        total = mine_ref[rows] + theirs_ref[rows].astype(jnp.float32)
-        result = total[:LAGS] / jnp.maximum(total[TALLY_ROW : TALLY_ROW + 1], 1.0)
-        for q in range(SLOTS):
-            out_ref[m, :, q] = result[:, q * STA : (q + 1) * STA]
+def combine_kernel(mine_ref, theirs_ref, out_hbm, out, sems):
+    parts = sems.shape[0]
+    step = out.shape[0] // parts
+    copies = []
+    for i in range(parts):
+        for m in range(i * step, (i + 1) * step):
+            rows = slice(m * LPAD, (m + 1) * LPAD)
+            total = mine_ref[rows] + theirs_ref[rows].astype(jnp.float32)
+            result = total[:LAGS] / jnp.maximum(total[TALLY_ROW : TALLY_ROW + 1], 1.0)
+            for q in range(SLOTS):
+                out[m, :, q] = result[:, q * STA : (q + 1) * STA]
+        here = pl.ds(i * step, step)
+        copies.append(pltpu.make_async_copy(out.at[here], out_hbm.at[here], sems.at[i]))
+        copies[-1].start()
+    for copy in copies:
+        copy.wait()
 
 
 def combined(mine, theirs):
-    stations = mine.shape[0] // LPAD
-    step = 4
-    block = pl.BlockSpec((step * LPAD, mine.shape[1]), lambda i: (i, 0))
+    shape = (mine.shape[0] // LPAD, LAGS, SLOTS, STA)
     out = pl.pallas_call(
         combine_kernel,
-        out_shape=jax.ShapeDtypeStruct((stations, LAGS, SLOTS, STA), jnp.float32),
-        grid=(stations // step,),
-        in_specs=[block, block],
-        out_specs=pl.BlockSpec((step, LAGS, SLOTS, STA), lambda i: (i, 0, 0, 0)),
+        out_shape=jax.ShapeDtypeStruct(shape, jnp.float32),
+        in_specs=[VMEM, VMEM],
+        out_specs=ANY,
+        scratch_shapes=[pltpu.VMEM(shape, jnp.float32), pltpu.SemaphoreType.DMA((8,))],
         compiler_params=pltpu.CompilerParams(vmem_limit_bytes=8 * MIB),
         name="combine",
     )(mine, theirs)
@@ -377,18 +386,19 @@
         back, on = send(white, to_block(1)), send(white, to_block(-1))
         return [back, on, send(back, to_block(1)), send(on, to_block(-1))]
 
-    def partner_rows(white):
-        held = chosen(partners, neighbours(white))
+    def spread(held):
         return [held] + [send(held, to_chip(by)) for by in TURNS[1:]]
 
     white = whitened(records, validity)
     other = send(white, to_other_half)
-    far, other_far = partner_rows(white), partner_rows(other)
-    own = own_stations(white, other)
+    rows = by_rows(rows_kernel, OWN // 2, white)
+    rows, other = lax.optimization_barrier((rows, other))
+    far, other_far = spread(chosen(partners, neighbours(white))), spread(chosen(partners, neighbours(other)))
+    own = by_rows(own_kernel, OWN, rows, other)
     own = turned_rows(lax.all_to_all(own, "tm", 0, 0, axis_index_groups=CHIP_GROUPS, tiled=True))
 
-    acc = into_lags(partners, own, far, 0, 0, CHIP_ROWS)
-    last = functools.partial(into_lags, partners, own, other_far, 1, acc=acc)
+    acc = into_lags(partners, own, [(0, 0, far)], 0, CHIP_ROWS)
+    last = functools.partial(into_lags, partners, own, [(1, 0, other_far)], acc=acc)
     theirs = send(last(0, ROW_BLOCK, dtype=jnp.bfloat16), to_core)
     return combined(last(ROW_BLOCK, ROW_BLOCK), theirs)
 

time: 114 us -> 113 us (level)
  starting transfers between devices: 74.5 us -> 76.9 us
  Pallas kernels: 23.6 us -> 21.8 us
    ppermute x16, starting transfers between devices: 70 us -> 72.3 us  [send(): return lax.ppermute(array, AXES, routes(target))]
    pallas_call x5 -> x6, Pallas kernels: 14.3 us -> 12.5 us  [the longest x3 9.92 us: into_lags(): pl.pallas_call(functools.partial(lags_kernel, spans, first, count, acc is...]
    unnamed x8 -> x6, local copies, waits for them, and re-layouts: 2.48 us -> 1.6 us
where the time goes in v4:
time: 113 us; the launch traced here: 112 us
  starting transfers between devices  76.9 us (68%)
  Pallas kernels  21.8 us (19%)
  waiting for transfers between devices  11.3 us (10%)
  local copies, waits for them, and re-layouts  1.6 us (1%)
    ppermute x16, starting transfers between devices, send(): return lax.ppermute(array, AXES, routes(target))  72.3 us
    ppermute x16, waiting for transfers between devices, send(): return lax.ppermute(array, AXES, routes(target))  11.3 us
    pallas_call x3, Pallas kernels, into_lags(): pl.pallas_call(functools.partial(lags_kernel, spans, first, count, acc is...  9.92 us
    pallas_call x1, Pallas kernels, turned_rows(): pl.pallas_call(turn_kernel, out_shape=[jax.ShapeDtypeStruct((2, height, D...  4.68 us
    all_to_all x1, starting transfers between devices, body(): lax.all_to_all(own, 'tm', 0, 0, axis_index_groups=CHIP_GROUPS, tiled=True)  4.53 us
    pallas_call x1, Pallas kernels, whitened(): pl.pallas_call(whiten_kernel, out_shape=jax.ShapeDtypeStruct((SENT, rows)...  3.35 us
  transfers between devices with their start and end apart: 17, of which 2 were waited for; matrix products, arithmetic and copies ran while one was open for 0% of the time, Pallas kernels for 13%

profile of v4, /device:TPU:11, one launch (start us, length us, event | category | flops | bytes accessed | tf_op | source)
XLA Modules:
  0.0 112.0 jit_solution(720638914138152769)
XLA Ops:
  0.0 3.3 %whiten.1.white_ref = bf16[400,256]{1,0:T(8,128)(2,1)} custom-call(bf16[1800,256]{1,0:T(8,128)(2,1)} %bitcast.9, s32[3,256]{1,0:T(4,128)} %bitcast.10, f32[64,64]{1,0:T(8,128)} %constant.4.clone.avg_hbm, bf16[3,128,616]{2,1,0:T(8,128)(2,1)} %constant.5.clone.table_hbm), custom_call_target="tpu_custom_call" | custom-call | tf_op jit(solution)/shard_map/whiten/pallas_call | solution.py:154
  3.4 11.0 %collective-permute-start.9 = (bf16[400,256]{1,0:T(8,128)(2,1)}, bf16[400,256]{1,0:T(8,128)(2,1)S(1)}, u32[]{:S(2)}, u32[]{:S(2)}) collective-permute-start(bf16[400,256]{1,0:T(8,128)(2,1)} %whiten.1.white_ref), channel_id=1, source_target_pairs={{16,0},{17,1},{18,2},{19,3},{20,4},{21,5},{22,6},{23,7},{24,8},{25... | collective-permute-start | bytes 614408 | tf_op jit(solution)/shard_map/ppermute | solution.py:104
  14.4 1.9 %collective-permute-start.8 = (bf16[400,256]{1,0:T(8,128)(2,1)}, bf16[400,256]{1,0:T(8,128)(2,1)S(1)}, u32[]{:S(2)}, u32[]{:S(2)}) collective-permute-start(bf16[400,256]{1,0:T(8,128)(2,1)} %whiten.1.white_ref), channel_id=1, source_target_pairs={{0,16},{1,17},{2,18},{3,19},{4,20},{5,21},{6,22},{7,23},{8,24},{9,... | collective-permute-start | bytes 614408 | tf_op jit(solution)/shard_map/ppermute | solution.py:104
  16.3 7.8 %collective-permute-start = (bf16[400,256]{1,0:T(8,128)(2,1)}, bf16[400,256]{1,0:T(8,128)(2,1)S(1)}, u32[]{:S(2)}, u32[]{:S(2)}) collective-permute-start(bf16[400,256]{1,0:T(8,128)(2,1)} %whiten.1.white_ref), channel_id=1, source_target_pairs={{0,8},{1,9},{2,10},{3,11},{4,12},{5,13},{6,14},{7,15},{8,0},{9,1},... | collective-permute-start | bytes 614408 | tf_op jit(solution)/shard_map/ppermute | solution.py:104
  24.1 0.0 collective-permute-done.9.refs_1_
  24.1 4.0 %collective-permute-start.11 = (bf16[400,256]{1,0:T(8,128)(2,1)S(1)}, bf16[400,256]{1,0:T(8,128)(2,1)S(1)}, u32[]{:S(2)}, u32[]{:S(2)}) collective-permute-start(bf16[400,256]{1,0:T(8,128)(2,1)S(1)} %collective-permute-done.9.refs_1_), channel_id=1, source_target_pairs={{16,0},{17,1},{18,2},{19,3},{20,4},{21,5},{22,6},{23,7},{24,8},{25... | collective-permute-start | bytes 614408 | tf_op jit(solution)/shard_map/ppermute | solution.py:104
  28.2 0.0 collective-permute-done.8.refs_0_
  28.2 1.9 %collective-permute-start.10 = (bf16[400,256]{1,0:T(8,128)(2,1)S(1)}, bf16[400,256]{1,0:T(8,128)(2,1)S(1)}, u32[]{:S(2)}, u32[]{:S(2)}) collective-permute-start(bf16[400,256]{1,0:T(8,128)(2,1)S(1)} %collective-permute-done.8.refs_0_), channel_id=1, source_target_pairs={{0,16},{1,17},{2,18},{3,19},{4,20},{5,21},{6,22},{7,23},{8,24},{9,... | collective-permute-start | bytes 614408 | tf_op jit(solution)/shard_map/ppermute | solution.py:104
  30.1 0.0 copy-start
  30.1 0.9 copy-done
  31.0 0.1 rows.2.first_ref
  31.2 10.0 %collective-permute-done.other_ref = bf16[400,256]{1,0:T(8,128)(2,1)S(1)} collective-permute-done((bf16[400,256]{1,0:T(8,128)(2,1)}, bf16[400,256]{1,0:T(8,128)(2,1)S(1)}, u32[]{:S(2)}, u32[]{:S(2)}) %collective-permute-start) | collective-permute-done | bytes 204832 | tf_op jit(solution)/shard_map/ppermute | solution.py:104
  41.2 6.5 %collective-permute-start.2 = (bf16[400,256]{1,0:T(8,128)(2,1)S(1)}, bf16[400,256]{1,0:T(8,128)(2,1)S(1)}, u32[]{:S(2)}, u32[]{:S(2)}) collective-permute-start(bf16[400,256]{1,0:T(8,128)(2,1)S(1)} %collective-permute-done.other_ref), channel_id=1, source_target_pairs={{16,0},{17,1},{18,2},{19,3},{20,4},{21,5},{22,6},{23,7},{24,8},{25... | collective-permute-start | bytes 614408 | tf_op jit(solution)/shard_map/ppermute | solution.py:104
  47.7 1.9 %collective-permute-start.1 = (bf16[400,256]{1,0:T(8,128)(2,1)S(1)}, bf16[400,256]{1,0:T(8,128)(2,1)S(1)}, u32[]{:S(2)}, u32[]{:S(2)}) collective-permute-start(bf16[400,256]{1,0:T(8,128)(2,1)S(1)} %collective-permute-done.other_ref), channel_id=1, source_target_pairs={{0,16},{1,17},{2,18},{3,19},{4,20},{5,21},{6,22},{7,23},{8,24},{9,... | collective-permute-start | bytes 614408 | tf_op jit(solution)/shard_map/ppermute | solution.py:104
  49.6 0.0 collective-permute-done.11.refs_3_
  49.6 0.0 collective-permute-done.10.refs_2_
  49.7 0.0 copy-start.1
  49.7 0.7 copy-done.1
  50.3 0.6 choose.3.refs_0_
  51.0 3.8 %collective-permute-start.14 = (bf16[800,256]{1,0:T(8,128)(2,1)S(1)}, bf16[800,256]{1,0:T(8,128)(2,1)S(1)}, u32[]{:S(2)}, u32[]{:S(2)}) collective-permute-start(bf16[800,256]{1,0:T(8,128)(2,1)S(1)} %choose.3.refs_0_), channel_id=1, source_target_pairs={{0,4},{1,5},{2,6},{3,7},{4,0},{5,1},{6,2},{7,3},{8,12},{9,13},{10,... | collective-permute-start | bytes 1228808 | tf_op jit(solution)/shard_map/ppermute | solution.py:104
  54.7 3.1 %collective-permute-start.13 = (bf16[800,256]{1,0:T(8,128)(2,1)S(1)}, bf16[800,256]{1,0:T(8,128)(2,1)S(1)}, u32[]{:S(2)}, u32[]{:S(2)}) collective-permute-start(bf16[800,256]{1,0:T(8,128)(2,1)S(1)} %choose.3.refs_0_), channel_id=1, source_target_pairs={{0,6},{1,7},{2,0},{3,1},{4,2},{5,3},{6,4},{7,5},{8,14},{9,15},{10,... | collective-permute-start | bytes 1228808 | tf_op jit(solution)/shard_map/ppermute | solution.py:104
  57.8 2.2 %collective-permute-start.12 = (bf16[800,256]{1,0:T(8,128)(2,1)S(1)}, bf16[800,256]{1,0:T(8,128)(2,1)S(1)}, u32[]{:S(2)}, u32[]{:S(2)}) collective-permute-start(bf16[800,256]{1,0:T(8,128)(2,1)S(1)} %choose.3.refs_0_), channel_id=1, source_target_pairs={{0,2},{1,3},{2,4},{3,5},{4,6},{5,7},{6,0},{7,1},{8,10},{9,11},{10,... | collective-permute-start | bytes 1228808 | tf_op jit(solution)/shard_map/ppermute | solution.py:104
  60.0 0.0 collective-permute-done.2.refs_1_
  60.0 5.5 %collective-permute-start.4 = (bf16[400,256]{1,0:T(8,128)(2,1)S(1)}, bf16[400,256]{1,0:T(8,128)(2,1)S(1)}, u32[]{:S(2)}, u32[]{:S(2)}) collective-permute-start(bf16[400,256]{1,0:T(8,128)(2,1)S(1)} %collective-permute-done.2.refs_1_), channel_id=1, source_target_pairs={{16,0},{17,1},{18,2},{19,3},{20,4},{21,5},{22,6},{23,7},{24,8},{25... | collective-permute-start | bytes 614408 | tf_op jit(solution)/shard_map/ppermute | solution.py:104
  65.5 0.0 collective-permute-done.1.refs_0_
  65.5 1.9 %collective-permute-start.3 = (bf16[400,256]{1,0:T(8,128)(2,1)S(1)}, bf16[400,256]{1,0:T(8,128)(2,1)S(1)}, u32[]{:S(2)}, u32[]{:S(2)}) collective-permute-start(bf16[400,256]{1,0:T(8,128)(2,1)S(1)} %collective-permute-done.1.refs_0_), channel_id=1, source_target_pairs={{0,16},{1,17},{2,18},{3,19},{4,20},{5,21},{6,22},{7,23},{8,24},{9,... | collective-permute-start | bytes 614408 | tf_op jit(solution)/shard_map/ppermute | solution.py:104
  67.5 0.9 rows.3
  68.3 4.5 %all-to-all-start = ((bf16[4,128,256]{2,1,0:T(8,128)(2,1)}), bf16[4,128,256]{2,1,0:T(8,128)(2,1)S(1)}, u32[]{:S(2)}, u32[]{:S(2)}) async-start(bf16[4,128,256]{2,1,0:T(8,128)(2,1)} %rows.3), calls=%async_computation | async-start | bytes 524288 | tf_op jit(solution)/shard_map/all_to_all | solution.py:398
  72.8 0.0 collective-permute-done.4.refs_3_
  72.9 1.3 %collective-permute-done.3.refs_2_ = bf16[400,256]{1,0:T(8,128)(2,1)S(1)} collective-permute-done((bf16[400,256]{1,0:T(8,128)(2,1)S(1)}, bf16[400,256]{1,0:T(8,128)(2,1)S(1)}, u32[]{:S(2)}, u32[]{:S(2)}) %collective-permute-start.3) | collective-permute-done | bytes 204832 | tf_op jit(solution)/shard_map/ppermute | solution.py:104
  74.2 0.6 choose.2.refs_0_
  74.8 4.2 %collective-permute-start.7 = (bf16[800,256]{1,0:T(8,128)(2,1)S(1)}, bf16[800,256]{1,0:T(8,128)(2,1)S(1)}, u32[]{:S(2)}, u32[]{:S(2)}) collective-permute-start(bf16[800,256]{1,0:T(8,128)(2,1)S(1)} %choose.2.refs_0_), channel_id=1, source_target_pairs={{0,4},{1,5},{2,6},{3,7},{4,0},{5,1},{6,2},{7,3},{8,12},{9,13},{10,... | collective-permute-start | bytes 1228808 | tf_op jit(solution)/shard_map/ppermute | solution.py:104
  79.0 1.9 %collective-permute-start.6 = (bf16[800,256]{1,0:T(8,128)(2,1)S(1)}, bf16[800,256]{1,0:T(8,128)(2,1)S(1)}, u32[]{:S(2)}, u32[]{:S(2)}) collective-permute-start(bf16[800,256]{1,0:T(8,128)(2,1)S(1)} %choose.2.refs_0_), channel_id=1, source_target_pairs={{0,6},{1,7},{2,0},{3,1},{4,2},{5,3},{6,4},{7,5},{8,14},{9,15},{10,... | collective-permute-start | bytes 1228808 | tf_op jit(solution)/shard_map/ppermute | solution.py:104
  81.0 0.0 collective-permute-done.14.refs_3_
  81.0 3.4 %collective-permute-start.5 = (bf16[800,256]{1,0:T(8,128)(2,1)S(1)}, bf16[800,256]{1,0:T(8,128)(2,1)S(1)}, u32[]{:S(2)}, u32[]{:S(2)}) collective-permute-start(bf16[800,256]{1,0:T(8,128)(2,1)S(1)} %choose.2.refs_0_), channel_id=1, source_target_pairs={{0,2},{1,3},{2,4},{3,5},{4,6},{5,7},{6,0},{7,1},{8,10},{9,11},{10,... | collective-permute-start | bytes 1228808 | tf_op jit(solution)/shard_map/ppermute | solution.py:104
  84.4 0.0 all-to-all-done.own_ref
  84.4 4.7 %turn.1 = (bf16[2,2304,1536]{2,1,0:T(8,128)(2,1)S(1)}, bf16[2,32,128]{2,1,0:T(8,128)(2,1)S(1)}) custom-call(bf16[4,128,256]{2,1,0:T(8,128)(2,1)S(1)} %all-to-all-done.own_ref), custom_call_target="tpu_custom_call" | custom-call | flops 21233664 | bytes 14155776 | tf_op jit(solution)/shard_map/turn/pallas_call | solution.py:275
  89.1 0.0 collective-permute-done.13.refs_2_
  89.1 0.0 collective-permute-done.12.refs_1_
  89.1 4.8 %lags.3.refs_4_ = f32[2304,512]{1,0:T(8,128)S(1)} custom-call(s32[2,32]{1,0:T(2,128)S(1)} %bitcast.6, bf16[2,2304,1536]{2,1,0:T(8,128)(2,1)S(1)} %get-tuple-element.11.turned_ref, bf16[2,32,128]{2,1,0:T(8,128)(2,1)S(1)} %get-tuple-element.12.valid_ref, bf16[800,256]{1,0:T(8,128)(2,1)S(1)} %choose.3.refs_0_, ...), custom_call_target="tpu_custom_call" | custom-call | flops 3623878656 | bytes 4718592 | tf_op jit(solution)/shard_map/lags/pallas_call | solution.py:335
  93.8 0.0 collective-permute-done.7.refs_3_
  93.8 0.0 collective-permute-done.6.refs_2_
  93.9 0.0 collective-permute-done.5.refs_1_
  93.9 2.6 %lags.5 = bf16[1152,512]{1,0:T(8,128)(2,1)S(1)} custom-call(s32[2,32]{1,0:T(2,128)S(1)} %bitcast.7, bf16[2,2304,1536]{2,1,0:T(8,128)(2,1)S(1)} %get-tuple-element.11.turned_ref, bf16[2,32,128]{2,1,0:T(8,128)(2,1)S(1)} %get-tuple-element.12.valid_ref, bf16[800,256]{1,0:T(8,128)(2,1)S(1)} %choose.2.refs_0_, ...), custom_call_target="tpu_custom_call" | custom-call | flops 1811939328 | bytes 2359296 | tf_op jit(solution)/shard_map/lags/pallas_call | solution.py:335
  96.5 11.3 %collective-permute-start.15 = (bf16[1152,512]{1,0:T(8,128)(2,1)S(1)}, bf16[1152,512]{1,0:T(8,128)(2,1)S(1)}, u32[]{:S(2)}, u32[]{:S(2)}) collective-permute-start(bf16[1152,512]{1,0:T(8,128)(2,1)S(1)} %lags.5), channel_id=1, source_target_pairs={{0,1},{1,0},{2,3},{3,2},{4,5},{5,4},{6,7},{7,6},{8,9},{9,8},{10,11... | collective-permute-start | bytes 3538952 | tf_op jit(solution)/shard_map/ppermute | solution.py:104
  107.7 2.6 %lags.4.mine_ref = f32[1152,512]{1,0:T(8,128)S(1)} custom-call(s32[2,32]{1,0:T(2,128)S(1)} %bitcast.8, bf16[2,2304,1536]{2,1,0:T(8,128)(2,1)S(1)} %get-tuple-element.11.turned_ref, bf16[2,32,128]{2,1,0:T(8,128)(2,1)S(1)} %get-tuple-element.12.valid_ref, bf16[800,256]{1,0:T(8,128)(2,1)S(1)} %choose.2.refs_0_, ...), custom_call_target="tpu_custom_call" | custom-call | flops 1811939328 | bytes 2359296 | tf_op jit(solution)/shard_map/lags/pallas_call | solution.py:335
  110.3 0.0 collective-permute-done.15.theirs_ref
  110.3 1.6 %combine.1 = f32[16,65,2,256]{3,2,1,0:T(2,128)} custom-call(f32[1152,512]{1,0:T(8,128)S(1)} %lags.4.mine_ref, bf16[1152,512]{1,0:T(8,128)(2,1)S(1)} %collective-permute-done.15.theirs_ref), custom_call_target="tpu_custom_call" | custom-call | tf_op jit(solution)/shard_map/combine/pallas_call | solution.py:370
  (2 shorter events, 0.0 us)
Async XLA Ops:
  0.0 74.2 %copy-start.2 = (s32[32,2]{0,1:T(2,128)S(1)}, s32[32,2]{0,1:T(2,128)}, u32[]{:S(2)}) copy-start(s32[32,2]{0,1:T(2,128)} %param.7) | copy-start | bytes 772
  3.4 20.7 %collective-permute-start.9 = (bf16[400,256]{1,0:T(8,128)(2,1)}, bf16[400,256]{1,0:T(8,128)(2,1)S(1)}, u32[]{:S(2)}, u32[]{:S(2)}) collective-permute-start(bf16[400,256]{1,0:T(8,128)(2,1)} %whiten.1.white_ref), channel_id=1, source_target_pairs={{16,0},{17,1},{18,2},{19,3},{20,4},{21,5},{22,6},{23,7},{24,8},{25... | collective-permute-start | bytes 614408 | tf_op jit(solution)/shard_map/ppermute | solution.py:104
  14.4 13.8 %collective-permute-start.8 = (bf16[400,256]{1,0:T(8,128)(2,1)}, bf16[400,256]{1,0:T(8,128)(2,1)S(1)}, u32[]{:S(2)}, u32[]{:S(2)}) collective-permute-start(bf16[400,256]{1,0:T(8,128)(2,1)} %whiten.1.white_ref), channel_id=1, source_target_pairs={{0,16},{1,17},{2,18},{3,19},{4,20},{5,21},{6,22},{7,23},{8,24},{9,... | collective-permute-start | bytes 614408 | tf_op jit(solution)/shard_map/ppermute | solution.py:104
  16.3 24.9 %collective-permute-start = (bf16[400,256]{1,0:T(8,128)(2,1)}, bf16[400,256]{1,0:T(8,128)(2,1)S(1)}, u32[]{:S(2)}, u32[]{:S(2)}) collective-permute-start(bf16[400,256]{1,0:T(8,128)(2,1)} %whiten.1.white_ref), channel_id=1, source_target_pairs={{0,8},{1,9},{2,10},{3,11},{4,12},{5,13},{6,14},{7,15},{8,0},{9,1},... | collective-permute-start | bytes 614408 | tf_op jit(solution)/shard_map/ppermute | solution.py:104
  24.1 25.5 %collective-permute-start.11 = (bf16[400,256]{1,0:T(8,128)(2,1)S(1)}, bf16[400,256]{1,0:T(8,128)(2,1)S(1)}, u32[]{:S(2)}, u32[]{:S(2)}) collective-permute-start(bf16[400,256]{1,0:T(8,128)(2,1)S(1)} %collective-permute-done.9.refs_1_), channel_id=1, source_target_pairs={{16,0},{17,1},{18,2},{19,3},{20,4},{21,5},{22,6},{23,7},{24,8},{25... | collective-permute-start | bytes 614408 | tf_op jit(solution)/shard_map/ppermute | solution.py:104
  28.2 21.5 %collective-permute-start.10 = (bf16[400,256]{1,0:T(8,128)(2,1)S(1)}, bf16[400,256]{1,0:T(8,128)(2,1)S(1)}, u32[]{:S(2)}, u32[]{:S(2)}) collective-permute-start(bf16[400,256]{1,0:T(8,128)(2,1)S(1)} %collective-permute-done.8.refs_0_), channel_id=1, source_target_pairs={{0,16},{1,17},{2,18},{3,19},{4,20},{5,21},{6,22},{7,23},{8,24},{9,... | collective-permute-start | bytes 614408 | tf_op jit(solution)/shard_map/ppermute | solution.py:104
  30.1 0.9 copy-start
  41.2 18.9 %collective-permute-start.2 = (bf16[400,256]{1,0:T(8,128)(2,1)S(1)}, bf16[400,256]{1,0:T(8,128)(2,1)S(1)}, u32[]{:S(2)}, u32[]{:S(2)}) collective-permute-start(bf16[400,256]{1,0:T(8,128)(2,1)S(1)} %collective-permute-done.other_ref), channel_id=1, source_target_pairs={{16,0},{17,1},{18,2},{19,3},{20,4},{21,5},{22,6},{23,7},{24,8},{25... | collective-permute-start | bytes 614408 | tf_op jit(solution)/shard_map/ppermute | solution.py:104
  47.7 17.8 %collective-permute-start.1 = (bf16[400,256]{1,0:T(8,128)(2,1)S(1)}, bf16[400,256]{1,0:T(8,128)(2,1)S(1)}, u32[]{:S(2)}, u32[]{:S(2)}) collective-permute-start(bf16[400,256]{1,0:T(8,128)(2,1)S(1)} %collective-permute-done.other_ref), channel_id=1, source_target_pairs={{0,16},{1,17},{2,18},{3,19},{4,20},{5,21},{6,22},{7,23},{8,24},{9,... | collective-permute-start | bytes 614408 | tf_op jit(solution)/shard_map/ppermute | solution.py:104
  49.7 0.7 copy-start.1
  51.0 30.0 %collective-permute-start.14 = (bf16[800,256]{1,0:T(8,128)(2,1)S(1)}, bf16[800,256]{1,0:T(8,128)(2,1)S(1)}, u32[]{:S(2)}, u32[]{:S(2)}) collective-permute-start(bf16[800,256]{1,0:T(8,128)(2,1)S(1)} %choose.3.refs_0_), channel_id=1, source_target_pairs={{0,4},{1,5},{2,6},{3,7},{4,0},{5,1},{6,2},{7,3},{8,12},{9,13},{10,... | collective-permute-start | bytes 1228808 | tf_op jit(solution)/shard_map/ppermute | solution.py:104
  54.7 34.3 %collective-permute-start.13 = (bf16[800,256]{1,0:T(8,128)(2,1)S(1)}, bf16[800,256]{1,0:T(8,128)(2,1)S(1)}, u32[]{:S(2)}, u32[]{:S(2)}) collective-permute-start(bf16[800,256]{1,0:T(8,128)(2,1)S(1)} %choose.3.refs_0_), channel_id=1, source_target_pairs={{0,6},{1,7},{2,0},{3,1},{4,2},{5,3},{6,4},{7,5},{8,14},{9,15},{10,... | collective-permute-start | bytes 1228808 | tf_op jit(solution)/shard_map/ppermute | solution.py:104
  57.8 31.3 %collective-permute-start.12 = (bf16[800,256]{1,0:T(8,128)(2,1)S(1)}, bf16[800,256]{1,0:T(8,128)(2,1)S(1)}, u32[]{:S(2)}, u32[]{:S(2)}) collective-permute-start(bf16[800,256]{1,0:T(8,128)(2,1)S(1)} %choose.3.refs_0_), channel_id=1, source_target_pairs={{0,2},{1,3},{2,4},{3,5},{4,6},{5,7},{6,0},{7,1},{8,10},{9,11},{10,... | collective-permute-start | bytes 1228808 | tf_op jit(solution)/shard_map/ppermute | solution.py:104
  60.0 12.8 %collective-permute-start.4 = (bf16[400,256]{1,0:T(8,128)(2,1)S(1)}, bf16[400,256]{1,0:T(8,128)(2,1)S(1)}, u32[]{:S(2)}, u32[]{:S(2)}) collective-permute-start(bf16[400,256]{1,0:T(8,128)(2,1)S(1)} %collective-permute-done.2.refs_1_), channel_id=1, source_target_pairs={{16,0},{17,1},{18,2},{19,3},{20,4},{21,5},{22,6},{23,7},{24,8},{25... | collective-permute-start | bytes 614408 | tf_op jit(solution)/shard_map/ppermute | solution.py:104
  65.5 8.6 %collective-permute-start.3 = (bf16[400,256]{1,0:T(8,128)(2,1)S(1)}, bf16[400,256]{1,0:T(8,128)(2,1)S(1)}, u32[]{:S(2)}, u32[]{:S(2)}) collective-permute-start(bf16[400,256]{1,0:T(8,128)(2,1)S(1)} %collective-permute-done.1.refs_0_), channel_id=1, source_target_pairs={{0,16},{1,17},{2,18},{3,19},{4,20},{5,21},{6,22},{7,23},{8,24},{9,... | collective-permute-start | bytes 614408 | tf_op jit(solution)/shard_map/ppermute | solution.py:104
  68.3 16.0 %all-to-all-start = ((bf16[4,128,256]{2,1,0:T(8,128)(2,1)}), bf16[4,128,256]{2,1,0:T(8,128)(2,1)S(1)}, u32[]{:S(2)}, u32[]{:S(2)}) async-start(bf16[4,128,256]{2,1,0:T(8,128)(2,1)} %rows.3), calls=%async_computation | async-start | bytes 524288 | tf_op jit(solution)/shard_map/all_to_all | solution.py:398
  74.8 19.0 %collective-permute-start.7 = (bf16[800,256]{1,0:T(8,128)(2,1)S(1)}, bf16[800,256]{1,0:T(8,128)(2,1)S(1)}, u32[]{:S(2)}, u32[]{:S(2)}) collective-permute-start(bf16[800,256]{1,0:T(8,128)(2,1)S(1)} %choose.2.refs_0_), channel_id=1, source_target_pairs={{0,4},{1,5},{2,6},{3,7},{4,0},{5,1},{6,2},{7,3},{8,12},{9,13},{10,... | collective-permute-start | bytes 1228808 | tf_op jit(solution)/shard_map/ppermute | solution.py:104
  79.0 14.8 %collective-permute-start.6 = (bf16[800,256]{1,0:T(8,128)(2,1)S(1)}, bf16[800,256]{1,0:T(8,128)(2,1)S(1)}, u32[]{:S(2)}, u32[]{:S(2)}) collective-permute-start(bf16[800,256]{1,0:T(8,128)(2,1)S(1)} %choose.2.refs_0_), channel_id=1, source_target_pairs={{0,6},{1,7},{2,0},{3,1},{4,2},{5,3},{6,4},{7,5},{8,14},{9,15},{10,... | collective-permute-start | bytes 1228808 | tf_op jit(solution)/shard_map/ppermute | solution.py:104
  81.0 12.9 %collective-permute-start.5 = (bf16[800,256]{1,0:T(8,128)(2,1)S(1)}, bf16[800,256]{1,0:T(8,128)(2,1)S(1)}, u32[]{:S(2)}, u32[]{:S(2)}) collective-permute-start(bf16[800,256]{1,0:T(8,128)(2,1)S(1)} %choose.2.refs_0_), channel_id=1, source_target_pairs={{0,2},{1,3},{2,4},{3,5},{4,6},{5,7},{6,0},{7,1},{8,10},{9,11},{10,... | collective-permute-start | bytes 1228808 | tf_op jit(solution)/shard_map/ppermute | solution.py:104
  96.5 13.9 %collective-permute-start.15 = (bf16[1152,512]{1,0:T(8,128)(2,1)S(1)}, bf16[1152,512]{1,0:T(8,128)(2,1)S(1)}, u32[]{:S(2)}, u32[]{:S(2)}) collective-permute-start(bf16[1152,512]{1,0:T(8,128)(2,1)S(1)} %lags.5), channel_id=1, source_target_pairs={{0,1},{1,0},{2,3},{3,2},{4,5},{5,4},{6,7},{7,6},{8,9},{9,8},{10,11... | collective-permute-start | bytes 3538952 | tf_op jit(solution)/shard_map/ppermute | solution.py:104

commit v5 on v4

--- a/solution.py
+++ b/solution.py
@@ -28,6 +28,7 @@
 WHITE = 3 * COLS
 SENT = WHITE + MASK_ROWS
 WIDE = WHITE + 128
+OWN_AT = SLOTS * SENT
 OWN = 4 * CHIP_ROWS
 TURNS = (0, 1, -1, 2)
 TILE = 16 * LPAD
@@ -168,62 +169,69 @@
     )(records.T, validity.T, band_average(), window_tables(win_dev))
 
 
-def rows_kernel(white_ref, out_ref, half=0):
+def store_rows(out_ref, white_ref, at):
     lanes = pl.ds(pl.multiple_of(place()[0] * 128, 128), 128)
     blocks = [white_ref[g * COLS : (g + 1) * COLS, lanes].astype(jnp.float32) for g in range(WHITE // COLS)]
     mask = white_ref[WHITE:SENT, lanes].astype(jnp.float32)
     blocks.append(jnp.concatenate([mask, jnp.zeros((128 - MASK_ROWS, 128), jnp.float32)], axis=0))
     for g, block in enumerate(blocks):
         rows = block.T.astype(jnp.bfloat16)
-        at = (half * 2 + g // 2) * CHIP_ROWS
+        here = slice(at + g // 2 * CHIP_ROWS, at + (g // 2 + 1) * CHIP_ROWS)
         for x in range(CHIPS):
             piece = rows[x * CHIP_ROWS : (x + 1) * CHIP_ROWS]
-            out_ref[x, at : at + CHIP_ROWS, g % 2 * 128 : (g % 2 + 1) * 128] = piece
-
-
-def own_kernel(first_ref, other_ref, out_ref):
-    out_ref[:, : OWN // 2] = first_ref[...]
-    rows_kernel(other_ref, out_ref, 1)
-
-
-def by_rows(kernel, height, *args):
+            out_ref[x, here, g % 2 * 128 : (g % 2 + 1) * 128] = piece
+
+
+def rows_kernel(partners_ref, white_ref, out_ref):
+    del partners_ref
+    store_rows(out_ref, white_ref, 0)
+
+
+def own_rows(partners, white):
     return pl.pallas_call(
-        kernel,
-        out_shape=jax.ShapeDtypeStruct((CHIPS, height, STA), jnp.bfloat16),
-        in_specs=[VMEM] * len(args),
+        rows_kernel,
+        out_shape=jax.ShapeDtypeStruct((CHIPS, OWN // 2, STA), jnp.bfloat16),
+        in_specs=[SMEM, VMEM],
         out_specs=VMEM,
         compiler_params=pltpu.CompilerParams(vmem_limit_bytes=4 * MIB),
         name="rows",
-    )(*args)
+    )(partners, white)
 
 
 def choose_kernel(partners_ref, *refs):
-    blocks, out_ref = refs[:-1], refs[-1]
+    blocks, own, out_ref = refs[:4], refs[4:-1], refs[-1]
+    if own:
+        rows_ref, other_ref = own
+        out_ref[:, OWN_AT : OWN_AT + OWN // 2] = rows_ref[...]
+        store_rows(out_ref, other_ref, OWN_AT + OWN // 2)
     for q in range(SLOTS):
-        rows = slice(q * SENT, (q + 1) * SENT)
+        here = slice(q * SENT, (q + 1) * SENT)
         block, target, _ = partner(partners_ref, q)
         by = jnp.where(target < 0, 0, target - block)
 
         @pl.when(by == 0)
         def _():
-            out_ref[rows] = jnp.zeros((SENT, STA), jnp.bfloat16)
+            for x in range(out_ref.shape[0]):
+                out_ref[x, here] = jnp.zeros((SENT, STA), jnp.bfloat16)
 
         for step, ref in zip((-1, 1, -2, 2), blocks):
 
             @pl.when(by == step)
             def _():
-                out_ref[rows] = ref[...]
-
-
-def chosen(partners, blocks):
+                for x in range(out_ref.shape[0]):
+                    out_ref[x, here] = ref[...]
+
+
+def chosen(partners, blocks, *own):
+    shape = (CHIPS, OWN_AT + OWN, STA) if own else (1, OWN_AT, STA)
     return pl.pallas_call(
         choose_kernel,
-        out_shape=jax.ShapeDtypeStruct((SLOTS * SENT, STA), jnp.bfloat16),
-        in_specs=[SMEM] + [VMEM] * len(blocks),
+        out_shape=jax.ShapeDtypeStruct(shape, jnp.bfloat16),
+        in_specs=[SMEM] + [VMEM] * (len(blocks) + len(own)),
         out_specs=VMEM,
         compiler_params=pltpu.CompilerParams(vmem_limit_bytes=4 * MIB),
         name="choose",
-    )(partners, *blocks)
+    )(partners, *blocks, *own)
 
 
 def lag_tables():
@@ -246,7 +254,8 @@
             for h, whose in enumerate((1 - core, core)):
                 here = slice(h * ROW_BLOCK, (h + 1) * ROW_BLOCK)
                 for part in range(2):
-                    start = pl.multiple_of((half * 2 + part) * CHIP_ROWS + whose * ROW_BLOCK, ROW_BLOCK)
+                    at = OWN_AT + (half * 2 + part) * CHIP_ROWS
+                    start = pl.multiple_of(at + whose * ROW_BLOCK, ROW_BLOCK)
                     rows = own_ref[source, pl.ds(start, ROW_BLOCK)]
                     held[d, here, part * STA : (part + 1) * STA] = rows.astype(jnp.float32)
         mask = held[0, :, WHITE:]
@@ -291,9 +300,14 @@
     acc_ref = refs[-2] if has_acc else None
     out_ref = refs[-1]
     taken, at = [], 0
-    for half, low, high in groups:
-        taken.append((half, low, high, refs[at : at + high - low]))
-        at += high - low
+    for half, low, high, gathered in groups:
+        if gathered:
+            chip = place()[1]
+            taken.append((half, low, high, [refs[at].at[lax.rem(chip + CHIPS - by, CHIPS)] for by in TURNS]))
+            at += 1
+        else:
+            taken.append((half, low, high, refs[at : at + high - low]))
+            at += high - low
 
     def half_of(q, half):
         return (partner(partners_ref, q)[2] + half) % 2
@@ -331,7 +345,10 @@
 def into_lags(partners, own, groups, first, count, acc=None, dtype=jnp.float32):
     far = [piece for _, _, pieces in groups for piece in pieces]
     args = [partners, *own, *far] + ([] if acc is None else [acc])
-    spans = tuple((half, low, low + len(pieces)) for half, low, pieces in groups)
+    spans = tuple(
+        (half, low, CHIPS if pieces[0].ndim == 3 else low + len(pieces), pieces[0].ndim == 3)
+        for half, low, pieces in groups
+    )
     return pl.pallas_call(
         functools.partial(lags_kernel, spans, first, count, acc is not None),
         out_shape=jax.ShapeDtypeStruct((count * LPAD, SLOTS * STA), dtype),
@@ -386,19 +403,22 @@
         back, on = send(white, to_block(1)), send(white, to_block(-1))
         return [back, on, send(back, to_block(1)), send(on, to_block(-1))]
 
-    def spread(held):
-        return [held] + [send(held, to_chip(by)) for by in TURNS[1:]]
+    def to_chips(array):
+        return lax.all_to_all(array, "tm", 0, 0, axis_index_groups=CHIP_GROUPS, tiled=True)
 
     white = whitened(records, validity)
     other = send(white, to_other_half)
-    rows = by_rows(rows_kernel, OWN // 2, white)
-    rows, other = lax.optimization_barrier((rows, other))
-    far, other_far = spread(chosen(partners, neighbours(white))), spread(chosen(partners, neighbours(other)))
-    own = by_rows(own_kernel, OWN, rows, other)
-    own = turned_rows(lax.all_to_all(own, "tm", 0, 0, axis_index_groups=CHIP_GROUPS, tiled=True))
-
-    acc = into_lags(partners, own, [(0, 0, far)], 0, CHIP_ROWS)
-    last = functools.partial(into_lags, partners, own, [(1, 0, other_far)], acc=acc)
+    rows, other = lax.optimization_barrier((own_rows(partners, white), other))
+    near = neighbours(white)
+    other_near = neighbours(other)
+    near[2], near[3], late = lax.optimization_barrier((near[2], near[3], other))
+    far = to_chips(chosen(partners, near, rows, late))
+    (held,) = chosen(partners, other_near)
+    other_far = [held] + [send(held, to_chip(by)) for by in TURNS[1:]]
+    own = turned_rows(far)
+
+    acc = into_lags(partners, own, [(0, 0, [far]), (1, 0, other_far[:1])], 0, CHIP_ROWS)
+    last = functools.partial(into_lags, partners, own, [(1, 1, other_far[1:])], acc=acc)
     theirs = send(last(0, ROW_BLOCK, dtype=jnp.bfloat16), to_core)
     return combined(last(ROW_BLOCK, ROW_BLOCK), theirs)
 

time: 113 us -> 114 us (level)
  the two profiles are of different devices: /device:TPU:11 before, /device:TPU:9 now
where the time goes in v5:
time: 114 us; the launch traced here: 113 us
  starting transfers between devices  63.6 us (56%)
  waiting for transfers between devices  24.3 us (21%)
  Pallas kernels  22.4 us (20%)
  local copies, waits for them, and re-layouts  2.85 us (2%)
    ppermute x13, starting transfers between devices, send(): return lax.ppermute(array, AXES, routes(target))  59.4 us
    ppermute x13, waiting for transfers between devices, send(): return lax.ppermute(array, AXES, routes(target))  24.3 us
    pallas_call x3, Pallas kernels, into_lags(): pl.pallas_call(functools.partial(lags_kernel, spans, first, count, acc is...  10.5 us
    pallas_call x1, Pallas kernels, turned_rows(): pl.pallas_call(turn_kernel, out_shape=[jax.ShapeDtypeStruct((2, height, D...  4.69 us
    all_to_all x1, starting transfers between devices, to_chips(): lax.all_to_all(array, 'tm', 0, 0, axis_index_groups=CHIP_GROUPS, tiled=True)  4.14 us
    pallas_call x1, Pallas kernels, whitened(): pl.pallas_call(whiten_kernel, out_shape=jax.ShapeDtypeStruct((SENT, rows)...  3.33 us
    unnamed x8, local copies, waits for them, and re-layouts  2.85 us
  transfers between devices with their start and end apart: 14, of which 7 were waited for; matrix products, arithmetic and copies ran while one was open for 0% of the time, Pallas kernels for 13%

profile of v5, /device:TPU:9, one launch (start us, length us, event | category | flops | bytes accessed | tf_op | source)
XLA Modules:
  0.0 113.3 jit_solution(5029914133284093196)
XLA Ops:
  0.0 3.3 %whiten.1.white_ref = bf16[400,256]{1,0:T(8,128)(2,1)} custom-call(bf16[1800,256]{1,0:T(8,128)(2,1)} %bitcast.15, s32[3,256]{1,0:T(4,128)} %bitcast.16, f32[64,64]{1,0:T(8,128)} %constant.4.clone.avg_hbm, bf16[3,128,616]{2,1,0:T(8,128)(2,1)} %constant.5.clone.table_hbm), custom_call_target="tpu_custom_call" | custom-call | tf_op jit(solution)/shard_map/whiten/pallas_call | solution.py:155
  3.3 11.0 %collective-permute-start.1 = (bf16[400,256]{1,0:T(8,128)(2,1)}, bf16[400,256]{1,0:T(8,128)(2,1)S(1)}, u32[]{:S(2)}, u32[]{:S(2)}) collective-permute-start(bf16[400,256]{1,0:T(8,128)(2,1)} %whiten.1.white_ref), channel_id=1, source_target_pairs={{16,0},{17,1},{18,2},{19,3},{20,4},{21,5},{22,6},{23,7},{24,8},{25... | collective-permute-start | bytes 614408 | tf_op jit(solution)/shard_map/ppermute | solution.py:105
  14.4 1.9 %collective-permute-start = (bf16[400,256]{1,0:T(8,128)(2,1)}, bf16[400,256]{1,0:T(8,128)(2,1)S(1)}, u32[]{:S(2)}, u32[]{:S(2)}) collective-permute-start(bf16[400,256]{1,0:T(8,128)(2,1)} %whiten.1.white_ref), channel_id=1, source_target_pairs={{0,16},{1,17},{2,18},{3,19},{4,20},{5,21},{6,22},{7,23},{8,24},{9,... | collective-permute-start | bytes 614408 | tf_op jit(solution)/shard_map/ppermute | solution.py:105
  16.3 7.8 %collective-permute-start.4 = (bf16[400,256]{1,0:T(8,128)(2,1)}, bf16[400,256]{1,0:T(8,128)(2,1)S(1)}, u32[]{:S(2)}, u32[]{:S(2)}) collective-permute-start(bf16[400,256]{1,0:T(8,128)(2,1)} %whiten.1.white_ref), channel_id=1, source_target_pairs={{0,8},{1,9},{2,10},{3,11},{4,12},{5,13},{6,14},{7,15},{8,0},{9,1},... | collective-permute-start | bytes 614408 | tf_op jit(solution)/shard_map/ppermute | solution.py:105
  24.1 0.0 collective-permute-done.1.refs_1_
  24.1 4.0 %collective-permute-start.3 = (bf16[400,256]{1,0:T(8,128)(2,1)S(1)}, bf16[400,256]{1,0:T(8,128)(2,1)S(1)}, u32[]{:S(2)}, u32[]{:S(2)}) collective-permute-start(bf16[400,256]{1,0:T(8,128)(2,1)S(1)} %collective-permute-done.1.refs_1_), channel_id=1, source_target_pairs={{16,0},{17,1},{18,2},{19,3},{20,4},{21,5},{22,6},{23,7},{24,8},{25... | collective-permute-start | bytes 614408 | tf_op jit(solution)/shard_map/ppermute | solution.py:105
  28.1 0.0 collective-permute-done.refs_0_
  28.1 1.9 %collective-permute-start.2 = (bf16[400,256]{1,0:T(8,128)(2,1)S(1)}, bf16[400,256]{1,0:T(8,128)(2,1)S(1)}, u32[]{:S(2)}, u32[]{:S(2)}) collective-permute-start(bf16[400,256]{1,0:T(8,128)(2,1)S(1)} %collective-permute-done.refs_0_), channel_id=1, source_target_pairs={{0,16},{1,17},{2,18},{3,19},{4,20},{5,21},{6,22},{7,23},{8,24},{9,... | collective-permute-start | bytes 614408 | tf_op jit(solution)/shard_map/ppermute | solution.py:105
  30.1 0.0 copy-start.1
  30.1 0.9 copy-done.1
  31.0 0.0 copy-start.2
  31.0 0.7 copy-done.2
  31.7 0.7 rows.1.refs_4_
  32.4 8.8 %collective-permute-done.4.refs_5_ = bf16[400,256]{1,0:T(8,128)(2,1)S(1)} collective-permute-done((bf16[400,256]{1,0:T(8,128)(2,1)}, bf16[400,256]{1,0:T(8,128)(2,1)S(1)}, u32[]{:S(2)}, u32[]{:S(2)}) %collective-permute-start.4) | collective-permute-done | bytes 204832 | tf_op jit(solution)/shard_map/ppermute | solution.py:105
  41.2 6.0 %collective-permute-done.3.refs_3_ = bf16[400,256]{1,0:T(8,128)(2,1)S(1)} collective-permute-done((bf16[400,256]{1,0:T(8,128)(2,1)S(1)}, bf16[400,256]{1,0:T(8,128)(2,1)S(1)}, u32[]{:S(2)}, u32[]{:S(2)}) %collective-permute-start.3) | collective-permute-done | bytes 204832 | tf_op jit(solution)/shard_map/ppermute | solution.py:105
  47.2 0.0 collective-permute-done.2.refs_2_
  47.2 0.8 choose.2
  48.0 0.0 copy-start
  48.0 1.2 %copy-done = bf16[4,928,256]{2,1,0:T(8,128)(2,1)} copy-done((bf16[4,928,256]{2,1,0:T(8,128)(2,1)}, bf16[4,928,256]{2,1,0:T(8,128)(2,1)S(1)}, u32[]{:S(2)}) %copy-start) | copy-done | bytes 1900568
  49.3 0.0 copy-start.3
  49.3 4.1 %all-to-all-start = ((bf16[4,928,256]{2,1,0:T(8,128)(2,1)}), bf16[4,928,256]{2,1,0:T(8,128)(2,1)S(1)}, u32[]{:S(2)}, u32[]{:S(2)}) async-start(bf16[4,928,256]{2,1,0:T(8,128)(2,1)} %copy-done), calls=%async_computation | async-start | bytes 3801088 | tf_op jit(solution)/shard_map/all_to_all | solution.py:407
  53.4 6.2 %collective-permute-start.6 = (bf16[400,256]{1,0:T(8,128)(2,1)S(1)}, bf16[400,256]{1,0:T(8,128)(2,1)S(1)}, u32[]{:S(2)}, u32[]{:S(2)}) collective-permute-start(bf16[400,256]{1,0:T(8,128)(2,1)S(1)} %collective-permute-done.4.refs_5_), channel_id=1, source_target_pairs={{16,0},{17,1},{18,2},{19,3},{20,4},{21,5},{22,6},{23,7},{24,8},{25... | collective-permute-start | bytes 614408 | tf_op jit(solution)/shard_map/ppermute | solution.py:105
  59.6 1.9 %collective-permute-start.5 = (bf16[400,256]{1,0:T(8,128)(2,1)S(1)}, bf16[400,256]{1,0:T(8,128)(2,1)S(1)}, u32[]{:S(2)}, u32[]{:S(2)}) collective-permute-start(bf16[400,256]{1,0:T(8,128)(2,1)S(1)} %collective-permute-done.4.refs_5_), channel_id=1, source_target_pairs={{0,16},{1,17},{2,18},{3,19},{4,20},{5,21},{6,22},{7,23},{8,24},{9,... | collective-permute-start | bytes 614408 | tf_op jit(solution)/shard_map/ppermute | solution.py:105
  61.6 0.8 collective-permute-done.6.refs_1_
  62.3 5.9 %collective-permute-start.8 = (bf16[400,256]{1,0:T(8,128)(2,1)S(1)}, bf16[400,256]{1,0:T(8,128)(2,1)S(1)}, u32[]{:S(2)}, u32[]{:S(2)}) collective-permute-start(bf16[400,256]{1,0:T(8,128)(2,1)S(1)} %collective-permute-done.6.refs_1_), channel_id=1, source_target_pairs={{16,0},{17,1},{18,2},{19,3},{20,4},{21,5},{22,6},{23,7},{24,8},{25... | collective-permute-start | bytes 614408 | tf_op jit(solution)/shard_map/ppermute | solution.py:105
  68.2 0.0 collective-permute-done.5.refs_0_
  68.3 1.9 %collective-permute-start.7 = (bf16[400,256]{1,0:T(8,128)(2,1)S(1)}, bf16[400,256]{1,0:T(8,128)(2,1)S(1)}, u32[]{:S(2)}, u32[]{:S(2)}) collective-permute-start(bf16[400,256]{1,0:T(8,128)(2,1)S(1)} %collective-permute-done.5.refs_0_), channel_id=1, source_target_pairs={{0,16},{1,17},{2,18},{3,19},{4,20},{5,21},{6,22},{7,23},{8,24},{9,... | collective-permute-start | bytes 614408 | tf_op jit(solution)/shard_map/ppermute | solution.py:105
  70.2 0.7 collective-permute-done.8.refs_3_
  70.9 6.2 %collective-permute-done.7.refs_2_ = bf16[400,256]{1,0:T(8,128)(2,1)S(1)} collective-permute-done((bf16[400,256]{1,0:T(8,128)(2,1)S(1)}, bf16[400,256]{1,0:T(8,128)(2,1)S(1)}, u32[]{:S(2)}, u32[]{:S(2)}) %collective-permute-start.7) | collective-permute-done | bytes 204832 | tf_op jit(solution)/shard_map/ppermute | solution.py:105
  77.2 0.0 copy-done.3
  77.2 0.6 choose.3
  77.8 4.6 %collective-permute-start.11 = (bf16[800,256]{1,0:T(8,128)(2,1)S(1)}, bf16[800,256]{1,0:T(8,128)(2,1)S(1)}, u32[]{:S(2)}, u32[]{:S(2)}) collective-permute-start(bf16[800,256]{1,0:T(8,128)(2,1)S(1)} %bitcast.5), channel_id=1, source_target_pairs={{0,4},{1,5},{2,6},{3,7},{4,0},{5,1},{6,2},{7,3},{8,12},{9,13},{10,... | collective-permute-start | bytes 1228808 | tf_op jit(solution)/shard_map/ppermute | solution.py:105
  82.4 2.8 %collective-permute-start.10 = (bf16[800,256]{1,0:T(8,128)(2,1)S(1)}, bf16[800,256]{1,0:T(8,128)(2,1)S(1)}, u32[]{:S(2)}, u32[]{:S(2)}) collective-permute-start(bf16[800,256]{1,0:T(8,128)(2,1)S(1)} %bitcast.6), channel_id=1, source_target_pairs={{0,6},{1,7},{2,0},{3,1},{4,2},{5,3},{6,4},{7,5},{8,14},{9,15},{10,... | collective-permute-start | bytes 1228808 | tf_op jit(solution)/shard_map/ppermute | solution.py:105
  85.2 2.5 %collective-permute-start.9 = (bf16[800,256]{1,0:T(8,128)(2,1)S(1)}, bf16[800,256]{1,0:T(8,128)(2,1)S(1)}, u32[]{:S(2)}, u32[]{:S(2)}) collective-permute-start(bf16[800,256]{1,0:T(8,128)(2,1)S(1)} %bitcast.7), channel_id=1, source_target_pairs={{0,2},{1,3},{2,4},{3,5},{4,6},{5,7},{6,0},{7,1},{8,10},{9,11},{10,... | collective-permute-start | bytes 1228808 | tf_op jit(solution)/shard_map/ppermute | solution.py:105
  87.7 0.0 all-to-all-done.own_ref.refs_0_
  87.7 4.7 %turn.1 = (bf16[2,2304,1536]{2,1,0:T(8,128)(2,1)S(1)}, bf16[2,32,128]{2,1,0:T(8,128)(2,1)S(1)}) custom-call(bf16[4,928,256]{2,1,0:T(8,128)(2,1)S(1)} %all-to-all-done.own_ref.refs_0_), custom_call_target="tpu_custom_call" | custom-call | flops 21233664 | bytes 14155776 | tf_op jit(solution)/shard_map/turn/pallas_call | solution.py:284
  92.4 6.0 %lags.3.refs_3_ = f32[2304,512]{1,0:T(8,128)S(1)} custom-call(s32[2,32]{1,0:T(2,128)S(1)} %bitcast.12, bf16[2,2304,1536]{2,1,0:T(8,128)(2,1)S(1)} %get-tuple-element.17.turned_ref, bf16[2,32,128]{2,1,0:T(8,128)(2,1)S(1)} %get-tuple-element.18.valid_ref, bf16[4,928,256]{2,1,0:T(8,128)(2,1)S(1)} %all-to-all-done.own_ref.refs_0_, bf16[800,256]{1,0:T(8,128)(2,1)S(1)} %bitcast.8), custom_call_target="tpu_custom_call" | custom-call | flops 1811939328 | bytes 4718592 | tf_op jit(solution)/shard_map/lags/pallas_call | solution.py:352
  98.4 0.0 collective-permute-done.11.refs_2_
  98.4 0.0 collective-permute-done.10.refs_1_
  98.4 1.6 %collective-permute-done.9.refs_0_ = bf16[800,256]{1,0:T(8,128)(2,1)S(1)} collective-permute-done((bf16[800,256]{1,0:T(8,128)(2,1)S(1)}, bf16[800,256]{1,0:T(8,128)(2,1)S(1)}, u32[]{:S(2)}, u32[]{:S(2)}) %collective-permute-start.9) | collective-permute-done | bytes 409632 | tf_op jit(solution)/shard_map/ppermute | solution.py:105
  100.0 2.3 %lags.5 = bf16[1152,512]{1,0:T(8,128)(2,1)S(1)} custom-call(s32[2,32]{1,0:T(2,128)S(1)} %bitcast.13, bf16[2,2304,1536]{2,1,0:T(8,128)(2,1)S(1)} %get-tuple-element.17.turned_ref, bf16[2,32,128]{2,1,0:T(8,128)(2,1)S(1)} %get-tuple-element.18.valid_ref, bf16[800,256]{1,0:T(8,128)(2,1)S(1)} %collective-permute-done.9.refs_0_, ...), custom_call_target="tpu_custom_call" | custom-call | flops 1358954496 | bytes 2359296 | tf_op jit(solution)/shard_map/lags/pallas_call | solution.py:352
  102.3 6.9 %collective-permute-start.12 = (bf16[1152,512]{1,0:T(8,128)(2,1)S(1)}, bf16[1152,512]{1,0:T(8,128)(2,1)S(1)}, u32[]{:S(2)}, u32[]{:S(2)}) collective-permute-start(bf16[1152,512]{1,0:T(8,128)(2,1)S(1)} %lags.5), channel_id=1, source_target_pairs={{0,1},{1,0},{2,3},{3,2},{4,5},{5,4},{6,7},{7,6},{8,9},{9,8},{10,11... | collective-permute-start | bytes 3538952 | tf_op jit(solution)/shard_map/ppermute | solution.py:105
  109.2 2.3 %lags.4.mine_ref = f32[1152,512]{1,0:T(8,128)S(1)} custom-call(s32[2,32]{1,0:T(2,128)S(1)} %bitcast.14, bf16[2,2304,1536]{2,1,0:T(8,128)(2,1)S(1)} %get-tuple-element.17.turned_ref, bf16[2,32,128]{2,1,0:T(8,128)(2,1)S(1)} %get-tuple-element.18.valid_ref, bf16[800,256]{1,0:T(8,128)(2,1)S(1)} %collective-permute-done.9.refs_0_, ...), custom_call_target="tpu_custom_call" | custom-call | flops 1358954496 | bytes 2359296 | tf_op jit(solution)/shard_map/lags/pallas_call | solution.py:352
  111.5 0.2 collective-permute-done.12.theirs_ref
  111.7 1.6 %combine.1 = f32[16,65,2,256]{3,2,1,0:T(2,128)} custom-call(f32[1152,512]{1,0:T(8,128)S(1)} %lags.4.mine_ref, bf16[1152,512]{1,0:T(8,128)(2,1)S(1)} %collective-permute-done.12.theirs_ref), custom_call_target="tpu_custom_call" | custom-call | tf_op jit(solution)/shard_map/combine/pallas_call | solution.py:387
Async XLA Ops:
  3.3 20.7 %collective-permute-start.1 = (bf16[400,256]{1,0:T(8,128)(2,1)}, bf16[400,256]{1,0:T(8,128)(2,1)S(1)}, u32[]{:S(2)}, u32[]{:S(2)}) collective-permute-start(bf16[400,256]{1,0:T(8,128)(2,1)} %whiten.1.white_ref), channel_id=1, source_target_pairs={{16,0},{17,1},{18,2},{19,3},{20,4},{21,5},{22,6},{23,7},{24,8},{25... | collective-permute-start | bytes 614408 | tf_op jit(solution)/shard_map/ppermute | solution.py:105
  14.4 13.8 %collective-permute-start = (bf16[400,256]{1,0:T(8,128)(2,1)}, bf16[400,256]{1,0:T(8,128)(2,1)S(1)}, u32[]{:S(2)}, u32[]{:S(2)}) collective-permute-start(bf16[400,256]{1,0:T(8,128)(2,1)} %whiten.1.white_ref), channel_id=1, source_target_pairs={{0,16},{1,17},{2,18},{3,19},{4,20},{5,21},{6,22},{7,23},{8,24},{9,... | collective-permute-start | bytes 614408 | tf_op jit(solution)/shard_map/ppermute | solution.py:105
  16.3 24.9 %collective-permute-start.4 = (bf16[400,256]{1,0:T(8,128)(2,1)}, bf16[400,256]{1,0:T(8,128)(2,1)S(1)}, u32[]{:S(2)}, u32[]{:S(2)}) collective-permute-start(bf16[400,256]{1,0:T(8,128)(2,1)} %whiten.1.white_ref), channel_id=1, source_target_pairs={{0,8},{1,9},{2,10},{3,11},{4,12},{5,13},{6,14},{7,15},{8,0},{9,1},... | collective-permute-start | bytes 614408 | tf_op jit(solution)/shard_map/ppermute | solution.py:105
  24.1 23.1 %collective-permute-start.3 = (bf16[400,256]{1,0:T(8,128)(2,1)S(1)}, bf16[400,256]{1,0:T(8,128)(2,1)S(1)}, u32[]{:S(2)}, u32[]{:S(2)}) collective-permute-start(bf16[400,256]{1,0:T(8,128)(2,1)S(1)} %collective-permute-done.1.refs_1_), channel_id=1, source_target_pairs={{16,0},{17,1},{18,2},{19,3},{20,4},{21,5},{22,6},{23,7},{24,8},{25... | collective-permute-start | bytes 614408 | tf_op jit(solution)/shard_map/ppermute | solution.py:105
  28.1 19.0 %collective-permute-start.2 = (bf16[400,256]{1,0:T(8,128)(2,1)S(1)}, bf16[400,256]{1,0:T(8,128)(2,1)S(1)}, u32[]{:S(2)}, u32[]{:S(2)}) collective-permute-start(bf16[400,256]{1,0:T(8,128)(2,1)S(1)} %collective-permute-done.refs_0_), channel_id=1, source_target_pairs={{0,16},{1,17},{2,18},{3,19},{4,20},{5,21},{6,22},{7,23},{8,24},{9,... | collective-permute-start | bytes 614408 | tf_op jit(solution)/shard_map/ppermute | solution.py:105
  30.1 0.9 copy-start.1
  31.0 0.7 copy-start.2
  48.0 1.3 %copy-start = (bf16[4,928,256]{2,1,0:T(8,128)(2,1)}, bf16[4,928,256]{2,1,0:T(8,128)(2,1)S(1)}, u32[]{:S(2)}) copy-start(bf16[4,928,256]{2,1,0:T(8,128)(2,1)S(1)} %choose.2) | copy-start | bytes 5701636
  49.3 27.9 %copy-start.3 = (s32[32,2]{0,1:T(2,128)S(1)}, s32[32,2]{0,1:T(2,128)}, u32[]{:S(2)}) copy-start(s32[32,2]{0,1:T(2,128)} %param.7) | copy-start | bytes 772
  49.3 38.4 %all-to-all-start = ((bf16[4,928,256]{2,1,0:T(8,128)(2,1)}), bf16[4,928,256]{2,1,0:T(8,128)(2,1)S(1)}, u32[]{:S(2)}, u32[]{:S(2)}) async-start(bf16[4,928,256]{2,1,0:T(8,128)(2,1)} %copy-done), calls=%async_computation | async-start | bytes 3801088 | tf_op jit(solution)/shard_map/all_to_all | solution.py:407
  53.4 8.9 %collective-permute-start.6 = (bf16[400,256]{1,0:T(8,128)(2,1)S(1)}, bf16[400,256]{1,0:T(8,128)(2,1)S(1)}, u32[]{:S(2)}, u32[]{:S(2)}) collective-permute-start(bf16[400,256]{1,0:T(8,128)(2,1)S(1)} %collective-permute-done.4.refs_5_), channel_id=1, source_target_pairs={{16,0},{17,1},{18,2},{19,3},{20,4},{21,5},{22,6},{23,7},{24,8},{25... | collective-permute-start | bytes 614408 | tf_op jit(solution)/shard_map/ppermute | solution.py:105
  59.6 8.6 %collective-permute-start.5 = (bf16[400,256]{1,0:T(8,128)(2,1)S(1)}, bf16[400,256]{1,0:T(8,128)(2,1)S(1)}, u32[]{:S(2)}, u32[]{:S(2)}) collective-permute-start(bf16[400,256]{1,0:T(8,128)(2,1)S(1)} %collective-permute-done.4.refs_5_), channel_id=1, source_target_pairs={{0,16},{1,17},{2,18},{3,19},{4,20},{5,21},{6,22},{7,23},{8,24},{9,... | collective-permute-start | bytes 614408 | tf_op jit(solution)/shard_map/ppermute | solution.py:105
  62.3 8.6 %collective-permute-start.8 = (bf16[400,256]{1,0:T(8,128)(2,1)S(1)}, bf16[400,256]{1,0:T(8,128)(2,1)S(1)}, u32[]{:S(2)}, u32[]{:S(2)}) collective-permute-start(bf16[400,256]{1,0:T(8,128)(2,1)S(1)} %collective-permute-done.6.refs_1_), channel_id=1, source_target_pairs={{16,0},{17,1},{18,2},{19,3},{20,4},{21,5},{22,6},{23,7},{24,8},{25... | collective-permute-start | bytes 614408 | tf_op jit(solution)/shard_map/ppermute | solution.py:105
  68.3 8.9 %collective-permute-start.7 = (bf16[400,256]{1,0:T(8,128)(2,1)S(1)}, bf16[400,256]{1,0:T(8,128)(2,1)S(1)}, u32[]{:S(2)}, u32[]{:S(2)}) collective-permute-start(bf16[400,256]{1,0:T(8,128)(2,1)S(1)} %collective-permute-done.5.refs_0_), channel_id=1, source_target_pairs={{0,16},{1,17},{2,18},{3,19},{4,20},{5,21},{6,22},{7,23},{8,24},{9,... | collective-permute-start | bytes 614408 | tf_op jit(solution)/shard_map/ppermute | solution.py:105
  77.8 20.6 %collective-permute-start.11 = (bf16[800,256]{1,0:T(8,128)(2,1)S(1)}, bf16[800,256]{1,0:T(8,128)(2,1)S(1)}, u32[]{:S(2)}, u32[]{:S(2)}) collective-permute-start(bf16[800,256]{1,0:T(8,128)(2,1)S(1)} %bitcast.5), channel_id=1, source_target_pairs={{0,4},{1,5},{2,6},{3,7},{4,0},{5,1},{6,2},{7,3},{8,12},{9,13},{10,... | collective-permute-start | bytes 1228808 | tf_op jit(solution)/shard_map/ppermute | solution.py:105
  82.4 16.0 %collective-permute-start.10 = (bf16[800,256]{1,0:T(8,128)(2,1)S(1)}, bf16[800,256]{1,0:T(8,128)(2,1)S(1)}, u32[]{:S(2)}, u32[]{:S(2)}) collective-permute-start(bf16[800,256]{1,0:T(8,128)(2,1)S(1)} %bitcast.6), channel_id=1, source_target_pairs={{0,6},{1,7},{2,0},{3,1},{4,2},{5,3},{6,4},{7,5},{8,14},{9,15},{10,... | collective-permute-start | bytes 1228808 | tf_op jit(solution)/shard_map/ppermute | solution.py:105
  85.2 14.8 %collective-permute-start.9 = (bf16[800,256]{1,0:T(8,128)(2,1)S(1)}, bf16[800,256]{1,0:T(8,128)(2,1)S(1)}, u32[]{:S(2)}, u32[]{:S(2)}) collective-permute-start(bf16[800,256]{1,0:T(8,128)(2,1)S(1)} %bitcast.7), channel_id=1, source_target_pairs={{0,2},{1,3},{2,4},{3,5},{4,6},{5,7},{6,0},{7,1},{8,10},{9,11},{10,... | collective-permute-start | bytes 1228808 | tf_op jit(solution)/shard_map/ppermute | solution.py:105
  102.3 9.4 %collective-permute-start.12 = (bf16[1152,512]{1,0:T(8,128)(2,1)S(1)}, bf16[1152,512]{1,0:T(8,128)(2,1)S(1)}, u32[]{:S(2)}, u32[]{:S(2)}) collective-permute-start(bf16[1152,512]{1,0:T(8,128)(2,1)S(1)} %lags.5), channel_id=1, source_target_pairs={{0,1},{1,0},{2,3},{3,2},{4,5},{5,4},{6,7},{7,6},{8,9},{9,8},{10,11... | collective-permute-start | bytes 3538952 | tf_op jit(solution)/shard_map/ppermute | solution.py:105

commit v6 on v4

--- a/solution.py
+++ b/solution.py
@@ -168,6 +168,11 @@
     )(records.T, validity.T, band_average(), window_tables(win_dev))
 
 
+def first_rows_kernel(partners_ref, white_ref, out_ref):
+    del partners_ref
+    rows_kernel(white_ref, out_ref)
+
+
 def rows_kernel(white_ref, out_ref, half=0):
     lanes = pl.ds(pl.multiple_of(place()[0] * 128, 128), 128)
     blocks = [white_ref[g * COLS : (g + 1) * COLS, lanes].astype(jnp.float32) for g in range(WHITE // COLS)]
@@ -190,7 +195,7 @@
     return pl.pallas_call(
         kernel,
         out_shape=jax.ShapeDtypeStruct((CHIPS, height, STA), jnp.bfloat16),
-        in_specs=[VMEM] * len(args),
+        in_specs=[SMEM if arg.dtype == jnp.int32 else VMEM for arg in args],
         out_specs=VMEM,
         compiler_params=pltpu.CompilerParams(vmem_limit_bytes=4 * MIB),
         name="rows",
@@ -239,7 +244,15 @@
 
 def turn_kernel(own_ref, out_ref, mask_ref, held):
     _, chip, core = place()
-    cosine, sine = lag_tables()
+    cosine, sine = (jnp.concatenate([table, table], axis=0).astype(jnp.bfloat16) for table in lag_tables())
+    upper = lax.broadcasted_iota(jnp.int32, (16, COLS), 0) < 8
+
+    def two(rows, k):
+        first, second = (jnp.broadcast_to(rows[m : m + 1], (16, COLS)) for m in (k, k + 1))
+        both = jnp.where(upper, first, second).astype(jnp.bfloat16)
+        first, second = first.astype(jnp.bfloat16), second.astype(jnp.bfloat16)
+        return jnp.concatenate([first] * (LPAD // 16) + [both] + [second] * (LPAD // 16), axis=0)
+
     for half in range(2):
         for d, by in enumerate(TURNS):
             source = lax.rem(chip + CHIPS - by, CHIPS)
@@ -262,9 +275,8 @@
                     swapped = pltpu.roll(block, BINS, 1)
                     lanes = slice(d * WHITE + g * COLS, d * WHITE + (g + 1) * COLS)
                     for k in range(0, 8, 2):
-                        turned = [block[m : m + 1] * cosine + swapped[m : m + 1] * sine for m in (k, k + 1)]
                         at = pl.multiple_of(i * 8 * LPAD + k * LPAD, 2 * LPAD)
-                        out_ref[half, pl.ds(at, 2 * LPAD), lanes] = jnp.concatenate(turned, axis=0).astype(jnp.bfloat16)
+                        out_ref[half, pl.ds(at, 2 * LPAD), lanes] = two(block, k) * cosine + two(swapped, k) * sine
             return carry
 
         lax.fori_loop(0, CHIP_ROWS // 8, eight, 0)
@@ -391,7 +403,7 @@
 
     white = whitened(records, validity)
     other = send(white, to_other_half)
-    rows = by_rows(rows_kernel, OWN // 2, white)
+    rows = by_rows(first_rows_kernel, OWN // 2, partners, white)
     rows, other = lax.optimization_barrier((rows, other))
     far, other_far = spread(chosen(partners, neighbours(white))), spread(chosen(partners, neighbours(other)))
     own = by_rows(own_kernel, OWN, rows, other)

time: 113 us -> 112 us (level)
  the two profiles are of different devices: /device:TPU:11 before, /device:TPU:9 now
where the time goes in v6:
time: 112 us
  starting transfers between devices  73.1 us (65%)
  Pallas kernels  21.5 us (19%)
  waiting for transfers between devices  15.2 us (14%)
  local copies, waits for them, and re-layouts  1.61 us (1%)
    ppermute x16, starting transfers between devices, send(): return lax.ppermute(array, AXES, routes(target))  69.7 us
    ppermute x16, waiting for transfers between devices, send(): return lax.ppermute(array, AXES, routes(target))  15.2 us
    pallas_call x3, Pallas kernels, into_lags(): pl.pallas_call(functools.partial(lags_kernel, spans, first, count, acc is...  9.92 us
    pallas_call x1, Pallas kernels, turned_rows(): pl.pallas_call(turn_kernel, out_shape=[jax.ShapeDtypeStruct((2, height, D...  3.74 us
    all_to_all x1, starting transfers between devices, body(): lax.all_to_all(own, 'tm', 0, 0, axis_index_groups=CHIP_GROUPS, tiled=True)  3.41 us
    pallas_call x1, Pallas kernels, whitened(): pl.pallas_call(whiten_kernel, out_shape=jax.ShapeDtypeStruct((SENT, rows)...  3.35 us
  transfers between devices with their start and end apart: 17, of which 3 were waited for; matrix products, arithmetic and copies ran while one was open for 0% of the time, Pallas kernels for 12%

profile of v6, /device:TPU:9, one launch (start us, length us, event | category | flops | bytes accessed | tf_op | source)
XLA Modules:
  0.0 111.7 jit_solution(10616809238003818637)
XLA Ops:
  0.0 3.3 %whiten.1.white_ref = bf16[400,256]{1,0:T(8,128)(2,1)} custom-call(bf16[1800,256]{1,0:T(8,128)(2,1)} %bitcast.10, s32[3,256]{1,0:T(4,128)} %bitcast.11, f32[64,64]{1,0:T(8,128)} %constant.4.clone.avg_hbm, bf16[3,128,616]{2,1,0:T(8,128)(2,1)} %constant.5.clone.table_hbm), custom_call_target="tpu_custom_call" | custom-call | tf_op jit(solution)/shard_map/whiten/pallas_call | solution.py:154
  3.4 11.0 %collective-permute-start.9 = (bf16[400,256]{1,0:T(8,128)(2,1)}, bf16[400,256]{1,0:T(8,128)(2,1)S(1)}, u32[]{:S(2)}, u32[]{:S(2)}) collective-permute-start(bf16[400,256]{1,0:T(8,128)(2,1)} %whiten.1.white_ref), channel_id=1, source_target_pairs={{16,0},{17,1},{18,2},{19,3},{20,4},{21,5},{22,6},{23,7},{24,8},{25... | collective-permute-start | bytes 614408 | tf_op jit(solution)/shard_map/ppermute | solution.py:104
  14.4 1.9 %collective-permute-start.8 = (bf16[400,256]{1,0:T(8,128)(2,1)}, bf16[400,256]{1,0:T(8,128)(2,1)S(1)}, u32[]{:S(2)}, u32[]{:S(2)}) collective-permute-start(bf16[400,256]{1,0:T(8,128)(2,1)} %whiten.1.white_ref), channel_id=1, source_target_pairs={{0,16},{1,17},{2,18},{3,19},{4,20},{5,21},{6,22},{7,23},{8,24},{9,... | collective-permute-start | bytes 614408 | tf_op jit(solution)/shard_map/ppermute | solution.py:104
  16.3 7.8 %collective-permute-start = (bf16[400,256]{1,0:T(8,128)(2,1)}, bf16[400,256]{1,0:T(8,128)(2,1)S(1)}, u32[]{:S(2)}, u32[]{:S(2)}) collective-permute-start(bf16[400,256]{1,0:T(8,128)(2,1)} %whiten.1.white_ref), channel_id=1, source_target_pairs={{0,8},{1,9},{2,10},{3,11},{4,12},{5,13},{6,14},{7,15},{8,0},{9,1},... | collective-permute-start | bytes 614408 | tf_op jit(solution)/shard_map/ppermute | solution.py:104
  24.1 0.0 collective-permute-done.9.refs_1_
  24.1 4.0 %collective-permute-start.11 = (bf16[400,256]{1,0:T(8,128)(2,1)S(1)}, bf16[400,256]{1,0:T(8,128)(2,1)S(1)}, u32[]{:S(2)}, u32[]{:S(2)}) collective-permute-start(bf16[400,256]{1,0:T(8,128)(2,1)S(1)} %collective-permute-done.9.refs_1_), channel_id=1, source_target_pairs={{16,0},{17,1},{18,2},{19,3},{20,4},{21,5},{22,6},{23,7},{24,8},{25... | collective-permute-start | bytes 614408 | tf_op jit(solution)/shard_map/ppermute | solution.py:104
  28.2 0.0 collective-permute-done.8.refs_0_
  28.2 1.9 %collective-permute-start.10 = (bf16[400,256]{1,0:T(8,128)(2,1)S(1)}, bf16[400,256]{1,0:T(8,128)(2,1)S(1)}, u32[]{:S(2)}, u32[]{:S(2)}) collective-permute-start(bf16[400,256]{1,0:T(8,128)(2,1)S(1)} %collective-permute-done.8.refs_0_), channel_id=1, source_target_pairs={{0,16},{1,17},{2,18},{3,19},{4,20},{5,21},{6,22},{7,23},{8,24},{9,... | collective-permute-start | bytes 614408 | tf_op jit(solution)/shard_map/ppermute | solution.py:104
  30.1 0.0 copy-start
  30.1 0.9 copy-done
  31.0 0.7 copy-done.1
  31.7 0.7 rows.2.first_ref
  32.4 8.8 %collective-permute-done.other_ref = bf16[400,256]{1,0:T(8,128)(2,1)S(1)} collective-permute-done((bf16[400,256]{1,0:T(8,128)(2,1)}, bf16[400,256]{1,0:T(8,128)(2,1)S(1)}, u32[]{:S(2)}, u32[]{:S(2)}) %collective-permute-start) | collective-permute-done | bytes 204832 | tf_op jit(solution)/shard_map/ppermute | solution.py:104
  41.2 6.5 %collective-permute-start.2 = (bf16[400,256]{1,0:T(8,128)(2,1)S(1)}, bf16[400,256]{1,0:T(8,128)(2,1)S(1)}, u32[]{:S(2)}, u32[]{:S(2)}) collective-permute-start(bf16[400,256]{1,0:T(8,128)(2,1)S(1)} %collective-permute-done.other_ref), channel_id=1, source_target_pairs={{16,0},{17,1},{18,2},{19,3},{20,4},{21,5},{22,6},{23,7},{24,8},{25... | collective-permute-start | bytes 614408 | tf_op jit(solution)/shard_map/ppermute | solution.py:104
  47.7 1.9 %collective-permute-start.1 = (bf16[400,256]{1,0:T(8,128)(2,1)S(1)}, bf16[400,256]{1,0:T(8,128)(2,1)S(1)}, u32[]{:S(2)}, u32[]{:S(2)}) collective-permute-start(bf16[400,256]{1,0:T(8,128)(2,1)S(1)} %collective-permute-done.other_ref), channel_id=1, source_target_pairs={{0,16},{1,17},{2,18},{3,19},{4,20},{5,21},{6,22},{7,23},{8,24},{9,... | collective-permute-start | bytes 614408 | tf_op jit(solution)/shard_map/ppermute | solution.py:104
  49.6 0.0 collective-permute-done.11.refs_3_
  49.7 0.0 collective-permute-done.10.refs_2_
  49.7 0.6 choose.3.refs_0_
  50.3 4.6 %collective-permute-start.14 = (bf16[800,256]{1,0:T(8,128)(2,1)S(1)}, bf16[800,256]{1,0:T(8,128)(2,1)S(1)}, u32[]{:S(2)}, u32[]{:S(2)}) collective-permute-start(bf16[800,256]{1,0:T(8,128)(2,1)S(1)} %choose.3.refs_0_), channel_id=1, source_target_pairs={{0,4},{1,5},{2,6},{3,7},{4,0},{5,1},{6,2},{7,3},{8,12},{9,13},{10,... | collective-permute-start | bytes 1228808 | tf_op jit(solution)/shard_map/ppermute | solution.py:104
  55.0 2.8 %collective-permute-start.13 = (bf16[800,256]{1,0:T(8,128)(2,1)S(1)}, bf16[800,256]{1,0:T(8,128)(2,1)S(1)}, u32[]{:S(2)}, u32[]{:S(2)}) collective-permute-start(bf16[800,256]{1,0:T(8,128)(2,1)S(1)} %choose.3.refs_0_), channel_id=1, source_target_pairs={{0,6},{1,7},{2,0},{3,1},{4,2},{5,3},{6,4},{7,5},{8,14},{9,15},{10,... | collective-permute-start | bytes 1228808 | tf_op jit(solution)/shard_map/ppermute | solution.py:104
  57.7 2.5 %collective-permute-start.12 = (bf16[800,256]{1,0:T(8,128)(2,1)S(1)}, bf16[800,256]{1,0:T(8,128)(2,1)S(1)}, u32[]{:S(2)}, u32[]{:S(2)}) collective-permute-start(bf16[800,256]{1,0:T(8,128)(2,1)S(1)} %choose.3.refs_0_), channel_id=1, source_target_pairs={{0,2},{1,3},{2,4},{3,5},{4,6},{5,7},{6,0},{7,1},{8,10},{9,11},{10,... | collective-permute-start | bytes 1228808 | tf_op jit(solution)/shard_map/ppermute | solution.py:104
  60.3 0.0 collective-permute-done.2.refs_1_
  60.3 5.5 %collective-permute-start.4 = (bf16[400,256]{1,0:T(8,128)(2,1)S(1)}, bf16[400,256]{1,0:T(8,128)(2,1)S(1)}, u32[]{:S(2)}, u32[]{:S(2)}) collective-permute-start(bf16[400,256]{1,0:T(8,128)(2,1)S(1)} %collective-permute-done.2.refs_1_), channel_id=1, source_target_pairs={{16,0},{17,1},{18,2},{19,3},{20,4},{21,5},{22,6},{23,7},{24,8},{25... | collective-permute-start | bytes 614408 | tf_op jit(solution)/shard_map/ppermute | solution.py:104
  65.7 0.0 collective-permute-done.1.refs_0_
  65.8 1.9 %collective-permute-start.3 = (bf16[400,256]{1,0:T(8,128)(2,1)S(1)}, bf16[400,256]{1,0:T(8,128)(2,1)S(1)}, u32[]{:S(2)}, u32[]{:S(2)}) collective-permute-start(bf16[400,256]{1,0:T(8,128)(2,1)S(1)} %collective-permute-done.1.refs_0_), channel_id=1, source_target_pairs={{0,16},{1,17},{2,18},{3,19},{4,20},{5,21},{6,22},{7,23},{8,24},{9,... | collective-permute-start | bytes 614408 | tf_op jit(solution)/shard_map/ppermute | solution.py:104
  67.7 0.9 rows.3
  68.5 3.4 %all-to-all-start = ((bf16[4,128,256]{2,1,0:T(8,128)(2,1)}), bf16[4,128,256]{2,1,0:T(8,128)(2,1)S(1)}, u32[]{:S(2)}, u32[]{:S(2)}) async-start(bf16[4,128,256]{2,1,0:T(8,128)(2,1)} %rows.3), calls=%async_computation | async-start | bytes 524288 | tf_op jit(solution)/shard_map/all_to_all | solution.py:410
  72.0 0.0 collective-permute-done.4.refs_3_
  72.0 2.4 %collective-permute-done.3.refs_2_ = bf16[400,256]{1,0:T(8,128)(2,1)S(1)} collective-permute-done((bf16[400,256]{1,0:T(8,128)(2,1)S(1)}, bf16[400,256]{1,0:T(8,128)(2,1)S(1)}, u32[]{:S(2)}, u32[]{:S(2)}) %collective-permute-start.3) | collective-permute-done | bytes 204832 | tf_op jit(solution)/shard_map/ppermute | solution.py:104
  74.4 0.0 copy-done.2
  74.4 0.6 choose.2.refs_0_
  75.0 2.6 %collective-permute-start.7 = (bf16[800,256]{1,0:T(8,128)(2,1)S(1)}, bf16[800,256]{1,0:T(8,128)(2,1)S(1)}, u32[]{:S(2)}, u32[]{:S(2)}) collective-permute-start(bf16[800,256]{1,0:T(8,128)(2,1)S(1)} %choose.2.refs_0_), channel_id=1, source_target_pairs={{0,4},{1,5},{2,6},{3,7},{4,0},{5,1},{6,2},{7,3},{8,12},{9,13},{10,... | collective-permute-start | bytes 1228808 | tf_op jit(solution)/shard_map/ppermute | solution.py:104
  77.6 4.0 %collective-permute-start.6 = (bf16[800,256]{1,0:T(8,128)(2,1)S(1)}, bf16[800,256]{1,0:T(8,128)(2,1)S(1)}, u32[]{:S(2)}, u32[]{:S(2)}) collective-permute-start(bf16[800,256]{1,0:T(8,128)(2,1)S(1)} %choose.2.refs_0_), channel_id=1, source_target_pairs={{0,6},{1,7},{2,0},{3,1},{4,2},{5,3},{6,4},{7,5},{8,14},{9,15},{10,... | collective-permute-start | bytes 1228808 | tf_op jit(solution)/shard_map/ppermute | solution.py:104
  81.6 0.0 collective-permute-done.14.refs_3_
  81.6 1.9 %collective-permute-start.5 = (bf16[800,256]{1,0:T(8,128)(2,1)S(1)}, bf16[800,256]{1,0:T(8,128)(2,1)S(1)}, u32[]{:S(2)}, u32[]{:S(2)}) collective-permute-start(bf16[800,256]{1,0:T(8,128)(2,1)S(1)} %choose.2.refs_0_), channel_id=1, source_target_pairs={{0,2},{1,3},{2,4},{3,5},{4,6},{5,7},{6,0},{7,1},{8,10},{9,11},{10,... | collective-permute-start | bytes 1228808 | tf_op jit(solution)/shard_map/ppermute | solution.py:104
  83.5 0.0 all-to-all-done.own_ref
  83.5 3.7 %turn.1 = (bf16[2,2304,1536]{2,1,0:T(8,128)(2,1)S(1)}, bf16[2,32,128]{2,1,0:T(8,128)(2,1)S(1)}) custom-call(bf16[4,128,256]{2,1,0:T(8,128)(2,1)S(1)} %all-to-all-done.own_ref), custom_call_target="tpu_custom_call" | custom-call | flops 21233664 | bytes 14155776 | tf_op jit(solution)/shard_map/turn/pallas_call | solution.py:287
  87.3 0.0 collective-permute-done.13.refs_2_
  87.3 0.0 collective-permute-done.12.refs_1_
  87.3 4.8 %lags.3.refs_4_ = f32[2304,512]{1,0:T(8,128)S(1)} custom-call(s32[2,32]{1,0:T(2,128)S(1)} %bitcast.7, bf16[2,2304,1536]{2,1,0:T(8,128)(2,1)S(1)} %get-tuple-element.11.turned_ref, bf16[2,32,128]{2,1,0:T(8,128)(2,1)S(1)} %get-tuple-element.12.valid_ref, bf16[800,256]{1,0:T(8,128)(2,1)S(1)} %choose.3.refs_0_, ...), custom_call_target="tpu_custom_call" | custom-call | flops 3623878656 | bytes 4718592 | tf_op jit(solution)/shard_map/lags/pallas_call | solution.py:347
  92.0 0.0 collective-permute-done.7.refs_3_
  92.0 0.0 collective-permute-done.6.refs_2_
  92.1 4.0 %collective-permute-done.5.refs_1_ = bf16[800,256]{1,0:T(8,128)(2,1)S(1)} collective-permute-done((bf16[800,256]{1,0:T(8,128)(2,1)S(1)}, bf16[800,256]{1,0:T(8,128)(2,1)S(1)}, u32[]{:S(2)}, u32[]{:S(2)}) %collective-permute-start.5) | collective-permute-done | bytes 409632 | tf_op jit(solution)/shard_map/ppermute | solution.py:104
  96.0 2.6 %lags.5 = bf16[1152,512]{1,0:T(8,128)(2,1)S(1)} custom-call(s32[2,32]{1,0:T(2,128)S(1)} %bitcast.8, bf16[2,2304,1536]{2,1,0:T(8,128)(2,1)S(1)} %get-tuple-element.11.turned_ref, bf16[2,32,128]{2,1,0:T(8,128)(2,1)S(1)} %get-tuple-element.12.valid_ref, bf16[800,256]{1,0:T(8,128)(2,1)S(1)} %choose.2.refs_0_, ...), custom_call_target="tpu_custom_call" | custom-call | flops 1811939328 | bytes 2359296 | tf_op jit(solution)/shard_map/lags/pallas_call | solution.py:347
  98.6 8.8 %collective-permute-start.15 = (bf16[1152,512]{1,0:T(8,128)(2,1)S(1)}, bf16[1152,512]{1,0:T(8,128)(2,1)S(1)}, u32[]{:S(2)}, u32[]{:S(2)}) collective-permute-start(bf16[1152,512]{1,0:T(8,128)(2,1)S(1)} %lags.5), channel_id=1, source_target_pairs={{0,1},{1,0},{2,3},{3,2},{4,5},{5,4},{6,7},{7,6},{8,9},{9,8},{10,11... | collective-permute-start | bytes 3538952 | tf_op jit(solution)/shard_map/ppermute | solution.py:104
  107.4 2.6 %lags.4.mine_ref = f32[1152,512]{1,0:T(8,128)S(1)} custom-call(s32[2,32]{1,0:T(2,128)S(1)} %bitcast.9, bf16[2,2304,1536]{2,1,0:T(8,128)(2,1)S(1)} %get-tuple-element.11.turned_ref, bf16[2,32,128]{2,1,0:T(8,128)(2,1)S(1)} %get-tuple-element.12.valid_ref, bf16[800,256]{1,0:T(8,128)(2,1)S(1)} %choose.2.refs_0_, ...), custom_call_target="tpu_custom_call" | custom-call | flops 1811939328 | bytes 2359296 | tf_op jit(solution)/shard_map/lags/pallas_call | solution.py:347
  110.0 0.0 collective-permute-done.15.theirs_ref
  110.0 1.6 %combine.1 = f32[16,65,2,256]{3,2,1,0:T(2,128)} custom-call(f32[1152,512]{1,0:T(8,128)S(1)} %lags.4.mine_ref, bf16[1152,512]{1,0:T(8,128)(2,1)S(1)} %collective-permute-done.15.theirs_ref), custom_call_target="tpu_custom_call" | custom-call | tf_op jit(solution)/shard_map/combine/pallas_call | solution.py:382
  (2 shorter events, 0.0 us)
Async XLA Ops:
  0.0 74.4 %copy-start.2 = (s32[32,2]{0,1:T(2,128)S(1)}, s32[32,2]{0,1:T(2,128)}, u32[]{:S(2)}) copy-start(s32[32,2]{0,1:T(2,128)} %param.7) | copy-start | bytes 772
  3.4 20.8 %collective-permute-start.9 = (bf16[400,256]{1,0:T(8,128)(2,1)}, bf16[400,256]{1,0:T(8,128)(2,1)S(1)}, u32[]{:S(2)}, u32[]{:S(2)}) collective-permute-start(bf16[400,256]{1,0:T(8,128)(2,1)} %whiten.1.white_ref), channel_id=1, source_target_pairs={{16,0},{17,1},{18,2},{19,3},{20,4},{21,5},{22,6},{23,7},{24,8},{25... | collective-permute-start | bytes 614408 | tf_op jit(solution)/shard_map/ppermute | solution.py:104
  14.4 13.8 %collective-permute-start.8 = (bf16[400,256]{1,0:T(8,128)(2,1)}, bf16[400,256]{1,0:T(8,128)(2,1)S(1)}, u32[]{:S(2)}, u32[]{:S(2)}) collective-permute-start(bf16[400,256]{1,0:T(8,128)(2,1)} %whiten.1.white_ref), channel_id=1, source_target_pairs={{0,16},{1,17},{2,18},{3,19},{4,20},{5,21},{6,22},{7,23},{8,24},{9,... | collective-permute-start | bytes 614408 | tf_op jit(solution)/shard_map/ppermute | solution.py:104
  16.3 24.9 %collective-permute-start = (bf16[400,256]{1,0:T(8,128)(2,1)}, bf16[400,256]{1,0:T(8,128)(2,1)S(1)}, u32[]{:S(2)}, u32[]{:S(2)}) collective-permute-start(bf16[400,256]{1,0:T(8,128)(2,1)} %whiten.1.white_ref), channel_id=1, source_target_pairs={{0,8},{1,9},{2,10},{3,11},{4,12},{5,13},{6,14},{7,15},{8,0},{9,1},... | collective-permute-start | bytes 614408 | tf_op jit(solution)/shard_map/ppermute | solution.py:104
  24.1 25.5 %collective-permute-start.11 = (bf16[400,256]{1,0:T(8,128)(2,1)S(1)}, bf16[400,256]{1,0:T(8,128)(2,1)S(1)}, u32[]{:S(2)}, u32[]{:S(2)}) collective-permute-start(bf16[400,256]{1,0:T(8,128)(2,1)S(1)} %collective-permute-done.9.refs_1_), channel_id=1, source_target_pairs={{16,0},{17,1},{18,2},{19,3},{20,4},{21,5},{22,6},{23,7},{24,8},{25... | collective-permute-start | bytes 614408 | tf_op jit(solution)/shard_map/ppermute | solution.py:104
  28.2 21.5 %collective-permute-start.10 = (bf16[400,256]{1,0:T(8,128)(2,1)S(1)}, bf16[400,256]{1,0:T(8,128)(2,1)S(1)}, u32[]{:S(2)}, u32[]{:S(2)}) collective-permute-start(bf16[400,256]{1,0:T(8,128)(2,1)S(1)} %collective-permute-done.8.refs_0_), channel_id=1, source_target_pairs={{0,16},{1,17},{2,18},{3,19},{4,20},{5,21},{6,22},{7,23},{8,24},{9,... | collective-permute-start | bytes 614408 | tf_op jit(solution)/shard_map/ppermute | solution.py:104
  30.1 0.9 copy-start
  31.0 0.7 copy-start.1
  41.2 19.1 %collective-permute-start.2 = (bf16[400,256]{1,0:T(8,128)(2,1)S(1)}, bf16[400,256]{1,0:T(8,128)(2,1)S(1)}, u32[]{:S(2)}, u32[]{:S(2)}) collective-permute-start(bf16[400,256]{1,0:T(8,128)(2,1)S(1)} %collective-permute-done.other_ref), channel_id=1, source_target_pairs={{16,0},{17,1},{18,2},{19,3},{20,4},{21,5},{22,6},{23,7},{24,8},{25... | collective-permute-start | bytes 614408 | tf_op jit(solution)/shard_map/ppermute | solution.py:104
  47.7 18.0 %collective-permute-start.1 = (bf16[400,256]{1,0:T(8,128)(2,1)S(1)}, bf16[400,256]{1,0:T(8,128)(2,1)S(1)}, u32[]{:S(2)}, u32[]{:S(2)}) collective-permute-start(bf16[400,256]{1,0:T(8,128)(2,1)S(1)} %collective-permute-done.other_ref), channel_id=1, source_target_pairs={{0,16},{1,17},{2,18},{3,19},{4,20},{5,21},{6,22},{7,23},{8,24},{9,... | collective-permute-start | bytes 614408 | tf_op jit(solution)/shard_map/ppermute | solution.py:104
  50.3 31.2 %collective-permute-start.14 = (bf16[800,256]{1,0:T(8,128)(2,1)S(1)}, bf16[800,256]{1,0:T(8,128)(2,1)S(1)}, u32[]{:S(2)}, u32[]{:S(2)}) collective-permute-start(bf16[800,256]{1,0:T(8,128)(2,1)S(1)} %choose.3.refs_0_), channel_id=1, source_target_pairs={{0,4},{1,5},{2,6},{3,7},{4,0},{5,1},{6,2},{7,3},{8,12},{9,13},{10,... | collective-permute-start | bytes 1228808 | tf_op jit(solution)/shard_map/ppermute | solution.py:104
  55.0 32.3 %collective-permute-start.13 = (bf16[800,256]{1,0:T(8,128)(2,1)S(1)}, bf16[800,256]{1,0:T(8,128)(2,1)S(1)}, u32[]{:S(2)}, u32[]{:S(2)}) collective-permute-start(bf16[800,256]{1,0:T(8,128)(2,1)S(1)} %choose.3.refs_0_), channel_id=1, source_target_pairs={{0,6},{1,7},{2,0},{3,1},{4,2},{5,3},{6,4},{7,5},{8,14},{9,15},{10,... | collective-permute-start | bytes 1228808 | tf_op jit(solution)/shard_map/ppermute | solution.py:104
  57.7 29.5 %collective-permute-start.12 = (bf16[800,256]{1,0:T(8,128)(2,1)S(1)}, bf16[800,256]{1,0:T(8,128)(2,1)S(1)}, u32[]{:S(2)}, u32[]{:S(2)}) collective-permute-start(bf16[800,256]{1,0:T(8,128)(2,1)S(1)} %choose.3.refs_0_), channel_id=1, source_target_pairs={{0,2},{1,3},{2,4},{3,5},{4,6},{5,7},{6,0},{7,1},{8,10},{9,11},{10,... | collective-permute-start | bytes 1228808 | tf_op jit(solution)/shard_map/ppermute | solution.py:104
  60.3 11.7 %collective-permute-start.4 = (bf16[400,256]{1,0:T(8,128)(2,1)S(1)}, bf16[400,256]{1,0:T(8,128)(2,1)S(1)}, u32[]{:S(2)}, u32[]{:S(2)}) collective-permute-start(bf16[400,256]{1,0:T(8,128)(2,1)S(1)} %collective-permute-done.2.refs_1_), channel_id=1, source_target_pairs={{16,0},{17,1},{18,2},{19,3},{20,4},{21,5},{22,6},{23,7},{24,8},{25... | collective-permute-start | bytes 614408 | tf_op jit(solution)/shard_map/ppermute | solution.py:104
  65.8 8.6 %collective-permute-start.3 = (bf16[400,256]{1,0:T(8,128)(2,1)S(1)}, bf16[400,256]{1,0:T(8,128)(2,1)S(1)}, u32[]{:S(2)}, u32[]{:S(2)}) collective-permute-start(bf16[400,256]{1,0:T(8,128)(2,1)S(1)} %collective-permute-done.1.refs_0_), channel_id=1, source_target_pairs={{0,16},{1,17},{2,18},{3,19},{4,20},{5,21},{6,22},{7,23},{8,24},{9,... | collective-permute-start | bytes 614408 | tf_op jit(solution)/shard_map/ppermute | solution.py:104
  68.5 15.0 %all-to-all-start = ((bf16[4,128,256]{2,1,0:T(8,128)(2,1)}), bf16[4,128,256]{2,1,0:T(8,128)(2,1)S(1)}, u32[]{:S(2)}, u32[]{:S(2)}) async-start(bf16[4,128,256]{2,1,0:T(8,128)(2,1)} %rows.3), calls=%async_computation | async-start | bytes 524288 | tf_op jit(solution)/shard_map/all_to_all | solution.py:410
  75.0 17.0 %collective-permute-start.7 = (bf16[800,256]{1,0:T(8,128)(2,1)S(1)}, bf16[800,256]{1,0:T(8,128)(2,1)S(1)}, u32[]{:S(2)}, u32[]{:S(2)}) collective-permute-start(bf16[800,256]{1,0:T(8,128)(2,1)S(1)} %choose.2.refs_0_), channel_id=1, source_target_pairs={{0,4},{1,5},{2,6},{3,7},{4,0},{5,1},{6,2},{7,3},{8,12},{9,13},{10,... | collective-permute-start | bytes 1228808 | tf_op jit(solution)/shard_map/ppermute | solution.py:104
  77.6 14.5 %collective-permute-start.6 = (bf16[800,256]{1,0:T(8,128)(2,1)S(1)}, bf16[800,256]{1,0:T(8,128)(2,1)S(1)}, u32[]{:S(2)}, u32[]{:S(2)}) collective-permute-start(bf16[800,256]{1,0:T(8,128)(2,1)S(1)} %choose.2.refs_0_), channel_id=1, source_target_pairs={{0,6},{1,7},{2,0},{3,1},{4,2},{5,3},{6,4},{7,5},{8,14},{9,15},{10,... | collective-permute-start | bytes 1228808 | tf_op jit(solution)/shard_map/ppermute | solution.py:104
  81.6 14.5 %collective-permute-start.5 = (bf16[800,256]{1,0:T(8,128)(2,1)S(1)}, bf16[800,256]{1,0:T(8,128)(2,1)S(1)}, u32[]{:S(2)}, u32[]{:S(2)}) collective-permute-start(bf16[800,256]{1,0:T(8,128)(2,1)S(1)} %choose.2.refs_0_), channel_id=1, source_target_pairs={{0,2},{1,3},{2,4},{3,5},{4,6},{5,7},{6,0},{7,1},{8,10},{9,11},{10,... | collective-permute-start | bytes 1228808 | tf_op jit(solution)/shard_map/ppermute | solution.py:104
  98.6 11.4 %collective-permute-start.15 = (bf16[1152,512]{1,0:T(8,128)(2,1)S(1)}, bf16[1152,512]{1,0:T(8,128)(2,1)S(1)}, u32[]{:S(2)}, u32[]{:S(2)}) collective-permute-start(bf16[1152,512]{1,0:T(8,128)(2,1)S(1)} %lags.5), channel_id=1, source_target_pairs={{0,1},{1,0},{2,3},{3,2},{4,5},{5,4},{6,7},{7,6},{8,9},{9,8},{10,11... | collective-permute-start | bytes 3538952 | tf_op jit(solution)/shard_map/ppermute | solution.py:104

commit v7 on v4

--- a/solution.py
+++ b/solution.py
@@ -168,6 +168,11 @@
     )(records.T, validity.T, band_average(), window_tables(win_dev))
 
 
+def first_rows_kernel(partners_ref, white_ref, out_ref):
+    del partners_ref
+    rows_kernel(white_ref, out_ref)
+
+
 def rows_kernel(white_ref, out_ref, half=0):
     lanes = pl.ds(pl.multiple_of(place()[0] * 128, 128), 128)
     blocks = [white_ref[g * COLS : (g + 1) * COLS, lanes].astype(jnp.float32) for g in range(WHITE // COLS)]
@@ -190,7 +195,7 @@
     return pl.pallas_call(
         kernel,
         out_shape=jax.ShapeDtypeStruct((CHIPS, height, STA), jnp.bfloat16),
-        in_specs=[VMEM] * len(args),
+        in_specs=[SMEM if arg.dtype == jnp.int32 else VMEM for arg in args],
         out_specs=VMEM,
         compiler_params=pltpu.CompilerParams(vmem_limit_bytes=4 * MIB),
         name="rows",
@@ -391,7 +396,7 @@
 
     white = whitened(records, validity)
     other = send(white, to_other_half)
-    rows = by_rows(rows_kernel, OWN // 2, white)
+    rows = by_rows(first_rows_kernel, OWN // 2, partners, white)
     rows, other = lax.optimization_barrier((rows, other))
     far, other_far = spread(chosen(partners, neighbours(white))), spread(chosen(partners, neighbours(other)))
     own = by_rows(own_kernel, OWN, rows, other)

time: 113 us -> 113 us (level)
  waiting for transfers between devices: 11.3 us -> 10.1 us
  starting transfers between devices: 76.9 us -> 78.1 us
    ppermute x16, starting transfers between devices: 72.3 us -> 73.6 us  [send(): return lax.ppermute(array, AXES, routes(target))]
    ppermute x16, waiting for transfers between devices: 11.3 us -> 10.1 us  [send(): return lax.ppermute(array, AXES, routes(target))]
where the time goes in v7:
time: 113 us
  starting transfers between devices  78.1 us (69%)
  Pallas kernels  22.4 us (20%)
  waiting for transfers between devices  10.1 us (9%)
  local copies, waits for them, and re-layouts  1.61 us (1%)
    ppermute x16, starting transfers between devices, send(): return lax.ppermute(array, AXES, routes(target))  73.6 us
    ppermute x16, waiting for transfers between devices, send(): return lax.ppermute(array, AXES, routes(target))  10.1 us
    pallas_call x3, Pallas kernels, into_lags(): pl.pallas_call(functools.partial(lags_kernel, spans, first, count, acc is...  9.91 us
    pallas_call x1, Pallas kernels, turned_rows(): pl.pallas_call(turn_kernel, out_shape=[jax.ShapeDtypeStruct((2, height, D...  4.68 us
    all_to_all x1, starting transfers between devices, body(): lax.all_to_all(own, 'tm', 0, 0, axis_index_groups=CHIP_GROUPS, tiled=True)  4.53 us
    pallas_call x1, Pallas kernels, whitened(): pl.pallas_call(whiten_kernel, out_shape=jax.ShapeDtypeStruct((SENT, rows)...  3.35 us
  transfers between devices with their start and end apart: 17, of which 2 were waited for; matrix products, arithmetic and copies ran while one was open for 0% of the time, Pallas kernels for 13%

profile of v7, /device:TPU:11, one launch (start us, length us, event | category | flops | bytes accessed | tf_op | source)
XLA Modules:
  0.0 112.5 jit_solution(10287750830815976984)
XLA Ops:
  0.0 3.3 %whiten.1.white_ref = bf16[400,256]{1,0:T(8,128)(2,1)} custom-call(bf16[1800,256]{1,0:T(8,128)(2,1)} %bitcast.10, s32[3,256]{1,0:T(4,128)} %bitcast.11, f32[64,64]{1,0:T(8,128)} %constant.4.clone.avg_hbm, bf16[3,128,616]{2,1,0:T(8,128)(2,1)} %constant.5.clone.table_hbm), custom_call_target="tpu_custom_call" | custom-call | tf_op jit(solution)/shard_map/whiten/pallas_call | solution.py:154
  3.4 11.0 %collective-permute-start.9 = (bf16[400,256]{1,0:T(8,128)(2,1)}, bf16[400,256]{1,0:T(8,128)(2,1)S(1)}, u32[]{:S(2)}, u32[]{:S(2)}) collective-permute-start(bf16[400,256]{1,0:T(8,128)(2,1)} %whiten.1.white_ref), channel_id=1, source_target_pairs={{16,0},{17,1},{18,2},{19,3},{20,4},{21,5},{22,6},{23,7},{24,8},{25... | collective-permute-start | bytes 614408 | tf_op jit(solution)/shard_map/ppermute | solution.py:104
  14.4 1.9 %collective-permute-start.8 = (bf16[400,256]{1,0:T(8,128)(2,1)}, bf16[400,256]{1,0:T(8,128)(2,1)S(1)}, u32[]{:S(2)}, u32[]{:S(2)}) collective-permute-start(bf16[400,256]{1,0:T(8,128)(2,1)} %whiten.1.white_ref), channel_id=1, source_target_pairs={{0,16},{1,17},{2,18},{3,19},{4,20},{5,21},{6,22},{7,23},{8,24},{9,... | collective-permute-start | bytes 614408 | tf_op jit(solution)/shard_map/ppermute | solution.py:104
  16.3 7.8 %collective-permute-start = (bf16[400,256]{1,0:T(8,128)(2,1)}, bf16[400,256]{1,0:T(8,128)(2,1)S(1)}, u32[]{:S(2)}, u32[]{:S(2)}) collective-permute-start(bf16[400,256]{1,0:T(8,128)(2,1)} %whiten.1.white_ref), channel_id=1, source_target_pairs={{0,8},{1,9},{2,10},{3,11},{4,12},{5,13},{6,14},{7,15},{8,0},{9,1},... | collective-permute-start | bytes 614408 | tf_op jit(solution)/shard_map/ppermute | solution.py:104
  24.1 0.0 collective-permute-done.9.refs_1_
  24.1 4.0 %collective-permute-start.11 = (bf16[400,256]{1,0:T(8,128)(2,1)S(1)}, bf16[400,256]{1,0:T(8,128)(2,1)S(1)}, u32[]{:S(2)}, u32[]{:S(2)}) collective-permute-start(bf16[400,256]{1,0:T(8,128)(2,1)S(1)} %collective-permute-done.9.refs_1_), channel_id=1, source_target_pairs={{16,0},{17,1},{18,2},{19,3},{20,4},{21,5},{22,6},{23,7},{24,8},{25... | collective-permute-start | bytes 614408 | tf_op jit(solution)/shard_map/ppermute | solution.py:104
  28.2 0.0 collective-permute-done.8.refs_0_
  28.2 1.9 %collective-permute-start.10 = (bf16[400,256]{1,0:T(8,128)(2,1)S(1)}, bf16[400,256]{1,0:T(8,128)(2,1)S(1)}, u32[]{:S(2)}, u32[]{:S(2)}) collective-permute-start(bf16[400,256]{1,0:T(8,128)(2,1)S(1)} %collective-permute-done.8.refs_0_), channel_id=1, source_target_pairs={{0,16},{1,17},{2,18},{3,19},{4,20},{5,21},{6,22},{7,23},{8,24},{9,... | collective-permute-start | bytes 614408 | tf_op jit(solution)/shard_map/ppermute | solution.py:104
  30.1 0.0 copy-start
  30.1 0.9 copy-done
  31.0 0.7 copy-done.1
  31.7 0.7 rows.2.first_ref
  32.4 8.8 %collective-permute-done.other_ref = bf16[400,256]{1,0:T(8,128)(2,1)S(1)} collective-permute-done((bf16[400,256]{1,0:T(8,128)(2,1)}, bf16[400,256]{1,0:T(8,128)(2,1)S(1)}, u32[]{:S(2)}, u32[]{:S(2)}) %collective-permute-start) | collective-permute-done | bytes 204832 | tf_op jit(solution)/shard_map/ppermute | solution.py:104
  41.2 6.5 %collective-permute-start.2 = (bf16[400,256]{1,0:T(8,128)(2,1)S(1)}, bf16[400,256]{1,0:T(8,128)(2,1)S(1)}, u32[]{:S(2)}, u32[]{:S(2)}) collective-permute-start(bf16[400,256]{1,0:T(8,128)(2,1)S(1)} %collective-permute-done.other_ref), channel_id=1, source_target_pairs={{16,0},{17,1},{18,2},{19,3},{20,4},{21,5},{22,6},{23,7},{24,8},{25... | collective-permute-start | bytes 614408 | tf_op jit(solution)/shard_map/ppermute | solution.py:104
  47.7 1.9 %collective-permute-start.1 = (bf16[400,256]{1,0:T(8,128)(2,1)S(1)}, bf16[400,256]{1,0:T(8,128)(2,1)S(1)}, u32[]{:S(2)}, u32[]{:S(2)}) collective-permute-start(bf16[400,256]{1,0:T(8,128)(2,1)S(1)} %collective-permute-done.other_ref), channel_id=1, source_target_pairs={{0,16},{1,17},{2,18},{3,19},{4,20},{5,21},{6,22},{7,23},{8,24},{9,... | collective-permute-start | bytes 614408 | tf_op jit(solution)/shard_map/ppermute | solution.py:104
  49.6 0.0 collective-permute-done.11.refs_3_
  49.6 0.0 collective-permute-done.10.refs_2_
  49.7 0.6 choose.3.refs_0_
  50.3 3.8 %collective-permute-start.14 = (bf16[800,256]{1,0:T(8,128)(2,1)S(1)}, bf16[800,256]{1,0:T(8,128)(2,1)S(1)}, u32[]{:S(2)}, u32[]{:S(2)}) collective-permute-start(bf16[800,256]{1,0:T(8,128)(2,1)S(1)} %choose.3.refs_0_), channel_id=1, source_target_pairs={{0,4},{1,5},{2,6},{3,7},{4,0},{5,1},{6,2},{7,3},{8,12},{9,13},{10,... | collective-permute-start | bytes 1228808 | tf_op jit(solution)/shard_map/ppermute | solution.py:104
  54.1 3.1 %collective-permute-start.13 = (bf16[800,256]{1,0:T(8,128)(2,1)S(1)}, bf16[800,256]{1,0:T(8,128)(2,1)S(1)}, u32[]{:S(2)}, u32[]{:S(2)}) collective-permute-start(bf16[800,256]{1,0:T(8,128)(2,1)S(1)} %choose.3.refs_0_), channel_id=1, source_target_pairs={{0,6},{1,7},{2,0},{3,1},{4,2},{5,3},{6,4},{7,5},{8,14},{9,15},{10,... | collective-permute-start | bytes 1228808 | tf_op jit(solution)/shard_map/ppermute | solution.py:104
  57.1 2.2 %collective-permute-start.12 = (bf16[800,256]{1,0:T(8,128)(2,1)S(1)}, bf16[800,256]{1,0:T(8,128)(2,1)S(1)}, u32[]{:S(2)}, u32[]{:S(2)}) collective-permute-start(bf16[800,256]{1,0:T(8,128)(2,1)S(1)} %choose.3.refs_0_), channel_id=1, source_target_pairs={{0,2},{1,3},{2,4},{3,5},{4,6},{5,7},{6,0},{7,1},{8,10},{9,11},{10,... | collective-permute-start | bytes 1228808 | tf_op jit(solution)/shard_map/ppermute | solution.py:104
  59.4 0.0 collective-permute-done.2.refs_1_
  59.4 5.5 %collective-permute-start.4 = (bf16[400,256]{1,0:T(8,128)(2,1)S(1)}, bf16[400,256]{1,0:T(8,128)(2,1)S(1)}, u32[]{:S(2)}, u32[]{:S(2)}) collective-permute-start(bf16[400,256]{1,0:T(8,128)(2,1)S(1)} %collective-permute-done.2.refs_1_), channel_id=1, source_target_pairs={{16,0},{17,1},{18,2},{19,3},{20,4},{21,5},{22,6},{23,7},{24,8},{25... | collective-permute-start | bytes 614408 | tf_op jit(solution)/shard_map/ppermute | solution.py:104
  64.8 0.0 collective-permute-done.1.refs_0_
  64.9 1.9 %collective-permute-start.3 = (bf16[400,256]{1,0:T(8,128)(2,1)S(1)}, bf16[400,256]{1,0:T(8,128)(2,1)S(1)}, u32[]{:S(2)}, u32[]{:S(2)}) collective-permute-start(bf16[400,256]{1,0:T(8,128)(2,1)S(1)} %collective-permute-done.1.refs_0_), channel_id=1, source_target_pairs={{0,16},{1,17},{2,18},{3,19},{4,20},{5,21},{6,22},{7,23},{8,24},{9,... | collective-permute-start | bytes 614408 | tf_op jit(solution)/shard_map/ppermute | solution.py:104
  66.8 0.9 rows.3
  67.6 4.5 %all-to-all-start = ((bf16[4,128,256]{2,1,0:T(8,128)(2,1)}), bf16[4,128,256]{2,1,0:T(8,128)(2,1)S(1)}, u32[]{:S(2)}, u32[]{:S(2)}) async-start(bf16[4,128,256]{2,1,0:T(8,128)(2,1)} %rows.3), calls=%async_computation | async-start | bytes 524288 | tf_op jit(solution)/shard_map/all_to_all | solution.py:403
  72.2 0.0 collective-permute-done.4.refs_3_
  72.2 1.3 %collective-permute-done.3.refs_2_ = bf16[400,256]{1,0:T(8,128)(2,1)S(1)} collective-permute-done((bf16[400,256]{1,0:T(8,128)(2,1)S(1)}, bf16[400,256]{1,0:T(8,128)(2,1)S(1)}, u32[]{:S(2)}, u32[]{:S(2)}) %collective-permute-start.3) | collective-permute-done | bytes 204832 | tf_op jit(solution)/shard_map/ppermute | solution.py:104
  73.5 0.0 copy-done.2
  73.5 0.6 choose.2.refs_0_
  74.1 4.2 %collective-permute-start.7 = (bf16[800,256]{1,0:T(8,128)(2,1)S(1)}, bf16[800,256]{1,0:T(8,128)(2,1)S(1)}, u32[]{:S(2)}, u32[]{:S(2)}) collective-permute-start(bf16[800,256]{1,0:T(8,128)(2,1)S(1)} %choose.2.refs_0_), channel_id=1, source_target_pairs={{0,4},{1,5},{2,6},{3,7},{4,0},{5,1},{6,2},{7,3},{8,12},{9,13},{10,... | collective-permute-start | bytes 1228808 | tf_op jit(solution)/shard_map/ppermute | solution.py:104
  78.4 1.9 %collective-permute-start.6 = (bf16[800,256]{1,0:T(8,128)(2,1)S(1)}, bf16[800,256]{1,0:T(8,128)(2,1)S(1)}, u32[]{:S(2)}, u32[]{:S(2)}) collective-permute-start(bf16[800,256]{1,0:T(8,128)(2,1)S(1)} %choose.2.refs_0_), channel_id=1, source_target_pairs={{0,6},{1,7},{2,0},{3,1},{4,2},{5,3},{6,4},{7,5},{8,14},{9,15},{10,... | collective-permute-start | bytes 1228808 | tf_op jit(solution)/shard_map/ppermute | solution.py:104
  80.3 0.0 collective-permute-done.14.refs_3_
  80.3 3.4 %collective-permute-start.5 = (bf16[800,256]{1,0:T(8,128)(2,1)S(1)}, bf16[800,256]{1,0:T(8,128)(2,1)S(1)}, u32[]{:S(2)}, u32[]{:S(2)}) collective-permute-start(bf16[800,256]{1,0:T(8,128)(2,1)S(1)} %choose.2.refs_0_), channel_id=1, source_target_pairs={{0,2},{1,3},{2,4},{3,5},{4,6},{5,7},{6,0},{7,1},{8,10},{9,11},{10,... | collective-permute-start | bytes 1228808 | tf_op jit(solution)/shard_map/ppermute | solution.py:104
  83.7 0.0 all-to-all-done.own_ref
  83.7 4.7 %turn.1 = (bf16[2,2304,1536]{2,1,0:T(8,128)(2,1)S(1)}, bf16[2,32,128]{2,1,0:T(8,128)(2,1)S(1)}) custom-call(bf16[4,128,256]{2,1,0:T(8,128)(2,1)S(1)} %all-to-all-done.own_ref), custom_call_target="tpu_custom_call" | custom-call | flops 21233664 | bytes 14155776 | tf_op jit(solution)/shard_map/turn/pallas_call | solution.py:280
  88.4 0.0 collective-permute-done.13.refs_2_
  88.4 0.0 collective-permute-done.12.refs_1_
  88.4 4.7 %lags.3.refs_4_ = f32[2304,512]{1,0:T(8,128)S(1)} custom-call(s32[2,32]{1,0:T(2,128)S(1)} %bitcast.7, bf16[2,2304,1536]{2,1,0:T(8,128)(2,1)S(1)} %get-tuple-element.11.turned_ref, bf16[2,32,128]{2,1,0:T(8,128)(2,1)S(1)} %get-tuple-element.12.valid_ref, bf16[800,256]{1,0:T(8,128)(2,1)S(1)} %choose.3.refs_0_, ...), custom_call_target="tpu_custom_call" | custom-call | flops 3623878656 | bytes 4718592 | tf_op jit(solution)/shard_map/lags/pallas_call | solution.py:340
  93.2 0.0 collective-permute-done.7.refs_3_
  93.2 0.0 collective-permute-done.6.refs_2_
  93.2 0.0 collective-permute-done.5.refs_1_
  93.2 2.6 %lags.5 = bf16[1152,512]{1,0:T(8,128)(2,1)S(1)} custom-call(s32[2,32]{1,0:T(2,128)S(1)} %bitcast.8, bf16[2,2304,1536]{2,1,0:T(8,128)(2,1)S(1)} %get-tuple-element.11.turned_ref, bf16[2,32,128]{2,1,0:T(8,128)(2,1)S(1)} %get-tuple-element.12.valid_ref, bf16[800,256]{1,0:T(8,128)(2,1)S(1)} %choose.2.refs_0_, ...), custom_call_target="tpu_custom_call" | custom-call | flops 1811939328 | bytes 2359296 | tf_op jit(solution)/shard_map/lags/pallas_call | solution.py:340
  95.8 12.5 %collective-permute-start.15 = (bf16[1152,512]{1,0:T(8,128)(2,1)S(1)}, bf16[1152,512]{1,0:T(8,128)(2,1)S(1)}, u32[]{:S(2)}, u32[]{:S(2)}) collective-permute-start(bf16[1152,512]{1,0:T(8,128)(2,1)S(1)} %lags.5), channel_id=1, source_target_pairs={{0,1},{1,0},{2,3},{3,2},{4,5},{5,4},{6,7},{7,6},{8,9},{9,8},{10,11... | collective-permute-start | bytes 3538952 | tf_op jit(solution)/shard_map/ppermute | solution.py:104
  108.3 2.6 %lags.4.mine_ref = f32[1152,512]{1,0:T(8,128)S(1)} custom-call(s32[2,32]{1,0:T(2,128)S(1)} %bitcast.9, bf16[2,2304,1536]{2,1,0:T(8,128)(2,1)S(1)} %get-tuple-element.11.turned_ref, bf16[2,32,128]{2,1,0:T(8,128)(2,1)S(1)} %get-tuple-element.12.valid_ref, bf16[800,256]{1,0:T(8,128)(2,1)S(1)} %choose.2.refs_0_, ...), custom_call_target="tpu_custom_call" | custom-call | flops 1811939328 | bytes 2359296 | tf_op jit(solution)/shard_map/lags/pallas_call | solution.py:340
  110.9 0.0 collective-permute-done.15.theirs_ref
  110.9 1.6 %combine.1 = f32[16,65,2,256]{3,2,1,0:T(2,128)} custom-call(f32[1152,512]{1,0:T(8,128)S(1)} %lags.4.mine_ref, bf16[1152,512]{1,0:T(8,128)(2,1)S(1)} %collective-permute-done.15.theirs_ref), custom_call_target="tpu_custom_call" | custom-call | tf_op jit(solution)/shard_map/combine/pallas_call | solution.py:375
  (2 shorter events, 0.0 us)
Async XLA Ops:
  0.0 73.5 %copy-start.2 = (s32[32,2]{0,1:T(2,128)S(1)}, s32[32,2]{0,1:T(2,128)}, u32[]{:S(2)}) copy-start(s32[32,2]{0,1:T(2,128)} %param.7) | copy-start | bytes 772
  3.4 20.7 %collective-permute-start.9 = (bf16[400,256]{1,0:T(8,128)(2,1)}, bf16[400,256]{1,0:T(8,128)(2,1)S(1)}, u32[]{:S(2)}, u32[]{:S(2)}) collective-permute-start(bf16[400,256]{1,0:T(8,128)(2,1)} %whiten.1.white_ref), channel_id=1, source_target_pairs={{16,0},{17,1},{18,2},{19,3},{20,4},{21,5},{22,6},{23,7},{24,8},{25... | collective-permute-start | bytes 614408 | tf_op jit(solution)/shard_map/ppermute | solution.py:104
  14.4 13.8 %collective-permute-start.8 = (bf16[400,256]{1,0:T(8,128)(2,1)}, bf16[400,256]{1,0:T(8,128)(2,1)S(1)}, u32[]{:S(2)}, u32[]{:S(2)}) collective-permute-start(bf16[400,256]{1,0:T(8,128)(2,1)} %whiten.1.white_ref), channel_id=1, source_target_pairs={{0,16},{1,17},{2,18},{3,19},{4,20},{5,21},{6,22},{7,23},{8,24},{9,... | collective-permute-start | bytes 614408 | tf_op jit(solution)/shard_map/ppermute | solution.py:104
  16.3 24.9 %collective-permute-start = (bf16[400,256]{1,0:T(8,128)(2,1)}, bf16[400,256]{1,0:T(8,128)(2,1)S(1)}, u32[]{:S(2)}, u32[]{:S(2)}) collective-permute-start(bf16[400,256]{1,0:T(8,128)(2,1)} %whiten.1.white_ref), channel_id=1, source_target_pairs={{0,8},{1,9},{2,10},{3,11},{4,12},{5,13},{6,14},{7,15},{8,0},{9,1},... | collective-permute-start | bytes 614408 | tf_op jit(solution)/shard_map/ppermute | solution.py:104
  24.1 25.5 %collective-permute-start.11 = (bf16[400,256]{1,0:T(8,128)(2,1)S(1)}, bf16[400,256]{1,0:T(8,128)(2,1)S(1)}, u32[]{:S(2)}, u32[]{:S(2)}) collective-permute-start(bf16[400,256]{1,0:T(8,128)(2,1)S(1)} %collective-permute-done.9.refs_1_), channel_id=1, source_target_pairs={{16,0},{17,1},{18,2},{19,3},{20,4},{21,5},{22,6},{23,7},{24,8},{25... | collective-permute-start | bytes 614408 | tf_op jit(solution)/shard_map/ppermute | solution.py:104
  28.2 21.5 %collective-permute-start.10 = (bf16[400,256]{1,0:T(8,128)(2,1)S(1)}, bf16[400,256]{1,0:T(8,128)(2,1)S(1)}, u32[]{:S(2)}, u32[]{:S(2)}) collective-permute-start(bf16[400,256]{1,0:T(8,128)(2,1)S(1)} %collective-permute-done.8.refs_0_), channel_id=1, source_target_pairs={{0,16},{1,17},{2,18},{3,19},{4,20},{5,21},{6,22},{7,23},{8,24},{9,... | collective-permute-start | bytes 614408 | tf_op jit(solution)/shard_map/ppermute | solution.py:104
  30.1 0.9 copy-start
  31.0 0.7 copy-start.1
  41.2 18.2 %collective-permute-start.2 = (bf16[400,256]{1,0:T(8,128)(2,1)S(1)}, bf16[400,256]{1,0:T(8,128)(2,1)S(1)}, u32[]{:S(2)}, u32[]{:S(2)}) collective-permute-start(bf16[400,256]{1,0:T(8,128)(2,1)S(1)} %collective-permute-done.other_ref), channel_id=1, source_target_pairs={{16,0},{17,1},{18,2},{19,3},{20,4},{21,5},{22,6},{23,7},{24,8},{25... | collective-permute-start | bytes 614408 | tf_op jit(solution)/shard_map/ppermute | solution.py:104
  47.7 17.1 %collective-permute-start.1 = (bf16[400,256]{1,0:T(8,128)(2,1)S(1)}, bf16[400,256]{1,0:T(8,128)(2,1)S(1)}, u32[]{:S(2)}, u32[]{:S(2)}) collective-permute-start(bf16[400,256]{1,0:T(8,128)(2,1)S(1)} %collective-permute-done.other_ref), channel_id=1, source_target_pairs={{0,16},{1,17},{2,18},{3,19},{4,20},{5,21},{6,22},{7,23},{8,24},{9,... | collective-permute-start | bytes 614408 | tf_op jit(solution)/shard_map/ppermute | solution.py:104
  50.3 30.0 %collective-permute-start.14 = (bf16[800,256]{1,0:T(8,128)(2,1)S(1)}, bf16[800,256]{1,0:T(8,128)(2,1)S(1)}, u32[]{:S(2)}, u32[]{:S(2)}) collective-permute-start(bf16[800,256]{1,0:T(8,128)(2,1)S(1)} %choose.3.refs_0_), channel_id=1, source_target_pairs={{0,4},{1,5},{2,6},{3,7},{4,0},{5,1},{6,2},{7,3},{8,12},{9,13},{10,... | collective-permute-start | bytes 1228808 | tf_op jit(solution)/shard_map/ppermute | solution.py:104
  54.1 34.3 %collective-permute-start.13 = (bf16[800,256]{1,0:T(8,128)(2,1)S(1)}, bf16[800,256]{1,0:T(8,128)(2,1)S(1)}, u32[]{:S(2)}, u32[]{:S(2)}) collective-permute-start(bf16[800,256]{1,0:T(8,128)(2,1)S(1)} %choose.3.refs_0_), channel_id=1, source_target_pairs={{0,6},{1,7},{2,0},{3,1},{4,2},{5,3},{6,4},{7,5},{8,14},{9,15},{10,... | collective-permute-start | bytes 1228808 | tf_op jit(solution)/shard_map/ppermute | solution.py:104
  57.1 31.3 %collective-permute-start.12 = (bf16[800,256]{1,0:T(8,128)(2,1)S(1)}, bf16[800,256]{1,0:T(8,128)(2,1)S(1)}, u32[]{:S(2)}, u32[]{:S(2)}) collective-permute-start(bf16[800,256]{1,0:T(8,128)(2,1)S(1)} %choose.3.refs_0_), channel_id=1, source_target_pairs={{0,2},{1,3},{2,4},{3,5},{4,6},{5,7},{6,0},{7,1},{8,10},{9,11},{10,... | collective-permute-start | bytes 1228808 | tf_op jit(solution)/shard_map/ppermute | solution.py:104
  59.4 12.8 %collective-permute-start.4 = (bf16[400,256]{1,0:T(8,128)(2,1)S(1)}, bf16[400,256]{1,0:T(8,128)(2,1)S(1)}, u32[]{:S(2)}, u32[]{:S(2)}) collective-permute-start(bf16[400,256]{1,0:T(8,128)(2,1)S(1)} %collective-permute-done.2.refs_1_), channel_id=1, source_target_pairs={{16,0},{17,1},{18,2},{19,3},{20,4},{21,5},{22,6},{23,7},{24,8},{25... | collective-permute-start | bytes 614408 | tf_op jit(solution)/shard_map/ppermute | solution.py:104
  64.9 8.6 %collective-permute-start.3 = (bf16[400,256]{1,0:T(8,128)(2,1)S(1)}, bf16[400,256]{1,0:T(8,128)(2,1)S(1)}, u32[]{:S(2)}, u32[]{:S(2)}) collective-permute-start(bf16[400,256]{1,0:T(8,128)(2,1)S(1)} %collective-permute-done.1.refs_0_), channel_id=1, source_target_pairs={{0,16},{1,17},{2,18},{3,19},{4,20},{5,21},{6,22},{7,23},{8,24},{9,... | collective-permute-start | bytes 614408 | tf_op jit(solution)/shard_map/ppermute | solution.py:104
  67.6 16.0 %all-to-all-start = ((bf16[4,128,256]{2,1,0:T(8,128)(2,1)}), bf16[4,128,256]{2,1,0:T(8,128)(2,1)S(1)}, u32[]{:S(2)}, u32[]{:S(2)}) async-start(bf16[4,128,256]{2,1,0:T(8,128)(2,1)} %rows.3), calls=%async_computation | async-start | bytes 524288 | tf_op jit(solution)/shard_map/all_to_all | solution.py:403
  74.1 19.0 %collective-permute-start.7 = (bf16[800,256]{1,0:T(8,128)(2,1)S(1)}, bf16[800,256]{1,0:T(8,128)(2,1)S(1)}, u32[]{:S(2)}, u32[]{:S(2)}) collective-permute-start(bf16[800,256]{1,0:T(8,128)(2,1)S(1)} %choose.2.refs_0_), channel_id=1, source_target_pairs={{0,4},{1,5},{2,6},{3,7},{4,0},{5,1},{6,2},{7,3},{8,12},{9,13},{10,... | collective-permute-start | bytes 1228808 | tf_op jit(solution)/shard_map/ppermute | solution.py:104
  78.4 14.8 %collective-permute-start.6 = (bf16[800,256]{1,0:T(8,128)(2,1)S(1)}, bf16[800,256]{1,0:T(8,128)(2,1)S(1)}, u32[]{:S(2)}, u32[]{:S(2)}) collective-permute-start(bf16[800,256]{1,0:T(8,128)(2,1)S(1)} %choose.2.refs_0_), channel_id=1, source_target_pairs={{0,6},{1,7},{2,0},{3,1},{4,2},{5,3},{6,4},{7,5},{8,14},{9,15},{10,... | collective-permute-start | bytes 1228808 | tf_op jit(solution)/shard_map/ppermute | solution.py:104
  80.3 12.9 %collective-permute-start.5 = (bf16[800,256]{1,0:T(8,128)(2,1)S(1)}, bf16[800,256]{1,0:T(8,128)(2,1)S(1)}, u32[]{:S(2)}, u32[]{:S(2)}) collective-permute-start(bf16[800,256]{1,0:T(8,128)(2,1)S(1)} %choose.2.refs_0_), channel_id=1, source_target_pairs={{0,2},{1,3},{2,4},{3,5},{4,6},{5,7},{6,0},{7,1},{8,10},{9,11},{10,... | collective-permute-start | bytes 1228808 | tf_op jit(solution)/shard_map/ppermute | solution.py:104
  95.8 15.1 %collective-permute-start.15 = (bf16[1152,512]{1,0:T(8,128)(2,1)S(1)}, bf16[1152,512]{1,0:T(8,128)(2,1)S(1)}, u32[]{:S(2)}, u32[]{:S(2)}) collective-permute-start(bf16[1152,512]{1,0:T(8,128)(2,1)S(1)} %lags.5), channel_id=1, source_target_pairs={{0,1},{1,0},{2,3},{3,2},{4,5},{5,4},{6,7},{7,6},{8,9},{9,8},{10,11... | collective-permute-start | bytes 3538952 | tf_op jit(solution)/shard_map/ppermute | solution.py:104

commit v8 on v6

--- a/solution.py
+++ b/solution.py
@@ -123,7 +123,7 @@
     return block, target, jnp.where(target // 8 == block // 8, 0, 1)
 
 
-def whiten_kernel(rec_hbm, mask_hbm, avg_hbm, table_hbm, out_ref, rec, mask_in, avg, table, sems):
+def whiten_kernel(rec_hbm, mask_hbm, avg_hbm, table_hbm, out_hbm, out_ref, rec, mask_in, avg, table, sems, out_sems):
     win_dev = table_hbm.shape[0]
     copies = [pltpu.make_async_copy(mask_hbm, mask_in, sems.at[0]), pltpu.make_async_copy(avg_hbm, avg, sems.at[1])]
     for w in range(win_dev):
@@ -135,6 +135,15 @@
     copies[0].wait()
     copies[1].wait()
     mask = mask_in[...].astype(jnp.float32)
+    empty = jnp.zeros((MASK_ROWS - win_dev, STA), jnp.float32)
+    out_ref[WHITE:] = jnp.concatenate([mask, empty], axis=0).astype(jnp.bfloat16)
+    leaving = []
+
+    def leave(rows):
+        leaving.append(pltpu.make_async_copy(out_ref.at[rows], out_hbm.at[rows], out_sems.at[len(leaving)]))
+        leaving[-1].start()
+
+    leave(pl.ds(WHITE, MASK_ROWS))
     for w in range(win_dev):
         copies[2 + 2 * w].wait()
         copies[3 + 2 * w].wait()
@@ -145,8 +154,9 @@
         scale = mask[w : w + 1] / jnp.sqrt(smooth + 0.05)
         out_ref[w * COLS : w * COLS + BINS] = (real * scale).astype(jnp.bfloat16)
         out_ref[w * COLS + BINS : (w + 1) * COLS] = (imag * scale).astype(jnp.bfloat16)
-    empty = jnp.zeros((MASK_ROWS - win_dev, STA), jnp.float32)
-    out_ref[WHITE:] = jnp.concatenate([mask, empty], axis=0).astype(jnp.bfloat16)
+        leave(pl.ds(w * COLS, COLS))
+    for copy in leaving:
+        copy.wait()
 
 
 def whitened(records, validity):
@@ -155,13 +165,15 @@
         whiten_kernel,
         out_shape=jax.ShapeDtypeStruct((SENT, rows), jnp.bfloat16),
         in_specs=[ANY] * 4,
-        out_specs=VMEM,
+        out_specs=ANY,
         scratch_shapes=[
+            pltpu.VMEM((SENT, rows), jnp.bfloat16),
             pltpu.VMEM((win_dev, SPAN, rows), records.dtype),
             pltpu.VMEM((win_dev, rows), jnp.int32),
             pltpu.VMEM((BINS, BINS), jnp.float32),
             pltpu.VMEM((win_dev, COLS, SPAN), jnp.bfloat16),
             pltpu.SemaphoreType.DMA((2 + 2 * win_dev,)),
+            pltpu.SemaphoreType.DMA((1 + win_dev,)),
         ],
         compiler_params=pltpu.CompilerParams(vmem_limit_bytes=60 * MIB),
         name="whiten",

time: 112 us -> 112 us (level)
  no operation moved by 1% of the time
where the time goes in v8:
time: 112 us
  starting transfers between devices  73.1 us (65%)
  Pallas kernels  21.5 us (19%)
  waiting for transfers between devices  15.2 us (14%)
  local copies, waits for them, and re-layouts  1.61 us (1%)
    ppermute x16, starting transfers between devices, send(): return lax.ppermute(array, AXES, routes(target))  69.7 us
    ppermute x16, waiting for transfers between devices, send(): return lax.ppermute(array, AXES, routes(target))  15.2 us
    pallas_call x3, Pallas kernels, into_lags(): pl.pallas_call(functools.partial(lags_kernel, spans, first, count, acc is...  9.92 us
    pallas_call x1, Pallas kernels, turned_rows(): pl.pallas_call(turn_kernel, out_shape=[jax.ShapeDtypeStruct((2, height, D...  3.74 us
    all_to_all x1, starting transfers between devices, body(): lax.all_to_all(own, 'tm', 0, 0, axis_index_groups=CHIP_GROUPS, tiled=True)  3.41 us
    pallas_call x1, Pallas kernels, whitened(): pl.pallas_call(whiten_kernel, out_shape=jax.ShapeDtypeStruct((SENT, rows)...  3.33 us
  transfers between devices with their start and end apart: 17, of which 3 were waited for; matrix products, arithmetic and copies ran while one was open for 0% of the time, Pallas kernels for 12%

profile of v8, /device:TPU:9, one launch (start us, length us, event | category | flops | bytes accessed | tf_op | source)
XLA Modules:
  0.0 111.7 jit_solution(8824741227120116257)
XLA Ops:
  0.0 3.3 %whiten.1.white_ref = bf16[400,256]{1,0:T(8,128)(2,1)} custom-call(bf16[1800,256]{1,0:T(8,128)(2,1)} %bitcast.10, s32[3,256]{1,0:T(4,128)} %bitcast.11, f32[64,64]{1,0:T(8,128)} %constant.4.clone.avg_hbm, bf16[3,128,616]{2,1,0:T(8,128)(2,1)} %constant.5.clone.table_hbm), custom_call_target="tpu_custom_call" | custom-call | tf_op jit(solution)/shard_map/whiten/pallas_call | solution.py:164
  3.3 11.0 %collective-permute-start.9 = (bf16[400,256]{1,0:T(8,128)(2,1)}, bf16[400,256]{1,0:T(8,128)(2,1)S(1)}, u32[]{:S(2)}, u32[]{:S(2)}) collective-permute-start(bf16[400,256]{1,0:T(8,128)(2,1)} %whiten.1.white_ref), channel_id=1, source_target_pairs={{16,0},{17,1},{18,2},{19,3},{20,4},{21,5},{22,6},{23,7},{24,8},{25... | collective-permute-start | bytes 614408 | tf_op jit(solution)/shard_map/ppermute | solution.py:104
  14.4 1.9 %collective-permute-start.8 = (bf16[400,256]{1,0:T(8,128)(2,1)}, bf16[400,256]{1,0:T(8,128)(2,1)S(1)}, u32[]{:S(2)}, u32[]{:S(2)}) collective-permute-start(bf16[400,256]{1,0:T(8,128)(2,1)} %whiten.1.white_ref), channel_id=1, source_target_pairs={{0,16},{1,17},{2,18},{3,19},{4,20},{5,21},{6,22},{7,23},{8,24},{9,... | collective-permute-start | bytes 614408 | tf_op jit(solution)/shard_map/ppermute | solution.py:104
  16.3 7.8 %collective-permute-start = (bf16[400,256]{1,0:T(8,128)(2,1)}, bf16[400,256]{1,0:T(8,128)(2,1)S(1)}, u32[]{:S(2)}, u32[]{:S(2)}) collective-permute-start(bf16[400,256]{1,0:T(8,128)(2,1)} %whiten.1.white_ref), channel_id=1, source_target_pairs={{0,8},{1,9},{2,10},{3,11},{4,12},{5,13},{6,14},{7,15},{8,0},{9,1},... | collective-permute-start | bytes 614408 | tf_op jit(solution)/shard_map/ppermute | solution.py:104
  24.1 0.0 collective-permute-done.9.refs_1_
  24.1 4.0 %collective-permute-start.11 = (bf16[400,256]{1,0:T(8,128)(2,1)S(1)}, bf16[400,256]{1,0:T(8,128)(2,1)S(1)}, u32[]{:S(2)}, u32[]{:S(2)}) collective-permute-start(bf16[400,256]{1,0:T(8,128)(2,1)S(1)} %collective-permute-done.9.refs_1_), channel_id=1, source_target_pairs={{16,0},{17,1},{18,2},{19,3},{20,4},{21,5},{22,6},{23,7},{24,8},{25... | collective-permute-start | bytes 614408 | tf_op jit(solution)/shard_map/ppermute | solution.py:104
  28.1 0.0 collective-permute-done.8.refs_0_
  28.1 1.9 %collective-permute-start.10 = (bf16[400,256]{1,0:T(8,128)(2,1)S(1)}, bf16[400,256]{1,0:T(8,128)(2,1)S(1)}, u32[]{:S(2)}, u32[]{:S(2)}) collective-permute-start(bf16[400,256]{1,0:T(8,128)(2,1)S(1)} %collective-permute-done.8.refs_0_), channel_id=1, source_target_pairs={{0,16},{1,17},{2,18},{3,19},{4,20},{5,21},{6,22},{7,23},{8,24},{9,... | collective-permute-start | bytes 614408 | tf_op jit(solution)/shard_map/ppermute | solution.py:104
  30.1 0.0 copy-start
  30.1 0.9 copy-done
  31.0 0.7 copy-done.1
  31.7 0.7 rows.2.first_ref
  32.4 8.8 %collective-permute-done.other_ref = bf16[400,256]{1,0:T(8,128)(2,1)S(1)} collective-permute-done((bf16[400,256]{1,0:T(8,128)(2,1)}, bf16[400,256]{1,0:T(8,128)(2,1)S(1)}, u32[]{:S(2)}, u32[]{:S(2)}) %collective-permute-start) | collective-permute-done | bytes 204832 | tf_op jit(solution)/shard_map/ppermute | solution.py:104
  41.2 6.5 %collective-permute-start.2 = (bf16[400,256]{1,0:T(8,128)(2,1)S(1)}, bf16[400,256]{1,0:T(8,128)(2,1)S(1)}, u32[]{:S(2)}, u32[]{:S(2)}) collective-permute-start(bf16[400,256]{1,0:T(8,128)(2,1)S(1)} %collective-permute-done.other_ref), channel_id=1, source_target_pairs={{16,0},{17,1},{18,2},{19,3},{20,4},{21,5},{22,6},{23,7},{24,8},{25... | collective-permute-start | bytes 614408 | tf_op jit(solution)/shard_map/ppermute | solution.py:104
  47.7 1.9 %collective-permute-start.1 = (bf16[400,256]{1,0:T(8,128)(2,1)S(1)}, bf16[400,256]{1,0:T(8,128)(2,1)S(1)}, u32[]{:S(2)}, u32[]{:S(2)}) collective-permute-start(bf16[400,256]{1,0:T(8,128)(2,1)S(1)} %collective-permute-done.other_ref), channel_id=1, source_target_pairs={{0,16},{1,17},{2,18},{3,19},{4,20},{5,21},{6,22},{7,23},{8,24},{9,... | collective-permute-start | bytes 614408 | tf_op jit(solution)/shard_map/ppermute | solution.py:104
  49.6 0.0 collective-permute-done.11.refs_3_
  49.6 0.0 collective-permute-done.10.refs_2_
  49.7 0.6 choose.3.refs_0_
  50.3 4.6 %collective-permute-start.14 = (bf16[800,256]{1,0:T(8,128)(2,1)S(1)}, bf16[800,256]{1,0:T(8,128)(2,1)S(1)}, u32[]{:S(2)}, u32[]{:S(2)}) collective-permute-start(bf16[800,256]{1,0:T(8,128)(2,1)S(1)} %choose.3.refs_0_), channel_id=1, source_target_pairs={{0,4},{1,5},{2,6},{3,7},{4,0},{5,1},{6,2},{7,3},{8,12},{9,13},{10,... | collective-permute-start | bytes 1228808 | tf_op jit(solution)/shard_map/ppermute | solution.py:104
  54.9 2.8 %collective-permute-start.13 = (bf16[800,256]{1,0:T(8,128)(2,1)S(1)}, bf16[800,256]{1,0:T(8,128)(2,1)S(1)}, u32[]{:S(2)}, u32[]{:S(2)}) collective-permute-start(bf16[800,256]{1,0:T(8,128)(2,1)S(1)} %choose.3.refs_0_), channel_id=1, source_target_pairs={{0,6},{1,7},{2,0},{3,1},{4,2},{5,3},{6,4},{7,5},{8,14},{9,15},{10,... | collective-permute-start | bytes 1228808 | tf_op jit(solution)/shard_map/ppermute | solution.py:104
  57.7 2.5 %collective-permute-start.12 = (bf16[800,256]{1,0:T(8,128)(2,1)S(1)}, bf16[800,256]{1,0:T(8,128)(2,1)S(1)}, u32[]{:S(2)}, u32[]{:S(2)}) collective-permute-start(bf16[800,256]{1,0:T(8,128)(2,1)S(1)} %choose.3.refs_0_), channel_id=1, source_target_pairs={{0,2},{1,3},{2,4},{3,5},{4,6},{5,7},{6,0},{7,1},{8,10},{9,11},{10,... | collective-permute-start | bytes 1228808 | tf_op jit(solution)/shard_map/ppermute | solution.py:104
  60.2 0.0 collective-permute-done.2.refs_1_
  60.3 5.5 %collective-permute-start.4 = (bf16[400,256]{1,0:T(8,128)(2,1)S(1)}, bf16[400,256]{1,0:T(8,128)(2,1)S(1)}, u32[]{:S(2)}, u32[]{:S(2)}) collective-permute-start(bf16[400,256]{1,0:T(8,128)(2,1)S(1)} %collective-permute-done.2.refs_1_), channel_id=1, source_target_pairs={{16,0},{17,1},{18,2},{19,3},{20,4},{21,5},{22,6},{23,7},{24,8},{25... | collective-permute-start | bytes 614408 | tf_op jit(solution)/shard_map/ppermute | solution.py:104
  65.7 0.0 collective-permute-done.1.refs_0_
  65.7 1.9 %collective-permute-start.3 = (bf16[400,256]{1,0:T(8,128)(2,1)S(1)}, bf16[400,256]{1,0:T(8,128)(2,1)S(1)}, u32[]{:S(2)}, u32[]{:S(2)}) collective-permute-start(bf16[400,256]{1,0:T(8,128)(2,1)S(1)} %collective-permute-done.1.refs_0_), channel_id=1, source_target_pairs={{0,16},{1,17},{2,18},{3,19},{4,20},{5,21},{6,22},{7,23},{8,24},{9,... | collective-permute-start | bytes 614408 | tf_op jit(solution)/shard_map/ppermute | solution.py:104
  67.7 0.9 rows.3
  68.5 3.4 %all-to-all-start = ((bf16[4,128,256]{2,1,0:T(8,128)(2,1)}), bf16[4,128,256]{2,1,0:T(8,128)(2,1)S(1)}, u32[]{:S(2)}, u32[]{:S(2)}) async-start(bf16[4,128,256]{2,1,0:T(8,128)(2,1)} %rows.3), calls=%async_computation | async-start | bytes 524288 | tf_op jit(solution)/shard_map/all_to_all | solution.py:422
  71.9 0.0 collective-permute-done.4.refs_3_
  72.0 2.4 %collective-permute-done.3.refs_2_ = bf16[400,256]{1,0:T(8,128)(2,1)S(1)} collective-permute-done((bf16[400,256]{1,0:T(8,128)(2,1)S(1)}, bf16[400,256]{1,0:T(8,128)(2,1)S(1)}, u32[]{:S(2)}, u32[]{:S(2)}) %collective-permute-start.3) | collective-permute-done | bytes 204832 | tf_op jit(solution)/shard_map/ppermute | solution.py:104
  74.4 0.0 copy-done.2
  74.4 0.6 choose.2.refs_0_
  75.0 2.6 %collective-permute-start.7 = (bf16[800,256]{1,0:T(8,128)(2,1)S(1)}, bf16[800,256]{1,0:T(8,128)(2,1)S(1)}, u32[]{:S(2)}, u32[]{:S(2)}) collective-permute-start(bf16[800,256]{1,0:T(8,128)(2,1)S(1)} %choose.2.refs_0_), channel_id=1, source_target_pairs={{0,4},{1,5},{2,6},{3,7},{4,0},{5,1},{6,2},{7,3},{8,12},{9,13},{10,... | collective-permute-start | bytes 1228808 | tf_op jit(solution)/shard_map/ppermute | solution.py:104
  77.6 4.0 %collective-permute-start.6 = (bf16[800,256]{1,0:T(8,128)(2,1)S(1)}, bf16[800,256]{1,0:T(8,128)(2,1)S(1)}, u32[]{:S(2)}, u32[]{:S(2)}) collective-permute-start(bf16[800,256]{1,0:T(8,128)(2,1)S(1)} %choose.2.refs_0_), channel_id=1, source_target_pairs={{0,6},{1,7},{2,0},{3,1},{4,2},{5,3},{6,4},{7,5},{8,14},{9,15},{10,... | collective-permute-start | bytes 1228808 | tf_op jit(solution)/shard_map/ppermute | solution.py:104
  81.5 0.0 collective-permute-done.14.refs_3_
  81.5 1.9 %collective-permute-start.5 = (bf16[800,256]{1,0:T(8,128)(2,1)S(1)}, bf16[800,256]{1,0:T(8,128)(2,1)S(1)}, u32[]{:S(2)}, u32[]{:S(2)}) collective-permute-start(bf16[800,256]{1,0:T(8,128)(2,1)S(1)} %choose.2.refs_0_), channel_id=1, source_target_pairs={{0,2},{1,3},{2,4},{3,5},{4,6},{5,7},{6,0},{7,1},{8,10},{9,11},{10,... | collective-permute-start | bytes 1228808 | tf_op jit(solution)/shard_map/ppermute | solution.py:104
  83.5 0.0 all-to-all-done.own_ref
  83.5 3.7 %turn.1 = (bf16[2,2304,1536]{2,1,0:T(8,128)(2,1)S(1)}, bf16[2,32,128]{2,1,0:T(8,128)(2,1)S(1)}) custom-call(bf16[4,128,256]{2,1,0:T(8,128)(2,1)S(1)} %all-to-all-done.own_ref), custom_call_target="tpu_custom_call" | custom-call | flops 21233664 | bytes 14155776 | tf_op jit(solution)/shard_map/turn/pallas_call | solution.py:299
  87.2 0.0 collective-permute-done.13.refs_2_
  87.2 0.0 collective-permute-done.12.refs_1_
  87.3 4.8 %lags.3.refs_4_ = f32[2304,512]{1,0:T(8,128)S(1)} custom-call(s32[2,32]{1,0:T(2,128)S(1)} %bitcast.7, bf16[2,2304,1536]{2,1,0:T(8,128)(2,1)S(1)} %get-tuple-element.11.turned_ref, bf16[2,32,128]{2,1,0:T(8,128)(2,1)S(1)} %get-tuple-element.12.valid_ref, bf16[800,256]{1,0:T(8,128)(2,1)S(1)} %choose.3.refs_0_, ...), custom_call_target="tpu_custom_call" | custom-call | flops 3623878656 | bytes 4718592 | tf_op jit(solution)/shard_map/lags/pallas_call | solution.py:359
  92.0 0.0 collective-permute-done.7.refs_3_
  92.0 0.0 collective-permute-done.6.refs_2_
  92.0 4.0 %collective-permute-done.5.refs_1_ = bf16[800,256]{1,0:T(8,128)(2,1)S(1)} collective-permute-done((bf16[800,256]{1,0:T(8,128)(2,1)S(1)}, bf16[800,256]{1,0:T(8,128)(2,1)S(1)}, u32[]{:S(2)}, u32[]{:S(2)}) %collective-permute-start.5) | collective-permute-done | bytes 409632 | tf_op jit(solution)/shard_map/ppermute | solution.py:104
  96.0 2.6 %lags.5 = bf16[1152,512]{1,0:T(8,128)(2,1)S(1)} custom-call(s32[2,32]{1,0:T(2,128)S(1)} %bitcast.8, bf16[2,2304,1536]{2,1,0:T(8,128)(2,1)S(1)} %get-tuple-element.11.turned_ref, bf16[2,32,128]{2,1,0:T(8,128)(2,1)S(1)} %get-tuple-element.12.valid_ref, bf16[800,256]{1,0:T(8,128)(2,1)S(1)} %choose.2.refs_0_, ...), custom_call_target="tpu_custom_call" | custom-call | flops 1811939328 | bytes 2359296 | tf_op jit(solution)/shard_map/lags/pallas_call | solution.py:359
  98.6 8.8 %collective-permute-start.15 = (bf16[1152,512]{1,0:T(8,128)(2,1)S(1)}, bf16[1152,512]{1,0:T(8,128)(2,1)S(1)}, u32[]{:S(2)}, u32[]{:S(2)}) collective-permute-start(bf16[1152,512]{1,0:T(8,128)(2,1)S(1)} %lags.5), channel_id=1, source_target_pairs={{0,1},{1,0},{2,3},{3,2},{4,5},{5,4},{6,7},{7,6},{8,9},{9,8},{10,11... | collective-permute-start | bytes 3538952 | tf_op jit(solution)/shard_map/ppermute | solution.py:104
  107.4 2.6 %lags.4.mine_ref = f32[1152,512]{1,0:T(8,128)S(1)} custom-call(s32[2,32]{1,0:T(2,128)S(1)} %bitcast.9, bf16[2,2304,1536]{2,1,0:T(8,128)(2,1)S(1)} %get-tuple-element.11.turned_ref, bf16[2,32,128]{2,1,0:T(8,128)(2,1)S(1)} %get-tuple-element.12.valid_ref, bf16[800,256]{1,0:T(8,128)(2,1)S(1)} %choose.2.refs_0_, ...), custom_call_target="tpu_custom_call" | custom-call | flops 1811939328 | bytes 2359296 | tf_op jit(solution)/shard_map/lags/pallas_call | solution.py:359
  110.0 0.0 collective-permute-done.15.theirs_ref
  110.0 1.6 %combine.1 = f32[16,65,2,256]{3,2,1,0:T(2,128)} custom-call(f32[1152,512]{1,0:T(8,128)S(1)} %lags.4.mine_ref, bf16[1152,512]{1,0:T(8,128)(2,1)S(1)} %collective-permute-done.15.theirs_ref), custom_call_target="tpu_custom_call" | custom-call | tf_op jit(solution)/shard_map/combine/pallas_call | solution.py:394
  (2 shorter events, 0.0 us)
Async XLA Ops:
  0.0 74.4 %copy-start.2 = (s32[32,2]{0,1:T(2,128)S(1)}, s32[32,2]{0,1:T(2,128)}, u32[]{:S(2)}) copy-start(s32[32,2]{0,1:T(2,128)} %param.7) | copy-start | bytes 772
  3.3 20.8 %collective-permute-start.9 = (bf16[400,256]{1,0:T(8,128)(2,1)}, bf16[400,256]{1,0:T(8,128)(2,1)S(1)}, u32[]{:S(2)}, u32[]{:S(2)}) collective-permute-start(bf16[400,256]{1,0:T(8,128)(2,1)} %whiten.1.white_ref), channel_id=1, source_target_pairs={{16,0},{17,1},{18,2},{19,3},{20,4},{21,5},{22,6},{23,7},{24,8},{25... | collective-permute-start | bytes 614408 | tf_op jit(solution)/shard_map/ppermute | solution.py:104
  14.4 13.8 %collective-permute-start.8 = (bf16[400,256]{1,0:T(8,128)(2,1)}, bf16[400,256]{1,0:T(8,128)(2,1)S(1)}, u32[]{:S(2)}, u32[]{:S(2)}) collective-permute-start(bf16[400,256]{1,0:T(8,128)(2,1)} %whiten.1.white_ref), channel_id=1, source_target_pairs={{0,16},{1,17},{2,18},{3,19},{4,20},{5,21},{6,22},{7,23},{8,24},{9,... | collective-permute-start | bytes 614408 | tf_op jit(solution)/shard_map/ppermute | solution.py:104
  16.3 24.9 %collective-permute-start = (bf16[400,256]{1,0:T(8,128)(2,1)}, bf16[400,256]{1,0:T(8,128)(2,1)S(1)}, u32[]{:S(2)}, u32[]{:S(2)}) collective-permute-start(bf16[400,256]{1,0:T(8,128)(2,1)} %whiten.1.white_ref), channel_id=1, source_target_pairs={{0,8},{1,9},{2,10},{3,11},{4,12},{5,13},{6,14},{7,15},{8,0},{9,1},... | collective-permute-start | bytes 614408 | tf_op jit(solution)/shard_map/ppermute | solution.py:104
  24.1 25.5 %collective-permute-start.11 = (bf16[400,256]{1,0:T(8,128)(2,1)S(1)}, bf16[400,256]{1,0:T(8,128)(2,1)S(1)}, u32[]{:S(2)}, u32[]{:S(2)}) collective-permute-start(bf16[400,256]{1,0:T(8,128)(2,1)S(1)} %collective-permute-done.9.refs_1_), channel_id=1, source_target_pairs={{16,0},{17,1},{18,2},{19,3},{20,4},{21,5},{22,6},{23,7},{24,8},{25... | collective-permute-start | bytes 614408 | tf_op jit(solution)/shard_map/ppermute | solution.py:104
  28.1 21.5 %collective-permute-start.10 = (bf16[400,256]{1,0:T(8,128)(2,1)S(1)}, bf16[400,256]{1,0:T(8,128)(2,1)S(1)}, u32[]{:S(2)}, u32[]{:S(2)}) collective-permute-start(bf16[400,256]{1,0:T(8,128)(2,1)S(1)} %collective-permute-done.8.refs_0_), channel_id=1, source_target_pairs={{0,16},{1,17},{2,18},{3,19},{4,20},{5,21},{6,22},{7,23},{8,24},{9,... | collective-permute-start | bytes 614408 | tf_op jit(solution)/shard_map/ppermute | solution.py:104
  30.1 0.9 copy-start
  31.0 0.7 copy-start.1
  41.2 19.1 %collective-permute-start.2 = (bf16[400,256]{1,0:T(8,128)(2,1)S(1)}, bf16[400,256]{1,0:T(8,128)(2,1)S(1)}, u32[]{:S(2)}, u32[]{:S(2)}) collective-permute-start(bf16[400,256]{1,0:T(8,128)(2,1)S(1)} %collective-permute-done.other_ref), channel_id=1, source_target_pairs={{16,0},{17,1},{18,2},{19,3},{20,4},{21,5},{22,6},{23,7},{24,8},{25... | collective-permute-start | bytes 614408 | tf_op jit(solution)/shard_map/ppermute | solution.py:104
  47.7 18.0 %collective-permute-start.1 = (bf16[400,256]{1,0:T(8,128)(2,1)S(1)}, bf16[400,256]{1,0:T(8,128)(2,1)S(1)}, u32[]{:S(2)}, u32[]{:S(2)}) collective-permute-start(bf16[400,256]{1,0:T(8,128)(2,1)S(1)} %collective-permute-done.other_ref), channel_id=1, source_target_pairs={{0,16},{1,17},{2,18},{3,19},{4,20},{5,21},{6,22},{7,23},{8,24},{9,... | collective-permute-start | bytes 614408 | tf_op jit(solution)/shard_map/ppermute | solution.py:104
  50.3 31.2 %collective-permute-start.14 = (bf16[800,256]{1,0:T(8,128)(2,1)S(1)}, bf16[800,256]{1,0:T(8,128)(2,1)S(1)}, u32[]{:S(2)}, u32[]{:S(2)}) collective-permute-start(bf16[800,256]{1,0:T(8,128)(2,1)S(1)} %choose.3.refs_0_), channel_id=1, source_target_pairs={{0,4},{1,5},{2,6},{3,7},{4,0},{5,1},{6,2},{7,3},{8,12},{9,13},{10,... | collective-permute-start | bytes 1228808 | tf_op jit(solution)/shard_map/ppermute | solution.py:104
  54.9 32.3 %collective-permute-start.13 = (bf16[800,256]{1,0:T(8,128)(2,1)S(1)}, bf16[800,256]{1,0:T(8,128)(2,1)S(1)}, u32[]{:S(2)}, u32[]{:S(2)}) collective-permute-start(bf16[800,256]{1,0:T(8,128)(2,1)S(1)} %choose.3.refs_0_), channel_id=1, source_target_pairs={{0,6},{1,7},{2,0},{3,1},{4,2},{5,3},{6,4},{7,5},{8,14},{9,15},{10,... | collective-permute-start | bytes 1228808 | tf_op jit(solution)/shard_map/ppermute | solution.py:104
  57.7 29.5 %collective-permute-start.12 = (bf16[800,256]{1,0:T(8,128)(2,1)S(1)}, bf16[800,256]{1,0:T(8,128)(2,1)S(1)}, u32[]{:S(2)}, u32[]{:S(2)}) collective-permute-start(bf16[800,256]{1,0:T(8,128)(2,1)S(1)} %choose.3.refs_0_), channel_id=1, source_target_pairs={{0,2},{1,3},{2,4},{3,5},{4,6},{5,7},{6,0},{7,1},{8,10},{9,11},{10,... | collective-permute-start | bytes 1228808 | tf_op jit(solution)/shard_map/ppermute | solution.py:104
  60.3 11.7 %collective-permute-start.4 = (bf16[400,256]{1,0:T(8,128)(2,1)S(1)}, bf16[400,256]{1,0:T(8,128)(2,1)S(1)}, u32[]{:S(2)}, u32[]{:S(2)}) collective-permute-start(bf16[400,256]{1,0:T(8,128)(2,1)S(1)} %collective-permute-done.2.refs_1_), channel_id=1, source_target_pairs={{16,0},{17,1},{18,2},{19,3},{20,4},{21,5},{22,6},{23,7},{24,8},{25... | collective-permute-start | bytes 614408 | tf_op jit(solution)/shard_map/ppermute | solution.py:104
  65.7 8.6 %collective-permute-start.3 = (bf16[400,256]{1,0:T(8,128)(2,1)S(1)}, bf16[400,256]{1,0:T(8,128)(2,1)S(1)}, u32[]{:S(2)}, u32[]{:S(2)}) collective-permute-start(bf16[400,256]{1,0:T(8,128)(2,1)S(1)} %collective-permute-done.1.refs_0_), channel_id=1, source_target_pairs={{0,16},{1,17},{2,18},{3,19},{4,20},{5,21},{6,22},{7,23},{8,24},{9,... | collective-permute-start | bytes 614408 | tf_op jit(solution)/shard_map/ppermute | solution.py:104
  68.5 15.0 %all-to-all-start = ((bf16[4,128,256]{2,1,0:T(8,128)(2,1)}), bf16[4,128,256]{2,1,0:T(8,128)(2,1)S(1)}, u32[]{:S(2)}, u32[]{:S(2)}) async-start(bf16[4,128,256]{2,1,0:T(8,128)(2,1)} %rows.3), calls=%async_computation | async-start | bytes 524288 | tf_op jit(solution)/shard_map/all_to_all | solution.py:422
  75.0 17.0 %collective-permute-start.7 = (bf16[800,256]{1,0:T(8,128)(2,1)S(1)}, bf16[800,256]{1,0:T(8,128)(2,1)S(1)}, u32[]{:S(2)}, u32[]{:S(2)}) collective-permute-start(bf16[800,256]{1,0:T(8,128)(2,1)S(1)} %choose.2.refs_0_), channel_id=1, source_target_pairs={{0,4},{1,5},{2,6},{3,7},{4,0},{5,1},{6,2},{7,3},{8,12},{9,13},{10,... | collective-permute-start | bytes 1228808 | tf_op jit(solution)/shard_map/ppermute | solution.py:104
  77.6 14.5 %collective-permute-start.6 = (bf16[800,256]{1,0:T(8,128)(2,1)S(1)}, bf16[800,256]{1,0:T(8,128)(2,1)S(1)}, u32[]{:S(2)}, u32[]{:S(2)}) collective-permute-start(bf16[800,256]{1,0:T(8,128)(2,1)S(1)} %choose.2.refs_0_), channel_id=1, source_target_pairs={{0,6},{1,7},{2,0},{3,1},{4,2},{5,3},{6,4},{7,5},{8,14},{9,15},{10,... | collective-permute-start | bytes 1228808 | tf_op jit(solution)/shard_map/ppermute | solution.py:104
  81.5 14.5 %collective-permute-start.5 = (bf16[800,256]{1,0:T(8,128)(2,1)S(1)}, bf16[800,256]{1,0:T(8,128)(2,1)S(1)}, u32[]{:S(2)}, u32[]{:S(2)}) collective-permute-start(bf16[800,256]{1,0:T(8,128)(2,1)S(1)} %choose.2.refs_0_), channel_id=1, source_target_pairs={{0,2},{1,3},{2,4},{3,5},{4,6},{5,7},{6,0},{7,1},{8,10},{9,11},{10,... | collective-permute-start | bytes 1228808 | tf_op jit(solution)/shard_map/ppermute | solution.py:104
  98.6 11.4 %collective-permute-start.15 = (bf16[1152,512]{1,0:T(8,128)(2,1)S(1)}, bf16[1152,512]{1,0:T(8,128)(2,1)S(1)}, u32[]{:S(2)}, u32[]{:S(2)}) collective-permute-start(bf16[1152,512]{1,0:T(8,128)(2,1)S(1)} %lags.5), channel_id=1, source_target_pairs={{0,1},{1,0},{2,3},{3,2},{4,5},{5,4},{6,7},{7,6},{8,9},{9,8},{10,11... | collective-permute-start | bytes 3538952 | tf_op jit(solution)/shard_map/ppermute | solution.py:104
